TPU v7x, 128 devices: a whole 4x4x4 slice. The times are simulated.
128 devices in a mesh: node: 64 (over x_lo, z, y, core), feat: 2 (over x_hi).
Axes of the slice: x: 4 (x_hi: 2, x_lo: 2; x = x_hi * 2 + x_lo), y: 4, z: 4, core: 2. Of those that a mesh axis runs over, the one named last changes fastest.
Arguments:
- node_feats: bfloat16 [65536, 1024], P('node', 'feat'), may hold values from -6 to 6
- edge_tiles: bfloat16 [1280, 128, 128], P('node'), may hold values from 0.001953125 to 0.078125
- slot_row: int32 [64, 20], P('node'), may hold values from 0 to 7
- slot_col: int32 [64, 20], P('node'), may hold values from 0 to 7
- slot_tile: int32 [64, 20], P('node'), may hold values from 0 to 19, each once within a row
- slot_count: int32 [64, 5], P('node'), may hold values from 1 to 4, as said below
- w_self: bfloat16 [1024, 1024], P('feat'), may hold values from -0.1875 to 0.1875
- w_neigh: bfloat16 [1024, 1024], P('feat'), may hold values from -0.1875 to 0.1875
- bias: float32 [1024], P('feat'), may hold values from -3 to 3
- cotangent: bfloat16 [65536, 1024], P('node', 'feat'), may hold values from -6 to 6
Outputs:
- hidden_out: bfloat16 [65536, 1024], P('node', 'feat')
- grad_nodes: bfloat16 [65536, 1024], P('node', 'feat')
- grad_self: float32 [1024, 1024], P('feat')
- grad_neigh: float32 [1024, 1024], P('feat')
- grad_bias: float32 [1024], P('feat')
Inputs may be any that keep to these rules, and one draw needn't show every extreme that they name: `slot_count`: 4 is reached on some device. `slot_tile`: each device's row names each of its tiles once.
All inputs are finite; a program needn't handle non-finite values.
Results may differ from a plain program's by a relative error of at most 0.007.
Values may be sent and summed in bfloat16 or wider, within the bound.
No kernel may reach another device: no remote copies, remote signals or barrier semaphores. Data moves between devices by JAX's collectives and lax.ppermute only.
A program may use at most 128 MiB of HBM per device.

v0:
```python
import jax
import jax.numpy as jnp
from jax import lax
from jax.sharding import PartitionSpec as P

REACH = 2
PAIR_MAX = 4


def from_behind(block, axis, distance):
    devices = range(lax.axis_size(axis))
    route = [((i - distance) % len(devices), i) for i in devices]
    return lax.ppermute(block, axis, route)


def place_rows(onehot, values):
    return jnp.einsum("rt,tbf->rbf", onehot, values, precision=lax.Precision.HIGHEST)


def slot_range(offset):
    return slice(offset * PAIR_MAX, (offset + 1) * PAIR_MAX)


def on_device(
    node_feats,
    edge_tiles,
    slot_row,
    slot_col,
    slot_tile,
    slot_count,
    w_self,
    w_neigh,
    bias,
    cotangent,
):
    node_rows, width = node_feats.shape
    block = edge_tiles.shape[1]
    row_blocks = node_rows // block
    tile_total = edge_tiles.shape[0]
    row_ids = slot_row[0]
    column_ids = slot_col[0]
    slot_index = jnp.arange(tile_total, dtype=jnp.int32)
    slot_live = slot_index % PAIR_MAX < slot_count[0][slot_index // PAIR_MAX]
    tile_values = jnp.where(
        slot_live[:, None, None], edge_tiles[slot_tile[0]], jnp.zeros((), edge_tiles.dtype)
    )
    levels = jnp.arange(row_blocks, dtype=jnp.int32)
    row_onehot = (row_ids[None, :] == levels[:, None]).astype(jnp.float32)
    col_onehot = (column_ids[None, :] == levels[:, None]).astype(jnp.float32)

    def picked_term(picked, offset):
        window_slots = slot_range(offset)
        product = jnp.einsum(
            "tab,tbf->taf", tile_values[window_slots], picked, preferred_element_type=jnp.float32
        )
        return place_rows(row_onehot[:, window_slots], product)

    def gather_term(source, offset):
        picked = source.reshape(row_blocks, block, width)[column_ids[slot_range(offset)]]
        return picked_term(picked, offset)

    summed = gather_term(node_feats, REACH)
    ahead = node_feats
    behind = node_feats
    for distance in range(1, REACH + 1):
        ahead = from_behind(ahead, "node", 1)
        summed = summed + gather_term(ahead, REACH - distance)
        behind = from_behind(behind, "node", -1)
        summed = summed + gather_term(behind, REACH + distance)
    aggregate = summed.reshape(node_rows, width).astype(jnp.bfloat16)
    partial_sum = jnp.dot(aggregate, w_neigh, preferred_element_type=jnp.float32) + jnp.dot(
        node_feats, w_self, preferred_element_type=jnp.float32
    )
    mixed = lax.psum_scatter(partial_sum, "feat", scatter_dimension=1, tiled=True)
    preact = mixed + bias
    sigma = jax.nn.sigmoid(preact)
    hidden_out = (preact * sigma).astype(jnp.bfloat16)
    delta = (cotangent.astype(jnp.float32) * sigma * (1.0 + preact * (1.0 - sigma))).astype(
        jnp.bfloat16
    )
    delta_full = lax.all_gather(delta, "feat", axis=1, tiled=True)
    neigh_part = jnp.einsum("nf,nh->fh", aggregate, delta_full, preferred_element_type=jnp.float32)
    self_part = jnp.einsum("nf,nh->fh", node_feats, delta_full, preferred_element_type=jnp.float32)
    bias_part = jnp.sum(delta.astype(jnp.float32), axis=0)
    neigh_sum, self_sum, bias_sum = lax.psum((neigh_part, self_part, bias_part), "node")
    scale = float(node_rows * lax.axis_size("node")) ** (-0.5)
    delta_agg = jnp.einsum(
        "nh,fh->nf", delta_full, w_neigh, preferred_element_type=jnp.float32
    ).astype(jnp.bfloat16)
    through_self = jnp.einsum("nh,fh->nf", delta_full, w_self, preferred_element_type=jnp.float32)
    delta_rows = delta_agg.reshape(row_blocks, block, width)

    def return_term(offset):
        window_slots = slot_range(offset)
        picked = delta_rows[row_ids[window_slots]]
        return jnp.einsum(
            "tab,taf->tbf", tile_values[window_slots], picked, preferred_element_type=jnp.float32
        )

    def placed_term(offset):
        return place_rows(col_onehot[:, slot_range(offset)], return_term(offset))

    back = placed_term(REACH)
    upward = placed_term(0)
    for distance in range(REACH, 0, -1):
        upward = from_behind(upward.astype(jnp.bfloat16), "node", -1).astype(upward.dtype)
        if distance > 1:
            upward = upward + placed_term(REACH - distance + 1)
    downward = placed_term(2 * REACH)
    for distance in range(REACH, 0, -1):
        downward = from_behind(downward.astype(jnp.bfloat16), "node", 1).astype(downward.dtype)
        if distance > 1:
            downward = downward + placed_term(REACH + distance - 1)
    back = back + upward + downward
    grad_nodes = (through_self + back.reshape(node_rows, width)).astype(jnp.bfloat16)
    return (hidden_out, grad_nodes, self_sum * scale, neigh_sum * scale, bias_sum * scale)


def solution(mesh):
    placed = (
        P("node", "feat"),
        P("node", None, None),
        P("node", None),
        P("node", None),
        P("node", None),
        P("node", None),
        P("feat", None),
        P("feat", None),
        P("feat"),
        P("node", "feat"),
    )
    return jax.shard_map(
        on_device,
        mesh=mesh,
        in_specs=placed,
        out_specs=(
            P("node", "feat"),
            P("node", "feat"),
            P("feat", None),
            P("feat", None),
            P("feat"),
        ),
        check_vma=False,
    )
```

profile of v0, /device:TPU:1, one launch (start us, length us, event | category | flops | bytes accessed | tf_op | source)
XLA Modules:
  0.0 752.5 jit_solution(578658103978517350)
XLA Ops:
  7.2 2.8 collective-permute-start
  15.8 3.2 fusion.20
  19.0 5.8 collective-permute-done.1
  26.7 2.6 gather_fusion.3
  29.3 3.6 collective-permute-start.3
  33.2 3.2 fusion.16
  36.7 3.1 fusion.18
  44.5 3.2 fusion.14
  47.6 1.8 gather_fusion.6
  49.8 4.4 add_convert_fusion.2
  56.7 3.2 convolution_add_fusion
  60.0 64.0 %reduce-scatter.2.cloned.1.call-done = f32[1024,512]{1,0:T(8,128)} async-done(((f32[1024,1024]{1,0:T(8,128)}), f32[1024,512]{1,0:T(8,128)}) %reduce-scatter.2.cloned.1.call-update) | async-done | bytes 2097168 | tf_op jit(solution)/shard_map/reduce_scatter | solution.py:74
  124.1 4.0 convert_reduce_fusion
  128.5 36.3 %all-gather.2.cloned.1.call-done = bf16[1024,1024]{1,0:T(8,128)(2,1)} async-done(((bf16[1024,512]{1,0:T(8,128)(2,1)}), bf16[1024,1024]{1,0:T(8,128)(2,1)}) %all-gather.2.cloned.1.call-update) | async-done | bytes 2097168 | tf_op jit(solution)/shard_map/all_gather | solution.py:81
  164.8 2.9 convolution_convert_fusion.2
  168.3 4.6 convolution_bitcast_fusion
  172.9 2.6 fusion.46
  176.0 2.8 convolution_convert_fusion
  181.6 2.9 convolution_convert_fusion.1
  186.5 7.2 collective-permute-done.6
  193.7 3.6 add_convert_fusion
  197.3 2.5 collective-permute-start.7
  200.8 3.6 add_convert_fusion.1
  204.4 2.4 collective-permute-start.5
  206.8 148.3 %psum.23 = f32[512]{0:T(512)S(1)} all-reduce(f32[512]{0:T(512)S(1)} %get-tuple-element.17), channel_id=1, replica_groups=mesh['node'=64,'feat'=2] {'node'}, use_global_device_ids=true, to_apply=%region_4.5 | all-reduce | flops 512 | bytes 4096 | tf_op jit(solution)/shard_map/psum | solution.py:85
  356.7 1.9 fusion.11
  358.6 2.0 convert_add_fusion
  362.5 2.3 fusion
  364.8 370.6 %all-reduce.3.cloned.1.call-done = (f32[512,1024]{0,1:T(8,128)}, f32[512,1024]{0,1:T(8,128)}) async-done(((f32[512,1024]{0,1:T(8,128)}, f32[512,1024]{0,1:T(8,128)}), (f32[512,1024]{0,1:T(8,128)}, f32[512,1024]{0,1:T(8,128)})) %all-reduce.3.cloned.1.call-update) | async-done | bytes 4194320 | tf_op jit(solution)/shard_map/psum | solution.py:85
  735.4 4.7 broadcast_multiply_fusion
  740.1 2.9 copy.22
  743.0 3.0 copy.23
  (87 shorter events, 26.6 us)
Async XLA Ops:
  7.2 48.3 %copy-start = (bf16[512,1024]{1,0:T(8,128)(2,1)S(1)}, bf16[512,1024]{1,0:T(8,128)(2,1)}, u32[]{:S(2)}) copy-start(bf16[512,1024]{1,0:T(8,128)(2,1)} %param.17) | copy-start | bytes 3145732
  7.2 7.6 %copy-start.2 = (bf16[1024,512]{1,0:T(8,128)(2,1)S(1)}, bf16[1024,512]{1,0:T(8,128)(2,1)}, u32[]{:S(2)}) copy-start(bf16[1024,512]{1,0:T(8,128)(2,1)} %param.10) | copy-start | bytes 3145732
  7.2 8.2 %copy-start.10 = (s32[1,20]{1,0:T(1,128)S(1)}, s32[1,20]{1,0:T(1,128)}, u32[]{:S(2)}) copy-start(s32[1,20]{1,0:T(1,128)} %param.12) | copy-start | bytes 244
  7.2 116.9 %reduce-scatter.2.cloned.1.call-start = ((), (), s32[]{:S(2)}) async-start(), calls=%async_computation.1 | async-start | bytes 6291456 | tf_op jit(solution)/shard_map/reduce_scatter | solution.py:74
  7.2 19.4 %collective-permute-start = (bf16[1024,512]{1,0:T(8,128)(2,1)}, bf16[1024,512]{1,0:T(8,128)(2,1)}, u32[]{:S(2)}, u32[]{:S(2)}) collective-permute-start(bf16[1024,512]{1,0:T(8,128)(2,1)} %param.10), channel_id=1, source_target_pairs={{126,0},{0,2},{2,4},{4,6},{6,8},{8,10},{10,12},{12,14},{14,16},{16... | collective-permute-start | bytes 3145736 | tf_op jit(solution)/shard_map/ppermute | solution.py:13
  10.0 14.8 %collective-permute-start.1 = (bf16[1024,512]{1,0:T(8,128)(2,1)}, bf16[1024,512]{1,0:T(8,128)(2,1)}, u32[]{:S(2)}, u32[]{:S(2)}) collective-permute-start(bf16[1024,512]{1,0:T(8,128)(2,1)} %param.10), channel_id=1, source_target_pairs={{2,0},{4,2},{6,4},{8,6},{10,8},{12,10},{14,12},{16,14},{18,16},{20... | collective-permute-start | bytes 3145736 | tf_op jit(solution)/shard_map/ppermute | solution.py:13
  29.3 7.1 copy-start.3
  29.3 12.1 %collective-permute-start.2 = (bf16[1024,512]{1,0:T(8,128)(2,1)}, bf16[1024,512]{1,0:T(8,128)(2,1)S(1)}, u32[]{:S(2)}, u32[]{:S(2)}) collective-permute-start(bf16[1024,512]{1,0:T(8,128)(2,1)} %collective-permute-done), channel_id=1, source_target_pairs={{126,0},{0,2},{2,4},{4,6},{6,8},{8,10},{10,12},{12,14},{14,16},{16... | collective-permute-start | bytes 3145736 | tf_op jit(solution)/shard_map/ppermute | solution.py:13
  29.3 18.4 %collective-permute-start.3 = (bf16[1024,512]{1,0:T(8,128)(2,1)}, bf16[1024,512]{1,0:T(8,128)(2,1)}, u32[]{:S(2)}, u32[]{:S(2)}) collective-permute-start(bf16[1024,512]{1,0:T(8,128)(2,1)} %collective-permute-done.1), channel_id=1, source_target_pairs={{2,0},{4,2},{6,4},{8,6},{10,8},{12,10},{14,12},{16,14},{18,16},{20... | collective-permute-start | bytes 3145736 | tf_op jit(solution)/shard_map/ppermute | solution.py:13
  41.3 1.0 copy-start.9
  54.5 1.0 copy-start.6
  55.5 1.3 copy-start.4
  59.9 64.1 %copy-start.8 = (bf16[1024,512]{1,0:T(8,128)(2,1)S(1)}, bf16[1024,512]{1,0:T(8,128)(2,1)}, u32[]{:S(2)}) copy-start(bf16[1024,512]{1,0:T(8,128)(2,1)} %param.19) | copy-start | bytes 3145732
  59.9 64.1 %copy-start.12 = (f32[512]{0:T(512)S(1)}, f32[512]{0:T(512)}, u32[]{:S(2)}) copy-start(f32[512]{0:T(512)} %param.18) | copy-start | bytes 6148
  60.0 68.5 %copy-start.11 = (s32[1,20]{1,0:T(1,128)S(1)}, s32[1,20]{1,0:T(1,128)}, u32[]{:S(2)}) copy-start(s32[1,20]{1,0:T(1,128)} %param.13) | copy-start | bytes 244
  60.0 104.8 %all-gather.2.cloned.1.call-start = ((), (), s32[]{:S(2)}) async-start(), calls=%async_computation.2 | async-start | bytes 3145728 | tf_op jit(solution)/shard_map/all_gather | solution.py:81
  128.1 607.3 %all-reduce.3.cloned.1.call-start = ((), (), s32[]{:S(2)}) async-start(), calls=%async_computation.3 | async-start | bytes 8388608 | tf_op jit(solution)/shard_map/psum | solution.py:85
  168.3 4.6 copy-start.7
  168.3 4.6 copy-start.13
  178.8 14.9 %collective-permute-start.6 = (bf16[8,128,512]{2,0,1:T(8,128)(2,1)}, bf16[8,128,512]{2,0,1:T(8,128)(2,1)}, u32[]{:S(2)}, u32[]{:S(2)}) collective-permute-start(bf16[8,128,512]{2,0,1:T(8,128)(2,1)} %convolution_convert_fusion), channel_id=1, source_target_pairs={{126,0},{0,2},{2,4},{4,6},{6,8},{8,10},{10,12},{12,14},{14,16},{16... | collective-permute-start | bytes 3145736 | tf_op jit(solution)/shard_map/ppermute | solution.py:13
  184.5 16.2 %collective-permute-start.4 = (bf16[8,128,512]{2,0,1:T(8,128)(2,1)}, bf16[8,128,512]{2,0,1:T(8,128)(2,1)}, u32[]{:S(2)}, u32[]{:S(2)}) collective-permute-start(bf16[8,128,512]{2,0,1:T(8,128)(2,1)} %convolution_convert_fusion.1), channel_id=1, source_target_pairs={{2,0},{4,2},{6,4},{8,6},{10,8},{12,10},{14,12},{16,14},{18,16},{20... | collective-permute-start | bytes 3145736 | tf_op jit(solution)/shard_map/ppermute | solution.py:13
  197.3 161.2 %collective-permute-start.7 = (bf16[8,128,512]{2,0,1:T(8,128)(2,1)}, bf16[8,128,512]{2,0,1:T(8,128)(2,1)}, u32[]{:S(2)}, u32[]{:S(2)}) collective-permute-start(bf16[8,128,512]{2,0,1:T(8,128)(2,1)} %add_convert_fusion), channel_id=1, source_target_pairs={{126,0},{0,2},{2,4},{4,6},{6,8},{8,10},{10,12},{12,14},{14,16},{16... | collective-permute-start | bytes 3145736 | tf_op jit(solution)/shard_map/ppermute | solution.py:13
  204.4 154.2 %collective-permute-start.5 = (bf16[8,128,512]{2,0,1:T(8,128)(2,1)}, bf16[8,128,512]{2,0,1:T(8,128)(2,1)}, u32[]{:S(2)}, u32[]{:S(2)}) collective-permute-start(bf16[8,128,512]{2,0,1:T(8,128)(2,1)} %add_convert_fusion.1), channel_id=1, source_target_pairs={{2,0},{4,2},{6,4},{8,6},{10,8},{12,10},{14,12},{16,14},{18,16},{20... | collective-permute-start | bytes 3145736 | tf_op jit(solution)/shard_map/ppermute | solution.py:13
  360.6 1.2 copy-start.5
  360.6 1.9 copy-start.14
  743.0 3.0 copy-start.1
Sparse Core Ops, SparseCore 0:
  60.1 63.9 reduce-scatter.1
  128.2 36.5 all-gather.1
  175.7 559.6 all-reduce.2
where the time goes:
time: 753 us; the launch traced here: 752 us
  waiting for transfers between devices  486 us (65%)
  blocking collectives  148 us (20%)
  matrix products  52.5 us (7%)
  local copies, waits for them, and re-layouts  24.7 us (3%)
  between operations  14.1 us (2%)
  starting transfers between devices  13.3 us (2%)
  other arithmetic  13.1 us (2%)
    psum x1, waiting for transfers between devices, on_device(): lax.psum((neigh_part, self_part, bias_part), 'node')  371 us
    psum x1, blocking collectives, on_device(): lax.psum((neigh_part, self_part, bias_part), 'node')  148 us
    reduce_scatter x1, waiting for transfers between devices, on_device(): lax.psum_scatter(partial_sum, 'feat', scatter_dimension=1, tiled=True)  64 us
    all_gather x1, waiting for transfers between devices, on_device(): delta_full = lax.all_gather(delta, 'feat', axis=1, tiled=True)  36.3 us
    dot_general x10, matrix products, place_rows(): jnp.einsum('rt,tbf->rbf', onehot, values, precision=lax.Precision.HIGHEST)  31.9 us
    ppermute x8, waiting for transfers between devices, from_behind(): return lax.ppermute(block, axis, route)  15.5 us
  transfers between devices with their start and end apart: 11, of which 7 were waited for; matrix products, arithmetic and copies ran while one was open for 6% of the time, Pallas kernels for 0%

commit v1 on v0

v1 whole, which is shorter than its diff:
```python
import jax
import jax.numpy as jnp
from jax import lax
from jax.experimental import pallas as pl
from jax.experimental.pallas import tpu as pltpu
from jax.sharding import Mesh, PartitionSpec as P

REACH = 2
PAIR_MAX = 4
BLOCK = 128
OFFSETS = (0, 1, 3, 4)
NODE = ("xl", "z", "y", "c")
CHIPS = ("xl", "z", "y")
VMEM = pl.BlockSpec(memory_space=pltpu.VMEM)
SMEM = pl.BlockSpec(memory_space=pltpu.SMEM)
BF = jnp.bfloat16
F32 = jnp.float32
MIB = 1 << 20


def dot(a, b, dims=((1,), (0,))):
    return lax.dot_general(a, b, (dims, ((), ())), preferred_element_type=F32)


def shift(block, distance):
    count = lax.axis_size(NODE)
    return lax.ppermute(block, NODE, [(i, (i + distance) % count) for i in range(count)])


def swap(block, axis):
    return lax.ppermute(block, axis, [(0, 1), (1, 0)])


def call(kernel, outs, in_specs, scratch=(), flops=0, moved=0, vmem=24):
    return pl.pallas_call(
        kernel,
        out_shape=outs,
        in_specs=in_specs,
        out_specs=[VMEM] * len(outs),
        scratch_shapes=list(scratch),
        compiler_params=pltpu.CompilerParams(vmem_limit_bytes=vmem * MIB),
        cost_estimate=pl.CostEstimate(flops=flops, bytes_accessed=moved, transcendentals=0),
    )


def shape(dims, kind):
    return jax.ShapeDtypeStruct(dims, kind)


def pick_kernel(cols, x, *outs):
    for i, out in enumerate(outs):
        for s in range(PAIR_MAX):
            out[s] = x[cols[i, s]]


def aggregate_kernel(place, row, col, tile, count, x, h0, h1, h3, h4, tiles, w_neigh, w_self, agg, send0, send1, acc):
    halos = (h0, h1, None, h3, h4)
    acc[...] = jnp.zeros_like(acc)
    for j in range(5 * PAIR_MAX):
        k, s = divmod(j, PAIR_MAX)

        @pl.when(s < count[0, k])
        def _():
            block = x[col[0, j]] if k == REACH else halos[k][s]
            acc[row[0, j]] += dot(tiles[tile[0, j]], block)

    half = send0.shape[1]
    other = (1 - place[0]) * (2 * half)

    def rows(r, _):
        mine = acc[r].astype(BF)
        agg[r] = mine
        for c, send in enumerate((send0, send1)):
            cols = pl.ds(pl.multiple_of(other + c * half, 128), half)
            send[pl.ds(pl.multiple_of(r * BLOCK, BLOCK), BLOCK), :] = (
                dot(mine, w_neigh[:, cols]) + dot(x[r], w_self[:, cols])
            ).astype(BF)
        return 0

    lax.fori_loop(0, x.shape[0], rows, 0)


def own_kernel(place, agg, x, w_neigh, w_self, bias, out):
    width = out.shape[1]
    cols = pl.ds(pl.multiple_of(place[0] * width, 128), width)
    out[...] = dot(agg[...], w_neigh[:, cols]) + dot(x[...], w_self[:, cols]) + bias[...]


def act_kernel(own, recv, cot, *rest):
    hidden, delta, sums = rest[-3:]
    pre = own[...] + recv[...].astype(F32)
    sigma = jax.nn.sigmoid(pre)
    hidden[...] = (pre * sigma).astype(BF)
    d = (cot[...].astype(F32) * sigma * (1.0 + pre * (1.0 - sigma))).astype(BF)
    delta[...] = d

    @pl.when(pl.program_id(0) == 0)
    def _():
        sums[...] = jnp.zeros_like(sums)

    sums[...] += jnp.sum(d.astype(F32).reshape(-1, 8, d.shape[1]), axis=0)


def weight_kernel(place, agg, x, d0, d1, send, keep):
    half = d0.shape[1]
    core = place[1]

    def cols(i, _):
        at = pl.ds(pl.multiple_of(i * BLOCK, BLOCK), BLOCK)
        for c, d in enumerate((d0, d1)):
            neigh = dot(agg[:, at], d[...], ((0,), (0,)))
            own = dot(x[:, at], d[...], ((0,), (0,)))
            first = core == 0
            span = slice(c * half, (c + 1) * half)
            send[at, span] = jnp.where(first, own, neigh).astype(BF)
            keep[at, span] = jnp.where(first, neigh, own)
        return 0

    lax.fori_loop(0, agg.shape[1] // BLOCK, cols, 0)


def back_kernel(place, row, col, tile, count, own0, own1, far0, far1, tiles, w_neigh, w_self, o0, o1, o3, o4, base, dagg):
    outs = (o0, o1, None, o3, o4)
    half = own0.shape[1]
    mine, other = place[0] * (2 * half), (1 - place[0]) * (2 * half)

    def rows(r, _):
        at = pl.ds(pl.multiple_of(r * BLOCK, BLOCK), BLOCK)
        to_neigh = jnp.zeros((BLOCK, dagg.shape[2]), F32)
        to_self = jnp.zeros((BLOCK, dagg.shape[2]), F32)
        for d, start in ((own0, mine), (own1, mine + half), (far0, other), (far1, other + half)):
            cols = pl.ds(pl.multiple_of(start, 128), half)
            to_neigh += dot(d[at, :], w_neigh[:, cols], ((1,), (1,)))
            to_self += dot(d[at, :], w_self[:, cols], ((1,), (1,)))
        dagg[r] = to_neigh.astype(BF)
        base[r] = to_self
        return 0

    lax.fori_loop(0, base.shape[0], rows, 0)
    for j in range(5 * PAIR_MAX):
        k, s = divmod(j, PAIR_MAX)
        weight = tiles[tile[0, j]]
        live = s < count[0, k]
        if k == REACH:

            @pl.when(live)
            def _():
                base[col[0, j]] += dot(weight, dagg[row[0, j]], ((0,), (0,)))
        else:

            @pl.when(live)
            def _():
                outs[k][s] = dot(weight, dagg[row[0, j]], ((0,), (0,))).astype(BF)

            @pl.when(jnp.logical_not(live))
            def _():
                outs[k][s] = jnp.zeros(outs[k].shape[1:], BF)


def place_kernel(cols, base, r0, r1, r3, r4, out, acc):
    acc[...] = base[...]
    for i, r in enumerate((r0, r1, r3, r4)):
        for s in range(PAIR_MAX):
            acc[cols[i, s]] += r[s].astype(F32)
    out[...] = acc[...].astype(BF)


def assemble_kernel(place, own_mine, own_swap, far_mine, far_swap, neigh, self_):
    width = own_mine.shape[1]
    core = place[1] == 0
    for a, b, side in ((own_mine, own_swap, place[0]), (far_mine, far_swap, 1 - place[0])):
        cols = pl.ds(pl.multiple_of(side * width, 128), width)
        neigh[:, cols] = jnp.where(core, a[...], b[...]).astype(F32)
        self_[:, cols] = jnp.where(core, b[...], a[...]).astype(F32)


def reduce_nodes(parts, scale):
    moved = lax.all_to_all(parts, CHIPS, 0, 0)
    total = jnp.sum(moved.astype(F32), axis=0) * scale
    return total


def spread(total):
    chips = lax.axis_size(CHIPS)
    whole = lax.all_to_all(jnp.broadcast_to(total.astype(BF)[None], (chips, *total.shape)), CHIPS, 0, 0)
    return whole.reshape(chips * total.shape[0], total.shape[1])


def on_device(node_feats, edge_tiles, slot_row, slot_col, slot_tile, slot_count, w_self, w_neigh, bias, cotangent):
    nodes, width = node_feats.shape
    blocks = nodes // BLOCK
    half = width // 2
    chips = lax.axis_size(CHIPS)
    piece = width // chips
    place = jnp.stack([lax.axis_index("f"), lax.axis_index("c")]).astype(jnp.int32)
    scale = float(nodes * lax.axis_size(NODE)) ** (-0.5)
    x = node_feats.reshape(blocks, BLOCK, width)
    lists = (place, slot_row, slot_col, slot_tile, slot_count)

    wanted = jnp.concatenate(
        [shift(slot_col[:, k * PAIR_MAX : (k + 1) * PAIR_MAX], k - REACH) for k in OFFSETS], axis=0
    )
    slab = shape((PAIR_MAX, BLOCK, width), BF)
    picked = call(pick_kernel, [slab] * 4, [SMEM, VMEM], moved=3 * MIB)(wanted, x)
    halos = [shift(p, REACH - k) for k, p in zip(OFFSETS, picked)]

    agg, send0, send1 = call(
        aggregate_kernel,
        [shape((blocks, BLOCK, width), BF)] + [shape((nodes, half), BF)] * 2,
        [SMEM] * 5 + [VMEM] * 8,
        [pltpu.VMEM((blocks, BLOCK, width), F32)],
        flops=2 * 10**9,
        moved=8 * MIB,
    )(*lists, x, *halos, edge_tiles, w_neigh, w_self)
    recv = [swap(send0, "f"), swap(send1, "f")]
    aggregate = agg.reshape(nodes, width)

    tall = nodes // 4
    own = pl.pallas_call(
        own_kernel,
        grid=(4,),
        out_shape=shape((nodes, width), F32),
        in_specs=[
            SMEM,
            pl.BlockSpec((tall, width), lambda i: (i, 0)),
            pl.BlockSpec((tall, width), lambda i: (i, 0)),
            pl.BlockSpec(w_neigh.shape, lambda i: (0, 0)),
            pl.BlockSpec(w_self.shape, lambda i: (0, 0)),
            pl.BlockSpec((1, width), lambda i: (0, 0)),
        ],
        out_specs=pl.BlockSpec((tall, width), lambda i: (i, 0)),
        compiler_params=pltpu.CompilerParams(vmem_limit_bytes=24 * MIB),
        cost_estimate=pl.CostEstimate(flops=10**9, bytes_accessed=6 * MIB, transcendentals=0),
    )(place, aggregate, node_feats, w_neigh, w_self, bias.reshape(1, width))

    hidden = None
    delta, sums = [], []
    for c in range(2):
        column = pl.BlockSpec((tall, half), lambda i, c=c: (i, c))
        alone = pl.BlockSpec((tall, half), lambda i: (i, 0))
        extra = [] if c == 0 else [hidden]
        hidden, d, s = pl.pallas_call(
            act_kernel,
            grid=(4,),
            out_shape=[shape((nodes, width), BF), shape((nodes, half), BF), shape((8, half), F32)],
            in_specs=[column, alone, column] + [pl.BlockSpec(memory_space=pl.ANY)] * len(extra),
            out_specs=[column, alone, pl.BlockSpec((8, half), lambda i: (0, 0))],
            input_output_aliases={3: 0} if extra else {},
            compiler_params=pltpu.CompilerParams(vmem_limit_bytes=24 * MIB),
            cost_estimate=pl.CostEstimate(flops=10**7, bytes_accessed=3 * MIB, transcendentals=10**6),
        )(own, recv[c], cotangent, *extra)
        delta.append(d)
        sums.append(s)
    far = [swap(d, "f") for d in delta]

    def weights(d0, d1):
        return call(
            weight_kernel,
            [shape((width, width), BF), shape((width, width), F32)],
            [SMEM] + [VMEM] * 4,
            flops=10**9,
            moved=5 * MIB,
        )(place, aggregate, node_feats, d0, d1)

    def high_low(v):
        high = v.astype(BF)
        low = (v - high.astype(F32)).astype(BF)
        return jnp.concatenate([high, low, jnp.zeros((6, v.shape[1]), BF)], axis=0)

    bias_part = jnp.sum(jnp.concatenate(sums, axis=1), axis=0, keepdims=True)
    send, keep = weights(*delta)
    got, bias_got = swap(send, "c"), swap(bias_part, "c")
    parts = (keep + got.astype(F32)).astype(BF).reshape(chips, piece, width)
    bias_rows = jnp.broadcast_to(high_low(bias_part + bias_got)[None], (chips, 8, width))
    total = reduce_nodes(jnp.concatenate([parts, bias_rows], axis=1), scale)
    own_mine = spread(total[:piece])
    own_swap = swap(own_mine, "c")
    grad_bias = total[piece] + total[piece + 1]

    *outward, base = call(
        back_kernel,
        [slab] * 4 + [shape((blocks, BLOCK, width), F32)],
        [SMEM] * 5 + [VMEM] * 7,
        [pltpu.VMEM((blocks, BLOCK, width), BF)],
        flops=2 * 10**9,
        moved=10 * MIB,
    )(*lists, *delta, *far, edge_tiles, w_neigh, w_self)
    returned = [shift(o, k - REACH) for k, o in zip(OFFSETS, outward)]

    send, keep = weights(*far)
    parts = (keep + swap(send, "c").astype(F32)).astype(BF).reshape(chips, piece, width)
    far_mine = spread(reduce_nodes(parts, scale))
    far_swap = swap(far_mine, "c")

    grad_nodes = call(
        place_kernel,
        [shape((blocks, BLOCK, width), BF)],
        [SMEM] + [VMEM] * 5,
        [pltpu.VMEM((blocks, BLOCK, width), F32)],
        moved=5 * MIB,
    )(wanted, base, *returned)[0].reshape(nodes, width)

    grad_neigh, grad_self = call(
        assemble_kernel,
        [shape((width, 2 * width), F32)] * 2,
        [SMEM] + [VMEM] * 4,
        moved=6 * MIB,
    )(place, own_mine, own_swap, far_mine, far_swap)
    return hidden, grad_nodes, grad_self, grad_neigh, grad_bias


def solution(mesh):
    fine = Mesh(mesh.devices.reshape(2, 4, 4, 2, 2), (*NODE, "f"))
    placed = (
        P(NODE, "f"),
        P(NODE, None, None),
        P(NODE, None),
        P(NODE, None),
        P(NODE, None),
        P(NODE, None),
        P("f", None),
        P("f", None),
        P("f"),
        P(NODE, "f"),
    )
    return jax.shard_map(
        on_device,
        mesh=fine,
        in_specs=placed,
        out_specs=(P(NODE, "f"), P(NODE, "f"), P("f", None), P("f", None), P("f")),
        check_vma=False,
    )
```

time: 753 us -> 222 us (0.29)
  waiting for transfers between devices: 486 us -> 94.2 us
  blocking collectives: 148 us -> 0 us
  matrix products: 52.5 us -> 0 us
  starting transfers between devices: 13.3 us -> 65.3 us
  Pallas kernels: 0 us -> 37.3 us
  between operations: 14.1 us -> 0.89 us
  other arithmetic: 13.1 us -> 3.05 us
    psum x1 -> x0, waiting for transfers between devices: 371 us -> none  [on_device(): lax.psum((neigh_part, self_part, bias_part), 'node')]
    psum x1 -> x0, blocking collectives: 148 us -> none  [on_device(): lax.psum((neigh_part, self_part, bias_part), 'node')]
    reduce_scatter x1 -> x0, waiting for transfers between devices: 64 us -> none  [on_device(): lax.psum_scatter(partial_sum, 'feat', scatter_dimension=1, tiled=True)]
    dot_general x26 -> x0, matrix products: 52.5 us -> none  [the longest x10 31.9 us: place_rows(): jnp.einsum('rt,tbf->rbf', onehot, values, precision=lax.Precision.HIGHEST)]
    ppermute x8 -> x21, waiting for transfers between devices: 15.5 us -> 66 us  [the longest x12 33.2 us: shift(): lax.ppermute(block, NODE, [(i, (i + distance) % count) for i in range(cou...]
    pallas_call x0 -> x10, Pallas kernels: none -> 37.3 us  [the longest x1 11.6 us: on_device(): call(back_kernel, [slab] * 4 + [shape((blocks, BLOCK, width), F32)], [SME...]
    all_gather x1 -> x0, waiting for transfers between devices: 36.3 us -> none  [on_device(): delta_full = lax.all_gather(delta, 'feat', axis=1, tiled=True)]
    ppermute x8 -> x21, starting transfers between devices: 13 us -> 43.9 us  [the longest x12 26.7 us: shift(): lax.ppermute(block, NODE, [(i, (i + distance) % count) for i in range(cou...]
  transfers between devices with their start and end apart: 11 -> 25, of which waited for: 7 -> 14; matrix products, arithmetic and copies ran while one was open for 6% -> 2% of each run, Pallas kernels for 0% -> 11%
where the time goes in v1:
time: 222 us; the launch traced here: 221 us
  waiting for transfers between devices  94.2 us (42%)
  starting transfers between devices  65.3 us (29%)
  Pallas kernels  37.3 us (17%)
  local copies, waits for them, and re-layouts  20.6 us (9%)
  other arithmetic  3.05 us (1%)
    ppermute x12, waiting for transfers between devices, shift(): lax.ppermute(block, NODE, [(i, (i + distance) % count) for i in range(cou...  33.2 us
    ppermute x9, waiting for transfers between devices, swap(): return lax.ppermute(block, axis, [(0, 1), (1, 0)])  32.8 us
    ppermute x12, starting transfers between devices, shift(): lax.ppermute(block, NODE, [(i, (i + distance) % count) for i in range(cou...  26.7 us
    all_to_all x2, waiting for transfers between devices, reduce_nodes(): moved = lax.all_to_all(parts, CHIPS, 0, 0)  21.9 us
    unnamed x62, local copies, waits for them, and re-layouts  17.9 us
    ppermute x9, starting transfers between devices, swap(): return lax.ppermute(block, axis, [(0, 1), (1, 0)])  17.3 us
    all_to_all x2, starting transfers between devices, reduce_nodes(): moved = lax.all_to_all(parts, CHIPS, 0, 0)  12.8 us
    pallas_call x1, Pallas kernels, on_device(): call(back_kernel, [slab] * 4 + [shape((blocks, BLOCK, width), F32)], [SME...  11.6 us
  transfers between devices with their start and end apart: 25, of which 14 were waited for; matrix products, arithmetic and copies ran while one was open for 2% of the time, Pallas kernels for 11%

profile of v1, /device:TPU:1, one launch (start us, length us, event | category | flops | bytes accessed | tf_op | source)
XLA Modules:
  0.0 221.4 jit_solution(10279238425029503762)
XLA Ops:
  1.5 8.0 %collective-permute-start = (s32[1,4]{1,0:T(1,128)S(1)}, s32[1,4]{1,0:T(1,128)S(1)}, u32[]{:S(2)}, u32[]{:S(2)}) collective-permute-start(s32[1,4]{1,0:T(1,128)S(1)} %get-tuple-element.55), channel_id=1, source_target_pairs={{0,124},{2,126},{4,0},{6,2},{8,4},{10,6},{12,8},{14,10},{16,12},{1... | collective-permute-start | bytes 56 | tf_op jit(solution)/shard_map/ppermute | solution.py:27
  10.4 5.6 %collective-permute-done.3 = s32[1,4]{1,0:T(1,128)S(1)} collective-permute-done((s32[1,4]{1,0:T(1,128)S(1)}, s32[1,4]{1,0:T(1,128)S(1)}, u32[]{:S(2)}, u32[]{:S(2)}) %collective-permute-start.3) | collective-permute-done | bytes 48 | tf_op jit(solution)/shard_map/ppermute | solution.py:27
  18.8 2.1 collective-permute-start.6
  20.9 6.0 %collective-permute-start.7 = (bf16[4,128,512]{2,1,0:T(8,128)(2,1)S(1)}, bf16[4,128,512]{2,1,0:T(8,128)(2,1)}, u32[]{:S(2)}, u32[]{:S(2)}) collective-permute-start(bf16[4,128,512]{2,1,0:T(8,128)(2,1)S(1)} %get-tuple-element.32), channel_id=1, source_target_pairs={{0,124},{2,126},{4,0},{6,2},{8,4},{10,6},{12,8},{14,10},{16,12},{1... | collective-permute-start | bytes 1572872 | tf_op jit(solution)/shard_map/ppermute | solution.py:27
  27.0 10.5 %collective-permute-done.4.h0 = bf16[4,128,512]{2,1,0:T(8,128)(2,1)S(1)} collective-permute-done((bf16[4,128,512]{2,1,0:T(8,128)(2,1)}, bf16[4,128,512]{2,1,0:T(8,128)(2,1)S(1)}, u32[]{:S(2)}, u32[]{:S(2)}) %collective-permute-start.4) | collective-permute-done | bytes 524320 | tf_op jit(solution)/shard_map/ppermute | solution.py:27
  45.8 6.7 %shard_map.138 = (bf16[8,128,512]{2,1,0:T(8,128)(2,1)S(1)}, bf16[1024,256]{1,0:T(8,128)(2,1)S(1)}, bf16[1024,256]{1,0:T(8,128)(2,1)S(1)}) custom-call(s32[2]{0:T(128)S(1)} %pad_add_fusion.1.place, s32[1,20]{1,0:T(1,128)S(1)} %copy-done.25, s32[1,20]{1,0:T(1,128)S(1)} %copy-done.9, s32[1,20]{1,0:T(1,128)S(1)} %copy-done.27, s32[1,5]{1,0:T(1,128)S(1)} %copy-done.29, ...), custom_call_target="tpu_custom_call" | custom-call | flops 2000000000 | bytes 8388608 | tf_op jit(solution)/shard_map/pallas_call | solution.py:207
  52.5 2.5 %collective-permute-start.9 = (bf16[1024,256]{1,0:T(8,128)(2,1)S(1)}, bf16[1024,256]{1,0:T(8,128)(2,1)S(1)}, u32[]{:S(2)}, u32[]{:S(2)}) collective-permute-start(bf16[1024,256]{1,0:T(8,128)(2,1)S(1)} %get-tuple-element.35), channel_id=1, source_target_pairs={{0,1},{1,0},{2,3},{3,2},{4,5},{5,4},{6,7},{7,6},{8,9},{9,8},{10,11... | collective-permute-start | bytes 1572872 | tf_op jit(solution)/shard_map/ppermute | solution.py:31
  55.6 2.4 %shard_map.139.own = f32[1024,512]{1,0:T(8,128)S(1)} custom-call(s32[2]{0:T(128)S(1)} %pad_add_fusion.1.place, bf16[1024,512]{1,0:T(8,128)(2,1)S(1)} %bitcast.18, bf16[1024,512]{1,0:T(8,128)(2,1)S(1)} %copy-done.2, bf16[512,1024]{1,0:T(8,128)(2,1)S(1)} %copy-done.4, bf16[512,1024]{1,0:T(8,128)(2,1)S(1)} %copy-done.7, f32[1,512]{1,0:T(1,128)S(1)} %bitcast.21), custom_call_target="tpu_custom_call" | custom-call | flops 1000000000 | bytes 6291456 | tf_op jit(solution)/shard_map/pallas_call | solution.py:219
  58.0 4.1 %collective-permute-done.9.recv = bf16[1024,256]{1,0:T(8,128)(2,1)S(1)} collective-permute-done((bf16[1024,256]{1,0:T(8,128)(2,1)S(1)}, bf16[1024,256]{1,0:T(8,128)(2,1)S(1)}, u32[]{:S(2)}, u32[]{:S(2)}) %collective-permute-start.9) | collective-permute-done | bytes 524320 | tf_op jit(solution)/shard_map/ppermute | solution.py:31
  62.1 1.9 shard_map.140
  64.0 8.9 %collective-permute-done.8.recv = bf16[1024,256]{1,0:T(8,128)(2,1)S(1)} collective-permute-done((bf16[1024,256]{1,0:T(8,128)(2,1)S(1)}, bf16[1024,256]{1,0:T(8,128)(2,1)S(1)}, u32[]{:S(2)}, u32[]{:S(2)}) %collective-permute-start.8) | collective-permute-done | bytes 524320 | tf_op jit(solution)/shard_map/ppermute | solution.py:31
  72.8 1.9 shard_map.141
  74.7 6.9 %collective-permute-start.17 = (f32[1,512]{1,0:T(1,128)S(1)}, f32[1,512]{1,0:T(1,128)S(1)}, u32[]{:S(2)}, u32[]{:S(2)}) collective-permute-start(f32[1,512]{1,0:T(1,128)S(1)} %bitcast.24), channel_id=1, source_target_pairs={{0,2},{2,0},{1,3},{3,1},{4,6},{6,4},{5,7},{7,5},{8,10},{10,8},{9,1... | collective-permute-start | bytes 6152 | tf_op jit(solution)/shard_map/ppermute | solution.py:31
  81.6 2.4 %collective-permute-start.11 = (bf16[1024,256]{1,0:T(8,128)(2,1)S(1)}, bf16[1024,256]{1,0:T(8,128)(2,1)S(1)}, u32[]{:S(2)}, u32[]{:S(2)}) collective-permute-start(bf16[1024,256]{1,0:T(8,128)(2,1)S(1)} %get-tuple-element.39.own1.d1), channel_id=1, source_target_pairs={{0,1},{1,0},{2,3},{3,2},{4,5},{5,4},{6,7},{7,6},{8,9},{9,8},{10,11... | collective-permute-start | bytes 1572872 | tf_op jit(solution)/shard_map/ppermute | solution.py:31
  84.6 2.5 %shard_map.144 = (bf16[512,512]{1,0:T(8,128)(2,1)S(1)}, f32[512,512]{1,0:T(8,128)S(1)}) custom-call(s32[2]{0:T(128)S(1)} %pad_add_fusion.1.place, bf16[1024,512]{1,0:T(8,128)(2,1)S(1)} %bitcast.19, bf16[1024,512]{1,0:T(8,128)(2,1)S(1)} %copy-done.2, bf16[1024,256]{1,0:T(8,128)(2,1)S(1)} %get-tuple-element.38.own0.d0, ...), custom_call_target="tpu_custom_call" | custom-call | flops 1000000000 | bytes 5242880 | tf_op jit(solution)/shard_map/pallas_call | solution.py:257
  87.9 8.7 %collective-permute-done.11.far1.d1 = bf16[1024,256]{1,0:T(8,128)(2,1)S(1)} collective-permute-done((bf16[1024,256]{1,0:T(8,128)(2,1)S(1)}, bf16[1024,256]{1,0:T(8,128)(2,1)S(1)}, u32[]{:S(2)}, u32[]{:S(2)}) %collective-permute-start.11) | collective-permute-done | bytes 524320 | tf_op jit(solution)/shard_map/ppermute | solution.py:31
  96.6 11.2 %collective-permute-done.10.far0.d0 = bf16[1024,256]{1,0:T(8,128)(2,1)S(1)} collective-permute-done((bf16[1024,256]{1,0:T(8,128)(2,1)S(1)}, bf16[1024,256]{1,0:T(8,128)(2,1)S(1)}, u32[]{:S(2)}, u32[]{:S(2)}) %collective-permute-start.10) | collective-permute-done | bytes 524320 | tf_op jit(solution)/shard_map/ppermute | solution.py:31
  107.8 2.5 %shard_map.145 = (bf16[512,512]{1,0:T(8,128)(2,1)S(1)}, f32[512,512]{1,0:T(8,128)S(1)}) custom-call(s32[2]{0:T(128)S(1)} %pad_add_fusion.1.place, bf16[1024,512]{1,0:T(8,128)(2,1)S(1)} %bitcast.20, bf16[1024,512]{1,0:T(8,128)(2,1)S(1)} %copy-done.2, bf16[1024,256]{1,0:T(8,128)(2,1)S(1)} %collective-permute-done.10.far0.d0, ...), custom_call_target="tpu_custom_call" | custom-call | flops 1000000000 | bytes 5242880 | tf_op jit(solution)/shard_map/pallas_call | solution.py:257
  112.5 7.5 %all-to-all-start = ((bf16[32,24,512]{2,1,0:T(8,128)(2,1)}), bf16[32,24,512]{2,1,0:T(8,128)(2,1)S(1)}, u32[]{:S(2)}, u32[]{:S(2)}) async-start(bf16[32,24,512]{2,1,0:T(8,128)(2,1)} %pad_maximum_fusion), calls=%async_computation | async-start | bytes 1572864 | tf_op jit(solution)/shard_map/all_to_all | solution.py:178
  121.0 12.1 %all-to-all-done = bf16[32,24,512]{2,1,0:T(8,128)(2,1)S(1)} async-done(((bf16[32,24,512]{2,1,0:T(8,128)(2,1)}), bf16[32,24,512]{2,1,0:T(8,128)(2,1)S(1)}, u32[]{:S(2)}, u32[]{:S(2)}) %all-to-all-start) | async-done | bytes 786464 | tf_op jit(solution)/shard_map/all_to_all | solution.py:178
  133.0 5.3 %all-to-all-start.2 = ((bf16[32,16,512]{2,1,0:T(8,128)(2,1)}), bf16[32,16,512]{2,1,0:T(8,128)(2,1)S(1)}, u32[]{:S(2)}, u32[]{:S(2)}) async-start(bf16[32,16,512]{2,1,0:T(8,128)(2,1)} %bitcast.9), calls=%async_computation.2 | async-start | bytes 1048576 | tf_op jit(solution)/shard_map/all_to_all | solution.py:178
  138.4 9.9 %all-to-all-done.2 = bf16[32,16,512]{2,1,0:T(8,128)(2,1)S(1)} async-done(((bf16[32,16,512]{2,1,0:T(8,128)(2,1)}), bf16[32,16,512]{2,1,0:T(8,128)(2,1)S(1)}, u32[]{:S(2)}, u32[]{:S(2)}) %all-to-all-start.2) | async-done | bytes 524320 | tf_op jit(solution)/shard_map/all_to_all | solution.py:178
  149.2 4.7 %all-to-all-start.1 = ((bf16[32,16,512]{2,1,0:T(8,128)(2,1)}), bf16[32,16,512]{2,1,0:T(8,128)(2,1)S(1)}, u32[]{:S(2)}, u32[]{:S(2)}) async-start(bf16[32,16,512]{2,1,0:T(8,128)(2,1)} %broadcast_in_dim.13), calls=%async_computation.1 | async-start | bytes 1048576 | tf_op jit(solution)/shard_map/all_to_all | solution.py:185
  161.6 11.6 %shard_map.142 = (bf16[4,128,512]{2,1,0:T(8,128)(2,1)}, bf16[4,128,512]{2,1,0:T(8,128)(2,1)S(1)}, bf16[4,128,512]{2,1,0:T(8,128)(2,1)S(1)}, bf16[4,128,512]{2,1,0:T(8,128)(2,1)S(1)}, f32[8,128,512]{2,1,0:T(8,128)S(1)}) custom-call(s32[2]{0:T(128)S(1)} %pad_add_fusion.1.place, s32[1,20]{1,0:T(1,128)S(1)} %copy-done.26, s32[1,20]{1,0:T(1,128)S(1)} %copy-done.10, ...), custom_call_target="tpu_custom_call" | custom-call | flops 2000000000 | bytes 10485760 | tf_op jit(solution)/shard_map/pallas_call | solution.py:280
  174.8 5.0 %collective-permute-start.12 = (bf16[4,128,512]{2,1,0:T(8,128)(2,1)}, bf16[4,128,512]{2,1,0:T(8,128)(2,1)}, u32[]{:S(2)}, u32[]{:S(2)}) collective-permute-start(bf16[4,128,512]{2,1,0:T(8,128)(2,1)} %get-tuple-element.41), channel_id=1, source_target_pairs={{0,124},{2,126},{4,0},{6,2},{8,4},{10,6},{12,8},{14,10},{16,12},{1... | collective-permute-start | bytes 1572872 | tf_op jit(solution)/shard_map/ppermute | solution.py:27
  180.7 3.9 %all-to-all-start.3 = ((bf16[32,16,512]{2,1,0:T(8,128)(2,1)}), bf16[32,16,512]{2,1,0:T(8,128)(2,1)S(1)}, u32[]{:S(2)}, u32[]{:S(2)}) async-start(bf16[32,16,512]{2,1,0:T(8,128)(2,1)} %broadcast_in_dim.28), calls=%async_computation.3 | async-start | bytes 1048576 | tf_op jit(solution)/shard_map/all_to_all | solution.py:185
  184.6 2.0 collective-permute-start.13
  190.6 2.0 collective-permute-done.12.r0
  192.6 6.2 %all-to-all-done.3 = bf16[32,16,512]{2,1,0:T(8,128)(2,1)S(1)} async-done(((bf16[32,16,512]{2,1,0:T(8,128)(2,1)}), bf16[32,16,512]{2,1,0:T(8,128)(2,1)S(1)}, u32[]{:S(2)}, u32[]{:S(2)}) %all-to-all-start.3) | async-done | bytes 524320 | tf_op jit(solution)/shard_map/all_to_all | solution.py:185
  200.5 13.8 %collective-permute-done.15.r4 = bf16[4,128,512]{2,1,0:T(8,128)(2,1)} collective-permute-done((bf16[4,128,512]{2,1,0:T(8,128)(2,1)}, bf16[4,128,512]{2,1,0:T(8,128)(2,1)}, u32[]{:S(2)}, u32[]{:S(2)}) %collective-permute-start.15) | collective-permute-done | bytes 524320 | tf_op jit(solution)/shard_map/ppermute | solution.py:27
  214.3 3.1 %shard_map.143 = bf16[8,128,512]{2,1,0:T(8,128)(2,1)} custom-call(s32[4,4]{1,0:T(4,128)S(1)} %pad_add_fusion.cols, f32[8,128,512]{2,1,0:T(8,128)S(1)} %get-tuple-element.40.base, bf16[4,128,512]{2,1,0:T(8,128)(2,1)} %collective-permute-done.12.r0, bf16[4,128,512]{2,1,0:T(8,128)(2,1)} %collective-permute-done.13.r1, ...), custom_call_target="tpu_custom_call" | custom-call | bytes 5242880 | tf_op jit(solution)/shard_map/pallas_call | solution.py:295
  218.0 3.4 %shard_map.146 = (f32[512,1024]{1,0:T(8,128)}, f32[512,1024]{1,0:T(8,128)}) custom-call(s32[2]{0:T(128)S(1)} %pad_add_fusion.1.place, bf16[512,512]{1,0:T(8,128)(2,1)S(1)} %bitcast.15, bf16[512,512]{1,0:T(8,128)(2,1)} %collective-permute-done.18.own_swap, bf16[512,512]{1,0:T(8,128)(2,1)S(1)} %bitcast.17, bf16[512,512]{1,0:T(8,128)(2,1)S(1)} %collective-permute-done.20.far_swap), custom_call_target="tpu_custom_call" | custom-call | bytes 6291456 | tf_op jit(solution)/shard_map/pallas_call | solution.py:303
  (110 shorter events, 35.5 us)
Async XLA Ops:
  1.5 8.9 %collective-permute-start = (s32[1,4]{1,0:T(1,128)S(1)}, s32[1,4]{1,0:T(1,128)S(1)}, u32[]{:S(2)}, u32[]{:S(2)}) collective-permute-start(s32[1,4]{1,0:T(1,128)S(1)} %get-tuple-element.55), channel_id=1, source_target_pairs={{0,124},{2,126},{4,0},{6,2},{8,4},{10,6},{12,8},{14,10},{16,12},{1... | collective-permute-start | bytes 56 | tf_op jit(solution)/shard_map/ppermute | solution.py:27
  9.5 6.6 %collective-permute-start.3 = (s32[1,4]{1,0:T(1,128)S(1)}, s32[1,4]{1,0:T(1,128)S(1)}, u32[]{:S(2)}, u32[]{:S(2)}) collective-permute-start(s32[1,4]{1,0:T(1,128)S(1)} %get-tuple-element.56), channel_id=1, source_target_pairs={{0,4},{2,6},{4,8},{6,10},{8,12},{10,14},{12,16},{14,18},{16,20},{1... | collective-permute-start | bytes 56 | tf_op jit(solution)/shard_map/ppermute | solution.py:27
  9.5 6.6 %collective-permute-start.2 = (s32[1,4]{1,0:T(1,128)S(1)}, s32[1,4]{1,0:T(1,128)S(1)}, u32[]{:S(2)}, u32[]{:S(2)}) collective-permute-start(s32[1,4]{1,0:T(1,128)S(1)} %get-tuple-element.57), channel_id=1, source_target_pairs={{0,2},{2,4},{4,6},{6,8},{8,10},{10,12},{12,14},{14,16},{16,18},{18... | collective-permute-start | bytes 56 | tf_op jit(solution)/shard_map/ppermute | solution.py:27
  9.5 6.6 %collective-permute-start.1 = (s32[1,4]{1,0:T(1,128)S(1)}, s32[1,4]{1,0:T(1,128)S(1)}, u32[]{:S(2)}, u32[]{:S(2)}) collective-permute-start(s32[1,4]{1,0:T(1,128)S(1)} %get-tuple-element.58), channel_id=1, source_target_pairs={{0,126},{2,0},{4,2},{6,4},{8,6},{10,8},{12,10},{14,12},{16,14},{18... | collective-permute-start | bytes 56 | tf_op jit(solution)/shard_map/ppermute | solution.py:27
  18.8 18.7 %collective-permute-start.4 = (bf16[4,128,512]{2,1,0:T(8,128)(2,1)}, bf16[4,128,512]{2,1,0:T(8,128)(2,1)S(1)}, u32[]{:S(2)}, u32[]{:S(2)}) collective-permute-start(bf16[4,128,512]{2,1,0:T(8,128)(2,1)} %get-tuple-element.29), channel_id=1, source_target_pairs={{0,4},{2,6},{4,8},{6,10},{8,12},{10,14},{12,16},{14,18},{16,20},{1... | collective-permute-start | bytes 1572872 | tf_op jit(solution)/shard_map/ppermute | solution.py:27
  18.8 18.7 %collective-permute-start.5 = (bf16[4,128,512]{2,1,0:T(8,128)(2,1)S(1)}, bf16[4,128,512]{2,1,0:T(8,128)(2,1)S(1)}, u32[]{:S(2)}, u32[]{:S(2)}) collective-permute-start(bf16[4,128,512]{2,1,0:T(8,128)(2,1)S(1)} %get-tuple-element.30), channel_id=1, source_target_pairs={{0,2},{2,4},{4,6},{6,8},{8,10},{10,12},{12,14},{14,16},{16,18},{18... | collective-permute-start | bytes 1572872 | tf_op jit(solution)/shard_map/ppermute | solution.py:27
  18.8 18.7 %collective-permute-start.6 = (bf16[4,128,512]{2,1,0:T(8,128)(2,1)S(1)}, bf16[4,128,512]{2,1,0:T(8,128)(2,1)S(1)}, u32[]{:S(2)}, u32[]{:S(2)}) collective-permute-start(bf16[4,128,512]{2,1,0:T(8,128)(2,1)S(1)} %get-tuple-element.31), channel_id=1, source_target_pairs={{0,126},{2,0},{4,2},{6,4},{8,6},{10,8},{12,10},{14,12},{16,14},{18... | collective-permute-start | bytes 1572872 | tf_op jit(solution)/shard_map/ppermute | solution.py:27
  20.9 17.5 %collective-permute-start.7 = (bf16[4,128,512]{2,1,0:T(8,128)(2,1)S(1)}, bf16[4,128,512]{2,1,0:T(8,128)(2,1)}, u32[]{:S(2)}, u32[]{:S(2)}) collective-permute-start(bf16[4,128,512]{2,1,0:T(8,128)(2,1)S(1)} %get-tuple-element.32), channel_id=1, source_target_pairs={{0,124},{2,126},{4,0},{6,2},{8,4},{10,6},{12,8},{14,10},{16,12},{1... | collective-permute-start | bytes 1572872 | tf_op jit(solution)/shard_map/ppermute | solution.py:27
  26.9 28.7 %copy-start.11 = (f32[512]{0:T(512)S(1)}, f32[512]{0:T(512)}, u32[]{:S(2)}) copy-start(f32[512]{0:T(512)} %param.18) | copy-start | bytes 6148
  52.5 9.6 %collective-permute-start.9 = (bf16[1024,256]{1,0:T(8,128)(2,1)S(1)}, bf16[1024,256]{1,0:T(8,128)(2,1)S(1)}, u32[]{:S(2)}, u32[]{:S(2)}) collective-permute-start(bf16[1024,256]{1,0:T(8,128)(2,1)S(1)} %get-tuple-element.35), channel_id=1, source_target_pairs={{0,1},{1,0},{2,3},{3,2},{4,5},{5,4},{6,7},{7,6},{8,9},{9,8},{10,11... | collective-permute-start | bytes 1572872 | tf_op jit(solution)/shard_map/ppermute | solution.py:31
  55.0 17.8 %collective-permute-start.8 = (bf16[1024,256]{1,0:T(8,128)(2,1)S(1)}, bf16[1024,256]{1,0:T(8,128)(2,1)S(1)}, u32[]{:S(2)}, u32[]{:S(2)}) collective-permute-start(bf16[1024,256]{1,0:T(8,128)(2,1)S(1)} %get-tuple-element.34), channel_id=1, source_target_pairs={{0,1},{1,0},{2,3},{3,2},{4,5},{5,4},{6,7},{7,6},{8,9},{9,8},{10,11... | collective-permute-start | bytes 1572872 | tf_op jit(solution)/shard_map/ppermute | solution.py:31
  64.0 20.6 %copy-start.14 = (bf16[1024,256]{1,0:T(8,128)(2,1)}, bf16[1024,256]{1,0:T(8,128)(2,1)S(1)}, u32[]{:S(2)}) copy-start(bf16[1024,256]{1,0:T(8,128)(2,1)S(1)} %get-tuple-element.38.own0.d0) | copy-start | bytes 1572868
  74.7 21.9 %copy-start.16 = (bf16[1024,256]{1,0:T(8,128)(2,1)}, bf16[1024,256]{1,0:T(8,128)(2,1)S(1)}, u32[]{:S(2)}) copy-start(bf16[1024,256]{1,0:T(8,128)(2,1)S(1)} %get-tuple-element.39.own1.d1) | copy-start | bytes 1572868
  74.7 13.1 %collective-permute-start.17 = (f32[1,512]{1,0:T(1,128)S(1)}, f32[1,512]{1,0:T(1,128)S(1)}, u32[]{:S(2)}, u32[]{:S(2)}) collective-permute-start(f32[1,512]{1,0:T(1,128)S(1)} %bitcast.24), channel_id=1, source_target_pairs={{0,2},{2,0},{1,3},{3,1},{4,6},{6,4},{5,7},{7,5},{8,10},{10,8},{9,1... | collective-permute-start | bytes 6152 | tf_op jit(solution)/shard_map/ppermute | solution.py:31
  81.6 15.0 %collective-permute-start.11 = (bf16[1024,256]{1,0:T(8,128)(2,1)S(1)}, bf16[1024,256]{1,0:T(8,128)(2,1)S(1)}, u32[]{:S(2)}, u32[]{:S(2)}) collective-permute-start(bf16[1024,256]{1,0:T(8,128)(2,1)S(1)} %get-tuple-element.39.own1.d1), channel_id=1, source_target_pairs={{0,1},{1,0},{2,3},{3,2},{4,5},{5,4},{6,7},{7,6},{8,9},{9,8},{10,11... | collective-permute-start | bytes 1572872 | tf_op jit(solution)/shard_map/ppermute | solution.py:31
  84.0 23.8 %collective-permute-start.10 = (bf16[1024,256]{1,0:T(8,128)(2,1)S(1)}, bf16[1024,256]{1,0:T(8,128)(2,1)S(1)}, u32[]{:S(2)}, u32[]{:S(2)}) collective-permute-start(bf16[1024,256]{1,0:T(8,128)(2,1)S(1)} %get-tuple-element.38.own0.d0), channel_id=1, source_target_pairs={{0,1},{1,0},{2,3},{3,2},{4,5},{5,4},{6,7},{7,6},{8,9},{9,8},{10,11... | collective-permute-start | bytes 1572872 | tf_op jit(solution)/shard_map/ppermute | solution.py:31
  87.1 24.2 %collective-permute-start.16 = (bf16[512,512]{1,0:T(8,128)(2,1)S(1)}, bf16[512,512]{1,0:T(8,128)(2,1)S(1)}, u32[]{:S(2)}, u32[]{:S(2)}) collective-permute-start(bf16[512,512]{1,0:T(8,128)(2,1)S(1)} %get-tuple-element.46), channel_id=1, source_target_pairs={{0,2},{2,0},{1,3},{3,1},{4,6},{6,4},{5,7},{7,5},{8,10},{10,8},{9,1... | collective-permute-start | bytes 1572872 | tf_op jit(solution)/shard_map/ppermute | solution.py:31
  110.4 9.6 %collective-permute-start.19 = (bf16[512,512]{1,0:T(8,128)(2,1)S(1)}, bf16[512,512]{1,0:T(8,128)(2,1)S(1)}, u32[]{:S(2)}, u32[]{:S(2)}) collective-permute-start(bf16[512,512]{1,0:T(8,128)(2,1)S(1)} %get-tuple-element.50), channel_id=1, source_target_pairs={{0,2},{2,0},{1,3},{3,1},{4,6},{6,4},{5,7},{7,5},{8,10},{10,8},{9,1... | collective-permute-start | bytes 1572872 | tf_op jit(solution)/shard_map/ppermute | solution.py:31
  112.5 20.6 %all-to-all-start = ((bf16[32,24,512]{2,1,0:T(8,128)(2,1)}), bf16[32,24,512]{2,1,0:T(8,128)(2,1)S(1)}, u32[]{:S(2)}, u32[]{:S(2)}) async-start(bf16[32,24,512]{2,1,0:T(8,128)(2,1)} %pad_maximum_fusion), calls=%async_computation | async-start | bytes 1572864 | tf_op jit(solution)/shard_map/all_to_all | solution.py:178
  121.0 32.9 %copy-start.10 = (s32[1,20]{1,0:T(1,128)S(1)}, s32[1,20]{1,0:T(1,128)}, u32[]{:S(2)}) copy-start(s32[1,20]{1,0:T(1,128)} %col.3) | copy-start | bytes 244
  121.0 32.9 %copy-start.26 = (s32[1,20]{1,0:T(1,128)S(1)}, s32[1,20]{1,0:T(1,128)}, u32[]{:S(2)}) copy-start(s32[1,20]{1,0:T(1,128)} %row.3) | copy-start | bytes 244
  121.0 32.9 %copy-start.28 = (s32[1,20]{1,0:T(1,128)S(1)}, s32[1,20]{1,0:T(1,128)}, u32[]{:S(2)}) copy-start(s32[1,20]{1,0:T(1,128)} %tile.3) | copy-start | bytes 244
  121.0 32.9 %copy-start.30 = (s32[1,5]{1,0:T(1,128)S(1)}, s32[1,5]{1,0:T(1,128)}, u32[]{:S(2)}) copy-start(s32[1,5]{1,0:T(1,128)} %count.3) | copy-start | bytes 64
  133.0 15.3 %all-to-all-start.2 = ((bf16[32,16,512]{2,1,0:T(8,128)(2,1)}), bf16[32,16,512]{2,1,0:T(8,128)(2,1)S(1)}, u32[]{:S(2)}, u32[]{:S(2)}) async-start(bf16[32,16,512]{2,1,0:T(8,128)(2,1)} %bitcast.9), calls=%async_computation.2 | async-start | bytes 1048576 | tf_op jit(solution)/shard_map/all_to_all | solution.py:178
  149.2 30.7 %all-to-all-start.1 = ((bf16[32,16,512]{2,1,0:T(8,128)(2,1)}), bf16[32,16,512]{2,1,0:T(8,128)(2,1)S(1)}, u32[]{:S(2)}, u32[]{:S(2)}) async-start(bf16[32,16,512]{2,1,0:T(8,128)(2,1)} %broadcast_in_dim.13), calls=%async_computation.1 | async-start | bytes 1048576 | tf_op jit(solution)/shard_map/all_to_all | solution.py:185
  174.8 17.8 %collective-permute-start.12 = (bf16[4,128,512]{2,1,0:T(8,128)(2,1)}, bf16[4,128,512]{2,1,0:T(8,128)(2,1)}, u32[]{:S(2)}, u32[]{:S(2)}) collective-permute-start(bf16[4,128,512]{2,1,0:T(8,128)(2,1)} %get-tuple-element.41), channel_id=1, source_target_pairs={{0,124},{2,126},{4,0},{6,2},{8,4},{10,6},{12,8},{14,10},{16,12},{1... | collective-permute-start | bytes 1572872 | tf_op jit(solution)/shard_map/ppermute | solution.py:27
  180.7 18.1 %all-to-all-start.3 = ((bf16[32,16,512]{2,1,0:T(8,128)(2,1)}), bf16[32,16,512]{2,1,0:T(8,128)(2,1)S(1)}, u32[]{:S(2)}, u32[]{:S(2)}) async-start(bf16[32,16,512]{2,1,0:T(8,128)(2,1)} %broadcast_in_dim.28), calls=%async_computation.3 | async-start | bytes 1048576 | tf_op jit(solution)/shard_map/all_to_all | solution.py:185
  184.6 15.7 %collective-permute-start.13 = (bf16[4,128,512]{2,1,0:T(8,128)(2,1)}, bf16[4,128,512]{2,1,0:T(8,128)(2,1)}, u32[]{:S(2)}, u32[]{:S(2)}) collective-permute-start(bf16[4,128,512]{2,1,0:T(8,128)(2,1)} %copy-done.24), channel_id=1, source_target_pairs={{0,126},{2,0},{4,2},{6,4},{8,6},{10,8},{12,10},{14,12},{16,14},{18... | collective-permute-start | bytes 1572872 | tf_op jit(solution)/shard_map/ppermute | solution.py:27
  186.6 13.9 %collective-permute-start.14 = (bf16[4,128,512]{2,1,0:T(8,128)(2,1)}, bf16[4,128,512]{2,1,0:T(8,128)(2,1)}, u32[]{:S(2)}, u32[]{:S(2)}) collective-permute-start(bf16[4,128,512]{2,1,0:T(8,128)(2,1)} %copy-done.23), channel_id=1, source_target_pairs={{0,2},{2,4},{4,6},{6,8},{8,10},{10,12},{12,14},{14,16},{16,18},{18... | collective-permute-start | bytes 1572872 | tf_op jit(solution)/shard_map/ppermute | solution.py:27
  188.1 26.2 %collective-permute-start.15 = (bf16[4,128,512]{2,1,0:T(8,128)(2,1)}, bf16[4,128,512]{2,1,0:T(8,128)(2,1)}, u32[]{:S(2)}, u32[]{:S(2)}) collective-permute-start(bf16[4,128,512]{2,1,0:T(8,128)(2,1)} %copy-done.22), channel_id=1, source_target_pairs={{0,4},{2,6},{4,8},{6,10},{8,12},{10,14},{12,16},{14,18},{16,20},{1... | collective-permute-start | bytes 1572872 | tf_op jit(solution)/shard_map/ppermute | solution.py:27
  189.3 28.7 %collective-permute-start.18 = (bf16[512,512]{1,0:T(8,128)(2,1)S(1)}, bf16[512,512]{1,0:T(8,128)(2,1)}, u32[]{:S(2)}, u32[]{:S(2)}) collective-permute-start(bf16[512,512]{1,0:T(8,128)(2,1)S(1)} %bitcast.14), channel_id=1, source_target_pairs={{0,2},{2,0},{1,3},{3,1},{4,6},{6,4},{5,7},{7,5},{8,10},{10,8},{9,1... | collective-permute-start | bytes 1572872 | tf_op jit(solution)/shard_map/ppermute | solution.py:31
  198.8 19.2 %collective-permute-start.20 = (bf16[512,512]{1,0:T(8,128)(2,1)S(1)}, bf16[512,512]{1,0:T(8,128)(2,1)S(1)}, u32[]{:S(2)}, u32[]{:S(2)}) collective-permute-start(bf16[512,512]{1,0:T(8,128)(2,1)S(1)} %bitcast.16), channel_id=1, source_target_pairs={{0,2},{2,0},{1,3},{3,1},{4,6},{6,4},{5,7},{7,5},{8,10},{10,8},{9,1... | collective-permute-start | bytes 1572872 | tf_op jit(solution)/shard_map/ppermute | solution.py:31
  (24 other events, 67.6 us)

commit v2 on v0

v2 whole, which is shorter than its diff:
```python
import jax
import jax.numpy as jnp
from jax import lax
from jax.experimental import pallas as pl
from jax.experimental.pallas import tpu as pltpu
from jax.sharding import Mesh, PartitionSpec as P

REACH = 2
PAIR_MAX = 4
BLOCK = 128
NODE = ("xl", "z", "y", "c")
CHIPS = ("xl", "z", "y")
PLANE = ("z", "y")
VMEM = pl.BlockSpec(memory_space=pltpu.VMEM)
SMEM = pl.BlockSpec(memory_space=pltpu.SMEM)
HBM = pl.BlockSpec(memory_space=pltpu.HBM)
ANY = pl.BlockSpec(memory_space=pl.ANY)
BF = jnp.bfloat16
F32 = jnp.float32
MIB = 1 << 20
ROLES = ((4, 0), (0, 4), (1, 3), (3, 1))
TALL = 256
COST = pl.CostEstimate(flops=10**4, bytes_accessed=10**4, transcendentals=0)


def dot(a, b, dims=((1,), (0,))):
    return lax.dot_general(a, b, (dims, ((), ())), preferred_element_type=F32)


def mirror(block, distance):
    count = lax.axis_size(NODE)
    return lax.ppermute(
        block, NODE, [(i, (i + (distance if i % 2 == 0 else -distance)) % count) for i in range(count)]
    )


def swap(block, axis):
    return lax.ppermute(block, axis, [(0, 1), (1, 0)])


def send_roles(blocks):
    ahead, behind, outer, sibling = blocks
    return [mirror(ahead, REACH), mirror(behind, -REACH), mirror(outer, -1), swap(sibling, "c")]


def shape(dims, kind):
    return jax.ShapeDtypeStruct(dims, kind)


def params(vmem):
    return pltpu.CompilerParams(vmem_limit_bytes=vmem * MIB)


def live(count, k, s):
    return s < count[0, k]


def pass_kernel(array, *rest):
    pass


def mark_kernel(*refs):
    refs[-1][...] = jnp.zeros_like(refs[-1])


def turn_kernel(x, w_neigh, w_self, tiles, x_t, neigh_t, self_t, tiles_t, token):
    x_t[...] = x[...].T
    neigh_t[...] = w_neigh[...].T
    self_t[...] = w_self[...].T
    for j in range(tiles.shape[0]):
        tiles_t[j] = tiles[j].T
    token[...] = jnp.zeros_like(token)


def early_kernel(row, col, tile, count, x, near, tiles, w_self, bias, after, acc, ahead, own, token):
    token[...] = jnp.zeros_like(token)
    core = lax.axis_index("c")
    acc[...] = jnp.zeros_like(acc)
    for k, source in ((REACH, x), (jnp.where(core == 0, 3, 1), near)):
        for s in range(PAIR_MAX):
            j = k * PAIR_MAX + s

            @pl.when(live(count, k, s))
            def _():
                acc[row[0, j]] += dot(tiles[tile[0, j]], source[col[0, j]])

    width = own.shape[1]
    side = lax.axis_index("f")
    rows = TALL
    for r in range(own.shape[0] // rows):
        at = slice(r * rows, (r + 1) * rows)
        mine = x[r * rows // BLOCK : (r + 1) * rows // BLOCK].reshape(rows, width)
        ahead[at, :] = dot(mine, w_self[:, pl.ds(pl.multiple_of((1 - side) * width, 128), width)])
        own[at, :] = dot(mine, w_self[:, pl.ds(pl.multiple_of(side * width, 128), width)]) + bias[...]


def aggregate_kernel(row, col, tile, count, ahead, passing, passed, acc0, part, tiles, w_neigh, agg, send0, send1, acc):
    core = lax.axis_index("c")
    acc[...] = acc0[...]
    for (k0, k1), source in zip(((0, 4), (4, 0), (1, 3)), (ahead, passing, passed)):
        k = jnp.where(core == 0, k0, k1)
        for s in range(PAIR_MAX):
            j = k * PAIR_MAX + s

            @pl.when(live(count, k, s))
            def _():
                acc[row[0, j]] += dot(tiles[tile[0, j]], source[col[0, j]])

    rows = acc.shape[0] * BLOCK // 2
    half = send0.shape[1]
    agg[...] = acc[...].astype(BF).reshape(agg.shape)
    other = (1 - lax.axis_index("f")) * (2 * half)
    for c, send in enumerate((send0, send1)):
        cols = pl.ds(pl.multiple_of(other + c * half, 128), half)
        span = slice(c * half, (c + 1) * half)
        for r in range(2):
            at = slice(r * rows, (r + 1) * rows)
            send[at, :] = (dot(agg[at, :], w_neigh[:, cols]) + part[at, span]).astype(BF)


def own_kernel(agg, own0, w_neigh, out, agg_t):
    width = out.shape[1]
    cols = pl.ds(pl.multiple_of(lax.axis_index("f") * width, 128), width)
    out[...] = dot(agg[...], w_neigh[:, cols]) + own0[...]
    agg_t[...] = agg[...].T


def act_kernel(own, recv, cot, *rest):
    hidden, delta, sums = rest[-3:]
    pre = own[...] + recv[...].astype(F32)
    sigma = jax.nn.sigmoid(pre)
    hidden[...] = (pre * sigma).astype(BF)
    d = (cot[...].astype(F32) * sigma * (1.0 + pre * (1.0 - sigma))).astype(BF)
    delta[...] = d

    @pl.when(pl.program_id(0) == 0)
    def _():
        sums[...] = jnp.zeros_like(sums)

    sums[...] += jnp.sum(d.astype(F32).reshape(-1, 8, d.shape[1]), axis=0)


def weight_kernel(agg_t, x_t, d, *rest):
    send, keep = rest[-2:]
    first = lax.axis_index("c") == 0
    neigh = dot(agg_t[...], d[...])
    own = dot(x_t[...], d[...])
    send[...] = jnp.where(first, own, neigh).astype(BF)
    keep[...] = jnp.where(first, neigh, own)


def weight_total_kernel(agg_t, x_t, d, moved, c0, c1, c2, c3, send, keep, total, token):
    token[...] = jnp.zeros_like(token)
    weight_kernel(agg_t, x_t, d, send, keep)
    total[...] = jnp.sum(moved[...].astype(F32), axis=0)


def bias_rows(sums):
    total = jnp.sum(sums, axis=0, keepdims=True)
    high = total.astype(BF)
    low = (total - high.astype(F32)).astype(BF)
    row = lax.broadcasted_iota(jnp.int32, (8, total.shape[1]), 0)
    return jnp.where(row == 0, high.astype(F32), jnp.where(row == 1, low.astype(F32), 0.0)).astype(BF)


def join_kernel(keep, got, *rest):
    out = rest[-1]
    pieces, tall, width = out.shape
    piece = keep.shape[0] // pieces
    both = (keep[...] + got[...].astype(F32)).astype(BF)
    out[:, :piece, :] = both.reshape(pieces, piece, width)
    if tall > piece:
        s0, s1, g0, g1 = rest[:-1]
        half = s0.shape[1]
        for c, (s, g) in enumerate(((s0, g0), (s1, g1))):
            rows = bias_rows(jnp.concatenate([s[...], g[...]], axis=0))
            out[:, piece:, c * half : (c + 1) * half] = jnp.broadcast_to(rows[None], (pieces, 8, half))


def spread_kernel(scale, a, b, moved, after, also, out, bias):
    piece = out.shape[1] // 2
    xl = lax.axis_index("xl")
    rows = pl.ds(pl.multiple_of(xl * piece, piece), piece)
    mine = (a[rows, :] + b[rows, :]) * scale
    far = jnp.sum(moved[...].astype(F32), axis=0) * scale
    out[:, :piece, :] = jnp.broadcast_to(mine.astype(BF)[None], (out.shape[0], *mine.shape))
    out[:, piece:, :] = jnp.broadcast_to(far.astype(BF)[None], (out.shape[0], *far.shape))
    bias[...] = jnp.sum((a[2 * piece :, :] + b[2 * piece :, :]) * scale, axis=0, keepdims=True)


def wide(own, far, turned, r, rows):
    side = lax.axis_index("f")
    width = own.shape[1]
    at = slice(r * rows, (r + 1) * rows)
    mine = turned[pl.ds(pl.multiple_of(side * width, 128), width), :]
    other = turned[pl.ds(pl.multiple_of((1 - side) * width, 128), width), :]
    return dot(own[at, :], mine) + dot(far[at, :], other)


def outward_kernel(
    row, tile, count, own, far, tiles, turned, after,
    o0, o1, o2, o3, dagg, token, ds, df, ts, wn, dg, built, sems, sent,
):
    token[...] = jnp.zeros_like(token)
    pieces = [(turned, wn), (own, ds), (far, df), (tiles, ts), (dg, dagg)]
    copies = [pltpu.make_async_copy(a, b, sems.at[i]) for i, (a, b) in enumerate(pieces)]
    for c in copies[:4]:
        c.start()
    for c in copies[:3]:
        c.wait()
    blocks = dg.shape[0]
    for r in range(2):
        total = wide(ds, df, wn, r, blocks * BLOCK // 2)
        dg[r * blocks // 2 : (r + 1) * blocks // 2] = total.astype(BF).reshape(blocks // 2, BLOCK, -1)
    copies[4].start()
    copies[3].wait()
    core = lax.axis_index("c")
    leaving = []
    for i, (out, (k0, k1)) in enumerate(zip((o0, o1, o2, o3), ROLES)):
        k = jnp.where(core == 0, k0, k1)
        for s in range(PAIR_MAX):
            j = k * PAIR_MAX + s

            @pl.when(live(count, k, s))
            def _():
                built[i, s] = dot(ts[tile[0, j]], dg[row[0, j]]).astype(BF)

            @pl.when(jnp.logical_not(live(count, k, s)))
            def _():
                built[i, s] = jnp.zeros(built.shape[2:], BF)

        leaving.append(pltpu.make_async_copy(built.at[i], out, sent.at[i]))
        leaving[-1].start()
    for c in (*leaving, copies[4]):
        c.wait()


def base_kernel(row, col, tile, count, own, far, dagg, tiles, turned, base, token, ds, df, ts, ws, dg, sems):
    token[...] = jnp.zeros_like(token)
    pieces = [(turned, ws), (own, ds), (far, df), (tiles, ts), (dagg, dg)]
    copies = [pltpu.make_async_copy(a, b, sems.at[i]) for i, (a, b) in enumerate(pieces)]
    for c in copies:
        c.start()
    for c in copies[:3]:
        c.wait()
    blocks = base.shape[0]
    for r in range(2):
        total = wide(ds, df, ws, r, blocks * BLOCK // 2)
        base[r * blocks // 2 : (r + 1) * blocks // 2] = total.reshape(blocks // 2, BLOCK, -1)
    for c in copies[3:]:
        c.wait()
    for s in range(PAIR_MAX):
        j = REACH * PAIR_MAX + s

        @pl.when(live(count, REACH, s))
        def _():
            base[col[0, j]] += dot(ts[tile[0, j]], dg[row[0, j]])


def place_kernel(c0, c1, c2, c3, base, r0, r1, r2, r3, out, token, acc):
    token[...] = jnp.zeros_like(token)
    core = lax.axis_index("c")
    acc[...] = base[...]
    for i, (cols, r, ks) in enumerate(zip((c0, c1, c2, c3), (r0, r1, r2, r3), ROLES)):
        sender = core if i < 2 else 1 - core
        k = jnp.where(sender == 0, ks[0], ks[1])
        for s in range(PAIR_MAX):
            acc[cols[0, k * PAIR_MAX + s]] += r[s].astype(F32)
    out[...] = acc[...].astype(BF)


def assemble_kernel(own_mine, own_swap, far_mine, far_swap, neigh, self_):
    first = lax.axis_index("c") == 0
    side = lax.axis_index("f")
    halves, planes, both, width = own_mine.shape
    piece = both // 2
    own_cols = pl.ds(pl.multiple_of(side * width, 128), width)
    far_cols = pl.ds(pl.multiple_of((1 - side) * width, 128), width)
    for out, a, b in ((neigh, own_mine, own_swap), (self_, own_swap, own_mine)):
        for p in range(planes):
            for h in range(halves):
                n = p * halves + h
                at = slice(n * piece, (n + 1) * piece)
                out[at, own_cols] = jnp.where(first, a[h, p, :piece], b[h, p, :piece]).astype(F32)
    for out, a, b in ((neigh, far_mine, far_swap), (self_, far_swap, far_mine)):
        for n in range(planes * halves):
            at = slice(n * piece, (n + 1) * piece)
            out[at, far_cols] = jnp.where(first, a[n, piece:], b[n, piece:]).astype(F32)


def run(kernel, outs, in_specs, out_specs=None, scratch=(), vmem=16, **more):
    many = isinstance(outs, list)
    return pl.pallas_call(
        kernel,
        out_shape=outs,
        in_specs=in_specs,
        out_specs=out_specs or ([VMEM] * len(outs) if many else VMEM),
        scratch_shapes=list(scratch),
        compiler_params=params(vmem),
        cost_estimate=COST,
        **more,
    )


def on_device(node_feats, edge_tiles, slot_row, slot_col, slot_tile, slot_count, w_self, w_neigh, bias, cotangent):
    nodes, width = node_feats.shape
    blocks = nodes // BLOCK
    half = width // 2
    scale = float(nodes * lax.axis_size(NODE)) ** (-0.5)
    x = node_feats.reshape(blocks, BLOCK, width)

    ints = (slot_row, slot_col, slot_tile, slot_count)
    passing = mirror(x, -REACH)
    ahead = mirror(x, REACH)
    near = swap(x, "c")
    mark = shape((8, 128), F32)
    x_t, neigh_t, self_t, tiles_t, token = run(
        turn_kernel,
        [shape((width, nodes), BF)] + [shape((2 * width, width), BF)] * 2 + [shape(edge_tiles.shape, BF), mark],
        [VMEM] * 4,
        vmem=20,
    )(node_feats, w_neigh, w_self, edge_tiles)
    acc0, part, own0, token = run(
        early_kernel,
        [shape((blocks, BLOCK, width), F32)] + [shape((nodes, width), F32)] * 2 + [mark],
        [SMEM] * 4 + [VMEM] * 5 + [ANY],
        vmem=20,
    )(*ints, x, near, edge_tiles, w_self, bias.reshape(1, width), token)

    def after(array, *others):
        return run(
            pass_kernel,
            shape(array.shape, array.dtype),
            [ANY] * (1 + len(others)),
            ANY,
            input_output_aliases={0: 0},
            vmem=2,
        )(array, *others)

    passing = after(passing, token)
    passed = swap(passing, "c")
    aggregate, send0, send1 = run(
        aggregate_kernel,
        [shape((nodes, width), BF)] + [shape((nodes, half), BF)] * 2,
        [SMEM] * 4 + [VMEM] * 7,
        scratch=[pltpu.VMEM((blocks, BLOCK, width), F32)],
        vmem=20,
    )(*ints, ahead, passing, passed, acc0, part, edge_tiles, w_neigh)
    recv = [swap(send0, "f"), swap(send1, "f")]

    tall = pl.BlockSpec((TALL, width), lambda i: (i, 0))
    own, agg_t = run(
        own_kernel,
        [shape((nodes, width), F32), shape((width, nodes), BF)],
        [tall, tall, pl.BlockSpec(w_neigh.shape, lambda i: (0, 0))],
        [tall, pl.BlockSpec((width, TALL), lambda i: (0, i))],
        grid=(nodes // TALL,),
    )(aggregate, own0, w_neigh)

    hidden, delta = None, None
    sums = []
    for c in range(2):
        column = pl.BlockSpec((TALL, half), lambda i, c=c: (i, c))
        alone = pl.BlockSpec((TALL, half), lambda i: (i, 0))
        extra = [hidden, delta] if c else []
        hidden, delta, total = run(
            act_kernel,
            [shape((nodes, width), BF), shape((nodes, width), BF), shape((8, half), F32)],
            [column, alone, column] + [ANY] * len(extra),
            [column, column, pl.BlockSpec((8, half), lambda i: (0, 0))],
            grid=(nodes // TALL,),
            input_output_aliases={3: 0, 4: 1} if c else {},
        )(own, recv[c], cotangent, *extra)
        sums.append(total)
    other = swap(delta, "f")

    plane, chips = lax.axis_size(PLANE), lax.axis_size(CHIPS)
    piece = width // plane
    strip = pl.BlockSpec((width // 2, nodes), lambda i: (i, 0))
    full = pl.BlockSpec((nodes, width), lambda i: (0, 0))
    out = pl.BlockSpec((width // 2, width), lambda i: (i, 0))
    pair = [shape((width, width), BF), shape((width, width), F32)]
    send, keep = run(weight_kernel, pair, [strip, strip, full], [out, out], grid=(2,))(agg_t, x_t, delta)
    got, *got_sums = [swap(v, "c") for v in (send, *sums)]
    steps = 4
    part = pl.BlockSpec((width // steps, width), lambda i: (i, 0))
    small = pl.BlockSpec((8, half), lambda i: (0, 0))
    parts = run(
        join_kernel,
        shape((plane, piece + 8, width), BF),
        [part, part] + [small] * 4,
        pl.BlockSpec((plane // steps, piece + 8, width), lambda i: (i, 0, 0)),
        grid=(steps,),
    )(keep, got, *sums, *got_sums)
    parts = lax.all_to_all(parts, PLANE, 0, 0)

    columns = send_roles([slot_col] * 4)
    moved = pl.BlockSpec((plane, piece + 8, width // 2), lambda i: (0, 0, i))
    summed = pl.BlockSpec((piece + 8, width // 2), lambda i: (0, i))
    send, keep, own_total, token = run(
        weight_total_kernel,
        pair + [shape((piece + 8, width), F32), mark],
        [strip, strip, full, moved] + [SMEM] * 4,
        [out, out, summed, pl.BlockSpec(mark.shape, lambda i: (0, 0))],
        grid=(2,),
        vmem=50,
    )(agg_t, x_t, other, parts, *columns)
    got = swap(send, "c")
    own_got = swap(own_total, "xl")
    *outward, dagg, token = run(
        outward_kernel,
        [shape((PAIR_MAX, BLOCK, width), BF)] * 4 + [shape((blocks, BLOCK, width), BF), mark],
        [SMEM] * 3 + [ANY] * 5,
        [ANY] * 5 + [VMEM],
        [
            pltpu.VMEM((nodes, width), BF),
            pltpu.VMEM((nodes, width), BF),
            pltpu.VMEM(edge_tiles.shape, BF),
            pltpu.VMEM(neigh_t.shape, BF),
            pltpu.VMEM((blocks, BLOCK, width), BF),
            pltpu.VMEM((4, PAIR_MAX, BLOCK, width), BF),
            pltpu.SemaphoreType.DMA((5,)),
            pltpu.SemaphoreType.DMA((4,)),
        ],
        vmem=56,
    )(slot_row, slot_tile, slot_count, delta, other, tiles_t, neigh_t, token)
    returned = send_roles(outward)
    parts = run(
        join_kernel,
        shape((chips, width // chips, width), BF),
        [part, part, ANY],
        pl.BlockSpec((chips // steps, width // chips, width), lambda i: (i, 0, 0)),
        grid=(steps,),
    )(keep, got, token)
    far_parts = lax.all_to_all(parts, CHIPS, 0, 0)

    base, token = run(
        base_kernel,
        [shape((blocks, BLOCK, width), F32), mark],
        [SMEM] * 4 + [ANY] * 5,
        [VMEM, VMEM],
        [
            pltpu.VMEM((nodes, width), BF),
            pltpu.VMEM((nodes, width), BF),
            pltpu.VMEM(edge_tiles.shape, BF),
            pltpu.VMEM(self_t.shape, BF),
            pltpu.VMEM((blocks, BLOCK, width), BF),
            pltpu.SemaphoreType.DMA((5,)),
        ],
        vmem=56,
    )(*ints, delta, other, dagg, tiles_t, self_t)

    corner = pl.BlockSpec((1, 16, BLOCK), lambda i: (0, 0, 0))
    arrived = run(
        mark_kernel, mark, [corner] * 4, pl.BlockSpec(mark.shape, lambda i: (0, 0)), grid=(1,), vmem=4
    )(*returned)
    spread, grad_bias = run(
        lambda *refs: spread_kernel(scale, *refs),
        [shape((chips, piece, width), BF), shape((1, width), F32)],
        [summed, summed, pl.BlockSpec((chips, width // chips, width // 2), lambda i: (0, 0, i)), ANY, ANY],
        [
            pl.BlockSpec((chips, piece, width // 2), lambda i: (0, 0, i)),
            pl.BlockSpec((1, width // 2), lambda i: (0, i)),
        ],
        grid=(2,),
    )(own_total, own_got, far_parts, token, arrived)
    column = pl.BlockSpec((blocks, BLOCK, BLOCK), lambda i: (0, 0, i))
    narrow = pl.BlockSpec((PAIR_MAX, BLOCK, BLOCK), lambda i: (0, 0, i))
    grad_nodes, token = run(
        place_kernel,
        [shape((blocks, BLOCK, width), BF), mark],
        [SMEM] * 4 + [column] + [narrow] * 4,
        [column, pl.BlockSpec(mark.shape, lambda i: (0, 0))],
        [pltpu.VMEM((blocks, BLOCK, BLOCK), F32)],
        grid=(width // BLOCK,),
    )(*columns, base, *returned)
    grad_nodes = grad_nodes.reshape(nodes, width)

    mine = after(lax.all_to_all(spread, CHIPS, 0, 0), token)
    swapped = swap(mine, "c")

    halves = lax.axis_size("xl")
    block = pl.BlockSpec((halves, plane // steps, piece, width), lambda i: (0, i, 0, 0))
    rows = pl.BlockSpec((width // steps, 2 * width), lambda i: (i, 0))
    by_chip = pl.BlockSpec((chips // steps, piece, width), lambda i: (i, 0, 0))
    view = (halves, plane, piece, width)
    grads = run(
        assemble_kernel,
        [shape((width, 2 * width), F32)] * 2,
        [block, block, by_chip, by_chip],
        [rows, rows],
        grid=(steps,),
    )(mine.reshape(view), swapped.reshape(view), mine, swapped)
    grad_neigh, grad_self = grads
    return hidden, grad_nodes, grad_self, grad_neigh, grad_bias.reshape(width)


def solution(mesh):
    fine = Mesh(mesh.devices.reshape(2, 4, 4, 2, 2), (*NODE, "f"))
    placed = (
        P(NODE, "f"),
        P(NODE, None, None),
        P(NODE, None),
        P(NODE, None),
        P(NODE, None),
        P(NODE, None),
        P("f", None),
        P("f", None),
        P("f"),
        P(NODE, "f"),
    )
    return jax.shard_map(
        on_device,
        mesh=fine,
        in_specs=placed,
        out_specs=(P(NODE, "f"), P(NODE, "f"), P("f", None), P("f", None), P("f")),
        check_vma=False,
    )
```

time: 753 us -> 172 us (0.23)
  waiting for transfers between devices: 486 us -> 55.5 us
  blocking collectives: 148 us -> 0 us
  matrix products: 52.5 us -> 0 us
  starting transfers between devices: 13.3 us -> 62.7 us
  Pallas kernels: 0 us -> 41.2 us
  local copies, waits for them, and re-layouts: 24.7 us -> 10.9 us
  between operations: 14.1 us -> 0.92 us
  other arithmetic: 13.1 us -> 0 us
    psum x1 -> x0, waiting for transfers between devices: 371 us -> none  [on_device(): lax.psum((neigh_part, self_part, bias_part), 'node')]
    psum x1 -> x0, blocking collectives: 148 us -> none  [on_device(): lax.psum((neigh_part, self_part, bias_part), 'node')]
    reduce_scatter x1 -> x0, waiting for transfers between devices: 64 us -> none  [on_device(): lax.psum_scatter(partial_sum, 'feat', scatter_dimension=1, tiled=True)]
    dot_general x26 -> x0, matrix products: 52.5 us -> none  [the longest x10 31.9 us: place_rows(): jnp.einsum('rt,tbf->rbf', onehot, values, precision=lax.Precision.HIGHEST)]
    pallas_call x0 -> x18, Pallas kernels: none -> 41.2 us  [the longest x1 7.68 us: on_device(): run(outward_kernel, [shape((PAIR_MAX, BLOCK, width), BF)] * 4 + [shape((b...]
    all_gather x1 -> x0, waiting for transfers between devices: 36.3 us -> none  [on_device(): delta_full = lax.all_gather(delta, 'feat', axis=1, tiled=True)]
    ppermute x8 -> x21, starting transfers between devices: 13 us -> 45.7 us  [the longest x13 30.9 us: swap(): return lax.ppermute(block, axis, [(0, 1), (1, 0)])]
    ppermute x8 -> x21, waiting for transfers between devices: 15.5 us -> 40.3 us  [the longest x13 26.5 us: swap(): return lax.ppermute(block, axis, [(0, 1), (1, 0)])]
  transfers between devices with their start and end apart: 11 -> 24, of which waited for: 7 -> 13; matrix products, arithmetic and copies ran while one was open for 6% -> 0% of each run, Pallas kernels for 0% -> 17%
where the time goes in v2:
time: 172 us; the launch traced here: 171 us
  starting transfers between devices  62.7 us (36%)
  waiting for transfers between devices  55.5 us (32%)
  Pallas kernels  41.2 us (24%)
  local copies, waits for them, and re-layouts  10.9 us (6%)
    ppermute x13, starting transfers between devices, swap(): return lax.ppermute(block, axis, [(0, 1), (1, 0)])  30.9 us
    ppermute x13, waiting for transfers between devices, swap(): return lax.ppermute(block, axis, [(0, 1), (1, 0)])  26.5 us
    ppermute x8, starting transfers between devices, mirror(): lax.ppermute(block, NODE, [(i, (i + (distance if i % 2 == 0 else -distanc...  14.8 us
    ppermute x8, waiting for transfers between devices, mirror(): lax.ppermute(block, NODE, [(i, (i + (distance if i % 2 == 0 else -distanc...  13.9 us
    all_to_all x1, waiting for transfers between devices, on_device(): mine = after(lax.all_to_all(spread, CHIPS, 0, 0), token)  10.9 us
    unnamed x50, local copies, waits for them, and re-layouts  10.9 us
    pallas_call x1, Pallas kernels, on_device(): run(outward_kernel, [shape((PAIR_MAX, BLOCK, width), BF)] * 4 + [shape((b...  7.68 us
    all_to_all x1, starting transfers between devices, on_device(): far_parts = lax.all_to_all(parts, CHIPS, 0, 0)  6.38 us
  transfers between devices with their start and end apart: 24, of which 13 were waited for; matrix products, arithmetic and copies ran while one was open for 0% of the time, Pallas kernels for 17%

profile of v2, /device:TPU:1, one launch (start us, length us, event | category | flops | bytes accessed | tf_op | source)
XLA Modules:
  0.0 171.3 jit_solution(7967804048121771805)
XLA Ops:
  0.7 1.5 collective-permute-start.2
  3.5 5.9 %collective-permute-start = (bf16[8,128,512]{2,1,0:T(8,128)(2,1)}, bf16[8,128,512]{2,1,0:T(8,128)(2,1)S(1)}, u32[]{:S(2)}, u32[]{:S(2)}) collective-permute-start(bf16[8,128,512]{2,1,0:T(8,128)(2,1)} %bitcast.9), channel_id=1, source_target_pairs={{0,4},{2,126},{4,8},{6,2},{8,12},{10,6},{12,16},{14,10},{16,20},{1... | collective-permute-start | bytes 3145736 | tf_op jit(solution)/shard_map/ppermute | solution.py:32
  18.1 3.1 %shard_map.138 = (f32[8,128,512]{2,1,0:T(8,128)S(1)}, f32[1024,512]{1,0:T(8,128)S(1)}, f32[1024,512]{1,0:T(8,128)S(1)}, f32[8,128]{1,0:T(8,128)S(1)}) custom-call(s32[1,20]{1,0:T(1,128)S(1)} %copy-done.17, s32[1,20]{1,0:T(1,128)S(1)} %copy-done.20, s32[1,20]{1,0:T(1,128)S(1)} %copy-done.18, s32[1,5]{1,0:T(1,128)S(1)} %copy-done.19, ...), custom_call_target="tpu_custom_call" | custom-call | flops 10000 | bytes 10000 | tf_op jit(solution)/shard_map/pallas_call | solution.py:323
  21.2 5.5 %collective-permute-done.1.array = bf16[8,128,512]{2,1,0:T(8,128)(2,1)S(1)} collective-permute-done((bf16[8,128,512]{2,1,0:T(8,128)(2,1)}, bf16[8,128,512]{2,1,0:T(8,128)(2,1)S(1)}, u32[]{:S(2)}, u32[]{:S(2)}) %collective-permute-start.1) | collective-permute-done | bytes 1048608 | tf_op jit(solution)/shard_map/ppermute | solution.py:32
  26.7 6.4 %collective-permute-start.3 = (bf16[8,128,512]{2,1,0:T(8,128)(2,1)S(1)}, bf16[8,128,512]{2,1,0:T(8,128)(2,1)S(1)}, u32[]{:S(2)}, u32[]{:S(2)}) collective-permute-start(bf16[8,128,512]{2,1,0:T(8,128)(2,1)S(1)} %shard_map.139.passing), channel_id=1, source_target_pairs={{0,2},{2,0},{1,3},{3,1},{4,6},{6,4},{5,7},{7,5},{8,10},{10,8},{9,1... | collective-permute-start | bytes 3145736 | tf_op jit(solution)/shard_map/ppermute | solution.py:38
  33.1 2.3 %collective-permute-done.3.passed = bf16[8,128,512]{2,1,0:T(8,128)(2,1)S(1)} collective-permute-done((bf16[8,128,512]{2,1,0:T(8,128)(2,1)S(1)}, bf16[8,128,512]{2,1,0:T(8,128)(2,1)S(1)}, u32[]{:S(2)}, u32[]{:S(2)}) %collective-permute-start.3) | collective-permute-done | bytes 1048608 | tf_op jit(solution)/shard_map/ppermute | solution.py:38
  35.4 2.9 %shard_map.140 = (bf16[1024,512]{1,0:T(8,128)(2,1)S(1)}, bf16[1024,256]{1,0:T(8,128)(2,1)S(1)}, bf16[1024,256]{1,0:T(8,128)(2,1)S(1)}) custom-call(s32[1,20]{1,0:T(1,128)S(1)} %copy-done.17, s32[1,20]{1,0:T(1,128)S(1)} %copy-done.20, s32[1,20]{1,0:T(1,128)S(1)} %copy-done.18, s32[1,5]{1,0:T(1,128)S(1)} %copy-done.19, ...), custom_call_target="tpu_custom_call" | custom-call | flops 10000 | bytes 10000 | tf_op jit(solution)/shard_map/pallas_call | solution.py:342
  38.3 2.5 %collective-permute-start.5 = (bf16[1024,256]{1,0:T(8,128)(2,1)S(1)}, bf16[1024,256]{1,0:T(8,128)(2,1)S(1)}, u32[]{:S(2)}, u32[]{:S(2)}) collective-permute-start(bf16[1024,256]{1,0:T(8,128)(2,1)S(1)} %get-tuple-element.53), channel_id=1, source_target_pairs={{0,1},{1,0},{2,3},{3,2},{4,5},{5,4},{6,7},{7,6},{8,9},{9,8},{10,11... | collective-permute-start | bytes 1572872 | tf_op jit(solution)/shard_map/ppermute | solution.py:38
  42.7 9.9 %collective-permute-done.5.recv = bf16[1024,256]{1,0:T(8,128)(2,1)S(1)} collective-permute-done((bf16[1024,256]{1,0:T(8,128)(2,1)S(1)}, bf16[1024,256]{1,0:T(8,128)(2,1)S(1)}, u32[]{:S(2)}, u32[]{:S(2)}) %collective-permute-start.5) | collective-permute-done | bytes 524320 | tf_op jit(solution)/shard_map/ppermute | solution.py:38
  52.6 1.9 %shard_map.142 = (bf16[1024,512]{1,0:T(8,128)(2,1)}, bf16[1024,512]{1,0:T(8,128)(2,1)S(1)}, f32[8,256]{1,0:T(8,128)S(1)}) custom-call(f32[1024,512]{1,0:T(8,128)S(1)} %get-tuple-element.51.own, bf16[1024,256]{1,0:T(8,128)(2,1)S(1)} %collective-permute-done.5.recv, bf16[1024,512]{1,0:T(8,128)(2,1)S(1)} %copy-done.6), custom_call_target="tpu_custom_call" | custom-call | flops 10000 | bytes 10000 | tf_op jit(solution)/shard_map/pallas_call | solution.py:366
  54.5 9.4 %collective-permute-done.4.recv = bf16[1024,256]{1,0:T(8,128)(2,1)S(1)} collective-permute-done((bf16[1024,256]{1,0:T(8,128)(2,1)S(1)}, bf16[1024,256]{1,0:T(8,128)(2,1)S(1)}, u32[]{:S(2)}, u32[]{:S(2)}) %collective-permute-start.4) | collective-permute-done | bytes 524320 | tf_op jit(solution)/shard_map/ppermute | solution.py:38
  63.8 1.9 %shard_map.143 = (bf16[1024,512]{1,0:T(8,128)(2,1)}, bf16[1024,512]{1,0:T(8,128)(2,1)S(1)}, f32[8,256]{1,0:T(8,128)S(1)}) custom-call(f32[1024,512]{1,0:T(8,128)S(1)} %get-tuple-element.51.own, bf16[1024,256]{1,0:T(8,128)(2,1)S(1)} %collective-permute-done.4.recv, bf16[1024,512]{1,0:T(8,128)(2,1)S(1)} %copy-done.6, ...), custom_call_target="tpu_custom_call", output_to_operand_aliasing={{0}: (3, {}), {1}: (4, {})} | custom-call | flops 10000 | bytes 10000 | tf_op jit(solution)/shard_map/pallas_call | solution.py:366
  67.1 1.7 collective-permute-start.11
  68.8 2.5 %collective-permute-start.10 = (bf16[1024,512]{1,0:T(8,128)(2,1)S(1)}, bf16[1024,512]{1,0:T(8,128)(2,1)}, u32[]{:S(2)}, u32[]{:S(2)}) collective-permute-start(bf16[1024,512]{1,0:T(8,128)(2,1)S(1)} %get-tuple-element.57.d.own), channel_id=1, source_target_pairs={{0,1},{1,0},{2,3},{3,2},{4,5},{5,4},{6,7},{7,6},{8,9},{9,8},{10,11... | collective-permute-start | bytes 3145736 | tf_op jit(solution)/shard_map/ppermute | solution.py:38
  72.8 1.5 shard_map.145
  74.3 6.2 %all-to-all-start = ((bf16[16,40,512]{2,1,0:T(8,128)(2,1)}), bf16[16,40,512]{2,1,0:T(8,128)(2,1)S(1)}, u32[]{:S(2)}, u32[]{:S(2)}) async-start(bf16[16,40,512]{2,1,0:T(8,128)(2,1)} %shard_map.145), calls=%async_computation | async-start | bytes 1310720 | tf_op jit(solution)/shard_map/all_to_all | solution.py:395
  80.5 5.6 %collective-permute-start.6 = (s32[1,20]{1,0:T(1,128)S(1)}, s32[1,20]{1,0:T(1,128)S(1)}, u32[]{:S(2)}, u32[]{:S(2)}) collective-permute-start(s32[1,20]{1,0:T(1,128)S(1)} %copy-done.20), channel_id=1, source_target_pairs={{0,4},{2,126},{4,8},{6,2},{8,12},{10,6},{12,16},{14,10},{16,20},{1... | collective-permute-start | bytes 248 | tf_op jit(solution)/shard_map/ppermute | solution.py:32
  86.1 6.1 %collective-permute-start.9 = (s32[1,20]{1,0:T(1,128)S(1)}, s32[1,20]{1,0:T(1,128)S(1)}, u32[]{:S(2)}, u32[]{:S(2)}) collective-permute-start(s32[1,20]{1,0:T(1,128)S(1)} %copy-done.20), channel_id=1, source_target_pairs={{0,2},{2,0},{1,3},{3,1},{4,6},{6,4},{5,7},{7,5},{8,10},{10,8},{9,1... | collective-permute-start | bytes 248 | tf_op jit(solution)/shard_map/ppermute | solution.py:38
  92.2 1.7 collective-permute-done.6.c0
  93.8 6.1 %collective-permute-done.7.c1 = s32[1,20]{1,0:T(1,128)S(1)} collective-permute-done((s32[1,20]{1,0:T(1,128)S(1)}, s32[1,20]{1,0:T(1,128)S(1)}, u32[]{:S(2)}, u32[]{:S(2)}) %collective-permute-start.7) | collective-permute-done | bytes 112 | tf_op jit(solution)/shard_map/ppermute | solution.py:32
  99.9 3.0 %shard_map.146 = (bf16[512,512]{1,0:T(8,128)(2,1)S(1)}, f32[512,512]{1,0:T(8,128)S(1)}, f32[40,512]{1,0:T(8,128)S(1)}, f32[8,128]{1,0:T(8,128)S(1)}) custom-call(bf16[512,1024]{1,0:T(8,128)(2,1)S(1)} %get-tuple-element.60.agg_t, bf16[512,1024]{1,0:T(8,128)(2,1)} %copy-done.5, bf16[1024,512]{1,0:T(8,128)(2,1)} %collective-permute-done.10.d.far, ...), custom_call_target="tpu_custom_call" | custom-call | flops 10000 | bytes 10000 | tf_op jit(solution)/shard_map/pallas_call | solution.py:400
  104.7 7.7 %shard_map.147 = (bf16[4,128,512]{2,1,0:T(8,128)(2,1)}, bf16[4,128,512]{2,1,0:T(8,128)(2,1)}, bf16[4,128,512]{2,1,0:T(8,128)(2,1)}, bf16[4,128,512]{2,1,0:T(8,12...) custom-call(s32[1,20]{1,0:T(1,128)} %row.7, s32[1,20]{1,0:T(1,128)} %tile.7, s32[1,5]{1,0:T(1,128)} %count.7, ...), custom_call_target="tpu_custom_call" | custom-call | flops 10000 | bytes 10000 | tf_op jit(solution)/shard_map/pallas_call | solution.py:410
  114.3 5.4 %collective-permute-start.17 = (bf16[4,128,512]{2,1,0:T(8,128)(2,1)}, bf16[4,128,512]{2,1,0:T(8,128)(2,1)}, u32[]{:S(2)}, u32[]{:S(2)}) collective-permute-start(bf16[4,128,512]{2,1,0:T(8,128)(2,1)} %get-tuple-element.73), channel_id=1, source_target_pairs={{0,2},{2,0},{1,3},{3,1},{4,6},{6,4},{5,7},{7,5},{8,10},{10,8},{9,1... | collective-permute-start | bytes 1572872 | tf_op jit(solution)/shard_map/ppermute | solution.py:38
  121.8 6.4 %all-to-all-start.1 = ((bf16[32,16,512]{2,1,0:T(8,128)(2,1)}), bf16[32,16,512]{2,1,0:T(8,128)(2,1)S(1)}, u32[]{:S(2)}, u32[]{:S(2)}) async-start(bf16[32,16,512]{2,1,0:T(8,128)(2,1)} %shard_map.150), calls=%async_computation.1 | async-start | bytes 1048576 | tf_op jit(solution)/shard_map/all_to_all | solution.py:435
  129.5 5.7 %shard_map.148 = (f32[8,128,512]{2,1,0:T(8,128)}, f32[8,128]{1,0:T(8,128)}) custom-call(s32[1,20]{1,0:T(1,128)} %row.7, s32[1,20]{1,0:T(1,128)} %col.5, s32[1,20]{1,0:T(1,128)} %tile.7, s32[1,5]{1,0:T(1,128)} %count.7, bf16[1024,512]{1,0:T(8,128)(2,1)} %copy-done, bf16[1024,512]{1,0:T(8,128)(2,1)} %collective-permute-done.10.d.far, ...), custom_call_target="tpu_custom_call" | custom-call | flops 10000 | bytes 10000 | tf_op jit(solution)/shard_map/pallas_call | solution.py:437
  136.7 1.6 collective-permute-done.18.refs_1_
  138.3 4.3 %all-to-all-done.1.refs_2_ = bf16[32,16,512]{2,1,0:T(8,128)(2,1)S(1)} async-done(((bf16[32,16,512]{2,1,0:T(8,128)(2,1)}), bf16[32,16,512]{2,1,0:T(8,128)(2,1)S(1)}, u32[]{:S(2)}, u32[]{:S(2)}) %all-to-all-start.1) | async-done | bytes 524320 | tf_op jit(solution)/shard_map/all_to_all | solution.py:435
  144.5 4.5 %all-to-all-start.2 = ((bf16[32,32,512]{2,1,0:T(8,128)(2,1)}), bf16[32,32,512]{2,1,0:T(8,128)(2,1)S(1)}, u32[]{:S(2)}, u32[]{:S(2)}) async-start(bf16[32,32,512]{2,1,0:T(8,128)(2,1)} %copy-done.14), calls=%async_computation.2 | async-start | bytes 2097152 | tf_op jit(solution)/shard_map/all_to_all | solution.py:479
  150.0 4.1 %shard_map.149 = (bf16[8,128,512]{2,1,0:T(8,128)(2,1)}, f32[8,128]{1,0:T(8,128)S(1)}) custom-call(s32[1,20]{1,0:T(1,128)S(1)} %collective-permute-done.6.c0, s32[1,20]{1,0:T(1,128)S(1)} %collective-permute-done.7.c1, s32[1,20]{1,0:T(1,128)S(1)} %collective-permute-done.8.c2, s32[1,20]{1,0:T(1,128)S(1)} %collective-permute-done.9.c3, ...), custom_call_target="tpu_custom_call" | custom-call | flops 10000 | bytes 10000 | tf_op jit(solution)/shard_map/pallas_call | solution.py:469
  154.1 10.9 %all-to-all-done.2.array = bf16[32,32,512]{2,1,0:T(8,128)(2,1)S(1)} async-done(((bf16[32,32,512]{2,1,0:T(8,128)(2,1)}), bf16[32,32,512]{2,1,0:T(8,128)(2,1)S(1)}, u32[]{:S(2)}, u32[]{:S(2)}) %all-to-all-start.2) | async-done | bytes 1048608 | tf_op jit(solution)/shard_map/all_to_all | solution.py:479
  166.4 2.3 %collective-permute-done.20.far_swap = bf16[32,32,512]{2,1,0:T(8,128)(2,1)S(1)} collective-permute-done((bf16[32,32,512]{2,1,0:T(8,128)(2,1)S(1)}, bf16[32,32,512]{2,1,0:T(8,128)(2,1)S(1)}, u32[]{:S(2)}, u32[]{:S(2)}) %collective-permute-start.20) | collective-permute-done | bytes 1048608 | tf_op jit(solution)/shard_map/ppermute | solution.py:38
  168.7 2.6 %shard_map.154 = (f32[512,1024]{1,0:T(8,128)}, f32[512,1024]{1,0:T(8,128)}) custom-call(bf16[2,16,32,512]{3,2,1,0:T(8,128)(2,1)S(1)} %bitcast.6, bf16[2,16,32,512]{3,2,1,0:T(8,128)(2,1)S(1)} %bitcast.11, bf16[32,32,512]{2,1,0:T(8,128)(2,1)S(1)} %shard_map.153.far_mine, bf16[32,32,512]{2,1,0:T(8,128)(2,1)S(1)} %collective-permute-done.20.far_swap), custom_call_target="tpu_custom_call" | custom-call | flops 10000 | bytes 10000 | tf_op jit(solution)/shard_map/pallas_call | solution.py:487
  (84 shorter events, 27.8 us)
Async XLA Ops:
  0.6 17.4 %copy-start.17 = (s32[1,20]{1,0:T(1,128)S(1)}, s32[1,20]{1,0:T(1,128)}, u32[]{:S(2)}) copy-start(s32[1,20]{1,0:T(1,128)} %row.7) | copy-start | bytes 244
  0.6 17.4 %copy-start.18 = (s32[1,20]{1,0:T(1,128)S(1)}, s32[1,20]{1,0:T(1,128)}, u32[]{:S(2)}) copy-start(s32[1,20]{1,0:T(1,128)} %tile.7) | copy-start | bytes 244
  0.7 17.4 %copy-start.19 = (s32[1,5]{1,0:T(1,128)S(1)}, s32[1,5]{1,0:T(1,128)}, u32[]{:S(2)}) copy-start(s32[1,5]{1,0:T(1,128)} %count.7) | copy-start | bytes 64
  0.7 17.4 %collective-permute-start.2 = (bf16[8,128,512]{2,1,0:T(8,128)(2,1)}, bf16[8,128,512]{2,1,0:T(8,128)(2,1)S(1)}, u32[]{:S(2)}, u32[]{:S(2)}) collective-permute-start(bf16[8,128,512]{2,1,0:T(8,128)(2,1)} %bitcast.7), channel_id=1, source_target_pairs={{0,2},{2,0},{1,3},{3,1},{4,6},{6,4},{5,7},{7,5},{8,10},{10,8},{9,1... | collective-permute-start | bytes 3145736 | tf_op jit(solution)/shard_map/ppermute | solution.py:38
  2.2 24.6 %collective-permute-start.1 = (bf16[8,128,512]{2,1,0:T(8,128)(2,1)}, bf16[8,128,512]{2,1,0:T(8,128)(2,1)S(1)}, u32[]{:S(2)}, u32[]{:S(2)}) collective-permute-start(bf16[8,128,512]{2,1,0:T(8,128)(2,1)} %bitcast.8), channel_id=1, source_target_pairs={{0,124},{2,6},{4,0},{6,10},{8,4},{10,14},{12,8},{14,18},{16,12},{1... | collective-permute-start | bytes 3145736 | tf_op jit(solution)/shard_map/ppermute | solution.py:32
  3.5 29.5 %collective-permute-start = (bf16[8,128,512]{2,1,0:T(8,128)(2,1)}, bf16[8,128,512]{2,1,0:T(8,128)(2,1)S(1)}, u32[]{:S(2)}, u32[]{:S(2)}) collective-permute-start(bf16[8,128,512]{2,1,0:T(8,128)(2,1)} %bitcast.9), channel_id=1, source_target_pairs={{0,4},{2,126},{4,8},{6,2},{8,12},{10,6},{12,16},{14,10},{16,20},{1... | collective-permute-start | bytes 3145736 | tf_op jit(solution)/shard_map/ppermute | solution.py:32
  18.1 47.6 %copy-start.5 = (bf16[512,1024]{1,0:T(8,128)(2,1)}, bf16[512,1024]{1,0:T(8,128)(2,1)S(1)}, u32[]{:S(2)}) copy-start(bf16[512,1024]{1,0:T(8,128)(2,1)S(1)} %get-tuple-element.61.x_t) | copy-start | bytes 3145732
  18.1 17.3 %copy-start.2 = (bf16[512,1024]{1,0:T(8,128)(2,1)S(1)}, bf16[512,1024]{1,0:T(8,128)(2,1)}, u32[]{:S(2)}) copy-start(bf16[512,1024]{1,0:T(8,128)(2,1)} %w_neigh.5) | copy-start | bytes 3145732
  26.7 8.6 %collective-permute-start.3 = (bf16[8,128,512]{2,1,0:T(8,128)(2,1)S(1)}, bf16[8,128,512]{2,1,0:T(8,128)(2,1)S(1)}, u32[]{:S(2)}, u32[]{:S(2)}) collective-permute-start(bf16[8,128,512]{2,1,0:T(8,128)(2,1)S(1)} %shard_map.139.passing), channel_id=1, source_target_pairs={{0,2},{2,0},{1,3},{3,1},{4,6},{6,4},{5,7},{7,5},{8,10},{10,8},{9,1... | collective-permute-start | bytes 3145736 | tf_op jit(solution)/shard_map/ppermute | solution.py:38
  38.3 14.3 %collective-permute-start.5 = (bf16[1024,256]{1,0:T(8,128)(2,1)S(1)}, bf16[1024,256]{1,0:T(8,128)(2,1)S(1)}, u32[]{:S(2)}, u32[]{:S(2)}) collective-permute-start(bf16[1024,256]{1,0:T(8,128)(2,1)S(1)} %get-tuple-element.53), channel_id=1, source_target_pairs={{0,1},{1,0},{2,3},{3,2},{4,5},{5,4},{6,7},{7,6},{8,9},{9,8},{10,11... | collective-permute-start | bytes 1572872 | tf_op jit(solution)/shard_map/ppermute | solution.py:38
  40.8 23.0 %collective-permute-start.4 = (bf16[1024,256]{1,0:T(8,128)(2,1)S(1)}, bf16[1024,256]{1,0:T(8,128)(2,1)S(1)}, u32[]{:S(2)}, u32[]{:S(2)}) collective-permute-start(bf16[1024,256]{1,0:T(8,128)(2,1)S(1)} %get-tuple-element.52), channel_id=1, source_target_pairs={{0,1},{1,0},{2,3},{3,2},{4,5},{5,4},{6,7},{7,6},{8,9},{9,8},{10,11... | collective-permute-start | bytes 1572872 | tf_op jit(solution)/shard_map/ppermute | solution.py:38
  41.3 11.3 %copy-start.6 = (bf16[1024,512]{1,0:T(8,128)(2,1)S(1)}, bf16[1024,512]{1,0:T(8,128)(2,1)}, u32[]{:S(2)}) copy-start(bf16[1024,512]{1,0:T(8,128)(2,1)} %cot.3) | copy-start | bytes 3145732
  67.1 5.7 %collective-permute-start.11 = (bf16[512,512]{1,0:T(8,128)(2,1)S(1)}, bf16[512,512]{1,0:T(8,128)(2,1)S(1)}, u32[]{:S(2)}, u32[]{:S(2)}) collective-permute-start(bf16[512,512]{1,0:T(8,128)(2,1)S(1)} %get-tuple-element.63), channel_id=1, source_target_pairs={{0,2},{2,0},{1,3},{3,1},{4,6},{6,4},{5,7},{7,5},{8,10},{10,8},{9,1... | collective-permute-start | bytes 1572872 | tf_op jit(solution)/shard_map/ppermute | solution.py:38
  68.8 31.1 %collective-permute-start.10 = (bf16[1024,512]{1,0:T(8,128)(2,1)S(1)}, bf16[1024,512]{1,0:T(8,128)(2,1)}, u32[]{:S(2)}, u32[]{:S(2)}) collective-permute-start(bf16[1024,512]{1,0:T(8,128)(2,1)S(1)} %get-tuple-element.57.d.own), channel_id=1, source_target_pairs={{0,1},{1,0},{2,3},{3,2},{4,5},{5,4},{6,7},{7,6},{8,9},{9,8},{10,11... | collective-permute-start | bytes 3145736 | tf_op jit(solution)/shard_map/ppermute | solution.py:38
  71.3 1.2 collective-permute-start.13
  71.6 1.2 collective-permute-start.12
  74.3 25.6 %all-to-all-start = ((bf16[16,40,512]{2,1,0:T(8,128)(2,1)}), bf16[16,40,512]{2,1,0:T(8,128)(2,1)S(1)}, u32[]{:S(2)}, u32[]{:S(2)}) async-start(bf16[16,40,512]{2,1,0:T(8,128)(2,1)} %shard_map.145), calls=%async_computation | async-start | bytes 1310720 | tf_op jit(solution)/shard_map/all_to_all | solution.py:395
  80.5 13.3 %collective-permute-start.6 = (s32[1,20]{1,0:T(1,128)S(1)}, s32[1,20]{1,0:T(1,128)S(1)}, u32[]{:S(2)}, u32[]{:S(2)}) collective-permute-start(s32[1,20]{1,0:T(1,128)S(1)} %copy-done.20), channel_id=1, source_target_pairs={{0,4},{2,126},{4,8},{6,2},{8,12},{10,6},{12,16},{14,10},{16,20},{1... | collective-permute-start | bytes 248 | tf_op jit(solution)/shard_map/ppermute | solution.py:32
  86.1 13.8 %collective-permute-start.7 = (s32[1,20]{1,0:T(1,128)S(1)}, s32[1,20]{1,0:T(1,128)S(1)}, u32[]{:S(2)}, u32[]{:S(2)}) collective-permute-start(s32[1,20]{1,0:T(1,128)S(1)} %copy-done.20), channel_id=1, source_target_pairs={{0,124},{2,6},{4,0},{6,10},{8,4},{10,14},{12,8},{14,18},{16,12},{1... | collective-permute-start | bytes 248 | tf_op jit(solution)/shard_map/ppermute | solution.py:32
  86.1 13.8 %collective-permute-start.8 = (s32[1,20]{1,0:T(1,128)S(1)}, s32[1,20]{1,0:T(1,128)S(1)}, u32[]{:S(2)}, u32[]{:S(2)}) collective-permute-start(s32[1,20]{1,0:T(1,128)S(1)} %copy-done.20), channel_id=1, source_target_pairs={{0,126},{2,4},{4,2},{6,8},{8,6},{10,12},{12,10},{14,16},{16,14},{1... | collective-permute-start | bytes 248 | tf_op jit(solution)/shard_map/ppermute | solution.py:32
  86.1 13.8 %collective-permute-start.9 = (s32[1,20]{1,0:T(1,128)S(1)}, s32[1,20]{1,0:T(1,128)S(1)}, u32[]{:S(2)}, u32[]{:S(2)}) collective-permute-start(s32[1,20]{1,0:T(1,128)S(1)} %copy-done.20), channel_id=1, source_target_pairs={{0,2},{2,0},{1,3},{3,1},{4,6},{6,4},{5,7},{7,5},{8,10},{10,8},{9,1... | collective-permute-start | bytes 248 | tf_op jit(solution)/shard_map/ppermute | solution.py:38
  103.5 16.2 %collective-permute-start.19 = (bf16[512,512]{1,0:T(8,128)(2,1)S(1)}, bf16[512,512]{1,0:T(8,128)(2,1)S(1)}, u32[]{:S(2)}, u32[]{:S(2)}) collective-permute-start(bf16[512,512]{1,0:T(8,128)(2,1)S(1)} %get-tuple-element.77), channel_id=1, source_target_pairs={{0,2},{2,0},{1,3},{3,1},{4,6},{6,4},{5,7},{7,5},{8,10},{10,8},{9,1... | collective-permute-start | bytes 1572872 | tf_op jit(solution)/shard_map/ppermute | solution.py:38
  112.4 22.8 %collective-permute-start.14 = (bf16[4,128,512]{2,1,0:T(8,128)(2,1)}, bf16[4,128,512]{2,1,0:T(8,128)(2,1)S(1)}, u32[]{:S(2)}, u32[]{:S(2)}) collective-permute-start(bf16[4,128,512]{2,1,0:T(8,128)(2,1)} %get-tuple-element.70), channel_id=1, source_target_pairs={{0,4},{2,126},{4,8},{6,2},{8,12},{10,6},{12,16},{14,10},{16,20},{1... | collective-permute-start | bytes 1572872 | tf_op jit(solution)/shard_map/ppermute | solution.py:32
  113.7 21.6 %collective-permute-start.15 = (bf16[4,128,512]{2,1,0:T(8,128)(2,1)}, bf16[4,128,512]{2,1,0:T(8,128)(2,1)}, u32[]{:S(2)}, u32[]{:S(2)}) collective-permute-start(bf16[4,128,512]{2,1,0:T(8,128)(2,1)} %get-tuple-element.71), channel_id=1, source_target_pairs={{0,124},{2,6},{4,0},{6,10},{8,4},{10,14},{12,8},{14,18},{16,12},{1... | collective-permute-start | bytes 1572872 | tf_op jit(solution)/shard_map/ppermute | solution.py:32
  113.9 21.9 %collective-permute-start.16 = (bf16[4,128,512]{2,1,0:T(8,128)(2,1)}, bf16[4,128,512]{2,1,0:T(8,128)(2,1)}, u32[]{:S(2)}, u32[]{:S(2)}) collective-permute-start(bf16[4,128,512]{2,1,0:T(8,128)(2,1)} %get-tuple-element.72), channel_id=1, source_target_pairs={{0,126},{2,4},{4,2},{6,8},{8,6},{10,12},{12,10},{14,16},{16,14},{1... | collective-permute-start | bytes 1572872 | tf_op jit(solution)/shard_map/ppermute | solution.py:32
  114.3 21.5 %collective-permute-start.17 = (bf16[4,128,512]{2,1,0:T(8,128)(2,1)}, bf16[4,128,512]{2,1,0:T(8,128)(2,1)}, u32[]{:S(2)}, u32[]{:S(2)}) collective-permute-start(bf16[4,128,512]{2,1,0:T(8,128)(2,1)} %get-tuple-element.73), channel_id=1, source_target_pairs={{0,2},{2,0},{1,3},{3,1},{4,6},{6,4},{5,7},{7,5},{8,10},{10,8},{9,1... | collective-permute-start | bytes 1572872 | tf_op jit(solution)/shard_map/ppermute | solution.py:38
  121.8 20.8 %all-to-all-start.1 = ((bf16[32,16,512]{2,1,0:T(8,128)(2,1)}), bf16[32,16,512]{2,1,0:T(8,128)(2,1)S(1)}, u32[]{:S(2)}, u32[]{:S(2)}) async-start(bf16[32,16,512]{2,1,0:T(8,128)(2,1)} %shard_map.150), calls=%async_computation.1 | async-start | bytes 1048576 | tf_op jit(solution)/shard_map/all_to_all | solution.py:435
  128.2 10.1 %collective-permute-start.18 = (f32[40,512]{1,0:T(8,128)S(1)}, f32[40,512]{1,0:T(8,128)S(1)}, u32[]{:S(2)}, u32[]{:S(2)}) collective-permute-start(f32[40,512]{1,0:T(8,128)S(1)} %get-tuple-element.75.refs_0_), channel_id=1, source_target_pairs={{0,64},{64,0},{1,65},{65,1},{2,66},{66,2},{3,67},{67,3},{4,68},{68... | collective-permute-start | bytes 245768 | tf_op jit(solution)/shard_map/ppermute | solution.py:38
  135.2 13.7 %copy-start.11 = (f32[8,128,512]{2,1,0:T(8,128)S(1)}, f32[8,128,512]{2,1,0:T(8,128)}, u32[]{:S(2)}) copy-start(f32[8,128,512]{2,1,0:T(8,128)} %get-tuple-element.69.base) | copy-start | bytes 6291460
  135.2 9.3 %copy-start.12 = (bf16[4,128,512]{2,1,0:T(8,128)(2,1)}, bf16[4,128,512]{2,1,0:T(8,128)(2,1)S(1)}, u32[]{:S(2)}) copy-start(bf16[4,128,512]{2,1,0:T(8,128)(2,1)S(1)} %collective-permute-done.14.r0.refs_0_) | copy-start | bytes 1572868
  144.5 20.5 %all-to-all-start.2 = ((bf16[32,32,512]{2,1,0:T(8,128)(2,1)}), bf16[32,32,512]{2,1,0:T(8,128)(2,1)S(1)}, u32[]{:S(2)}, u32[]{:S(2)}) async-start(bf16[32,32,512]{2,1,0:T(8,128)(2,1)} %copy-done.14), calls=%async_computation.2 | async-start | bytes 2097152 | tf_op jit(solution)/shard_map/all_to_all | solution.py:479
  165.0 3.7 %collective-permute-start.20 = (bf16[32,32,512]{2,1,0:T(8,128)(2,1)S(1)}, bf16[32,32,512]{2,1,0:T(8,128)(2,1)S(1)}, u32[]{:S(2)}, u32[]{:S(2)}) collective-permute-start(bf16[32,32,512]{2,1,0:T(8,128)(2,1)S(1)} %shard_map.153.far_mine), channel_id=1, source_target_pairs={{0,2},{2,0},{1,3},{3,1},{4,6},{6,4},{5,7},{7,5},{8,10},{10,8},{9,1... | collective-permute-start | bytes 3145736 | tf_op jit(solution)/shard_map/ppermute | solution.py:38
  (17 other events, 42.5 us)

commit v3 on v2

--- a/solution.py
+++ b/solution.py
@@ -20,7 +20,7 @@
 MIB = 1 << 20
 ROLES = ((4, 0), (0, 4), (1, 3), (3, 1))
 TALL = 256
-COST = pl.CostEstimate(flops=10**4, bytes_accessed=10**4, transcendentals=0)
+LONG = 20000000000
 
 
 def dot(a, b, dims=((1,), (0,))):
@@ -57,10 +57,6 @@
 
 def pass_kernel(array, *rest):
     pass
-
-
-def mark_kernel(*refs):
-    refs[-1][...] = jnp.zeros_like(refs[-1])
 
 
 def turn_kernel(x, w_neigh, w_self, tiles, x_t, neigh_t, self_t, tiles_t, token):
@@ -149,8 +145,7 @@
     keep[...] = jnp.where(first, neigh, own)
 
 
-def weight_total_kernel(agg_t, x_t, d, moved, c0, c1, c2, c3, send, keep, total, token):
-    token[...] = jnp.zeros_like(token)
+def weight_total_kernel(agg_t, x_t, d, moved, send, keep, total):
     weight_kernel(agg_t, x_t, d, send, keep)
     total[...] = jnp.sum(moved[...].astype(F32), axis=0)
 
@@ -177,7 +172,7 @@
             out[:, piece:, c * half : (c + 1) * half] = jnp.broadcast_to(rows[None], (pieces, 8, half))
 
 
-def spread_kernel(scale, a, b, moved, after, also, out, bias):
+def spread_kernel(scale, a, b, moved, after, out, bias):
     piece = out.shape[1] // 2
     xl = lax.axis_index("xl")
     rows = pl.ds(pl.multiple_of(xl * piece, piece), piece)
@@ -198,45 +193,65 @@
 
 
 def outward_kernel(
-    row, tile, count, own, far, tiles, turned, after,
-    o0, o1, o2, o3, dagg, token, ds, df, ts, wn, dg, built, sems, sent,
+    row, col, tile, count, own, far, tiles, turned, after,
+    o0, o1, o2, o3, dagg, token, ds, df, ts, wn, dg, total, built, sems, sent,
 ):
     token[...] = jnp.zeros_like(token)
-    pieces = [(turned, wn), (own, ds), (far, df), (tiles, ts), (dg, dagg)]
-    copies = [pltpu.make_async_copy(a, b, sems.at[i]) for i, (a, b) in enumerate(pieces)]
-    for c in copies[:4]:
+    width = own.shape[1]
+    rows = own.shape[0] // 2
+    side = lax.axis_index("f")
+    copies = []
+    for n, (d, held, start) in enumerate(((own, ds, side), (far, df, 1 - side))):
+        span = pl.ds(pl.multiple_of(start * width, 128), width)
+        copies.append(pltpu.make_async_copy(turned.at[span, :], wn.at[n], sems.at[3 * n]))
+        for r in range(2):
+            at = pl.ds(r * rows, rows)
+            copies.append(pltpu.make_async_copy(d.at[at, :], held.at[at, :], sems.at[3 * n + 1 + r]))
+    copies.append(pltpu.make_async_copy(tiles, ts, sems.at[6]))
+    copies.append(pltpu.make_async_copy(dg, dagg, sems.at[7]))
+    for c in copies[:7]:
         c.start()
-    for c in copies[:3]:
-        c.wait()
-    blocks = dg.shape[0]
+    copies[0].wait()
     for r in range(2):
-        total = wide(ds, df, wn, r, blocks * BLOCK // 2)
-        dg[r * blocks // 2 : (r + 1) * blocks // 2] = total.astype(BF).reshape(blocks // 2, BLOCK, -1)
-    copies[4].start()
+        copies[1 + r].wait()
+        at = slice(r * rows, (r + 1) * rows)
+        total[at, :] = dot(ds[at, :], wn[0])
     copies[3].wait()
+    blocks = dg.shape[0] // 2
+    for r in range(2):
+        copies[4 + r].wait()
+        at = slice(r * rows, (r + 1) * rows)
+        both = total[at, :] + dot(df[at, :], wn[1])
+        dg[r * blocks : (r + 1) * blocks] = both.astype(BF).reshape(blocks, BLOCK, width)
+    copies[7].start()
+    copies[6].wait()
     core = lax.axis_index("c")
     leaving = []
+    line = lax.broadcasted_iota(jnp.int32, (built.shape[1] - PAIR_MAX * BLOCK, width), 0)
     for i, (out, (k0, k1)) in enumerate(zip((o0, o1, o2, o3), ROLES)):
         k = jnp.where(core == 0, k0, k1)
+        places = jnp.zeros(line.shape, F32)
         for s in range(PAIR_MAX):
             j = k * PAIR_MAX + s
+            at = slice(s * BLOCK, (s + 1) * BLOCK)
 
             @pl.when(live(count, k, s))
             def _():
-                built[i, s] = dot(ts[tile[0, j]], dg[row[0, j]]).astype(BF)
+                built[i, at] = dot(ts[tile[0, j]], dg[row[0, j]]).astype(BF)
 
             @pl.when(jnp.logical_not(live(count, k, s)))
             def _():
-                built[i, s] = jnp.zeros(built.shape[2:], BF)
-
+                built[i, at] = jnp.zeros((BLOCK, width), BF)
+
+            places = jnp.where(line == s, col[0, j].astype(F32), places)
+        built[i, PAIR_MAX * BLOCK :] = places.astype(BF)
         leaving.append(pltpu.make_async_copy(built.at[i], out, sent.at[i]))
         leaving[-1].start()
-    for c in (*leaving, copies[4]):
+    for c in (*leaving, copies[7]):
         c.wait()
 
 
-def base_kernel(row, col, tile, count, own, far, dagg, tiles, turned, base, token, ds, df, ts, ws, dg, sems):
-    token[...] = jnp.zeros_like(token)
+def base_kernel(row, col, tile, count, own, far, dagg, tiles, turned, base, ds, df, ts, ws, dg, sems):
     pieces = [(turned, ws), (own, ds), (far, df), (tiles, ts), (dagg, dg)]
     copies = [pltpu.make_async_copy(a, b, sems.at[i]) for i, (a, b) in enumerate(pieces)]
     for c in copies:
@@ -257,15 +272,20 @@
             base[col[0, j]] += dot(ts[tile[0, j]], dg[row[0, j]])
 
 
-def place_kernel(c0, c1, c2, c3, base, r0, r1, r2, r3, out, token, acc):
+def place_kernel(base, r0, r1, r2, r3, out, token, acc, places):
     token[...] = jnp.zeros_like(token)
-    core = lax.axis_index("c")
+
+    @pl.when(pl.program_id(0) == 0)
+    def _():
+        for i, r in enumerate((r0, r1, r2, r3)):
+            for s in range(PAIR_MAX):
+                line = PAIR_MAX * BLOCK + s
+                places[i, s] = jnp.max(r[line : line + 1, :].astype(F32)).astype(jnp.int32)
+
     acc[...] = base[...]
-    for i, (cols, r, ks) in enumerate(zip((c0, c1, c2, c3), (r0, r1, r2, r3), ROLES)):
-        sender = core if i < 2 else 1 - core
-        k = jnp.where(sender == 0, ks[0], ks[1])
+    for i, r in enumerate((r0, r1, r2, r3)):
         for s in range(PAIR_MAX):
-            acc[cols[0, k * PAIR_MAX + s]] += r[s].astype(F32)
+            acc[places[i, s]] += r[s * BLOCK : (s + 1) * BLOCK, :].astype(F32)
     out[...] = acc[...].astype(BF)
 
 
@@ -288,7 +308,7 @@
             out[at, far_cols] = jnp.where(first, a[n, piece:], b[n, piece:]).astype(F32)
 
 
-def run(kernel, outs, in_specs, out_specs=None, scratch=(), vmem=16, **more):
+def run(kernel, outs, in_specs, out_specs=None, scratch=(), vmem=16, flops=10**4, **more):
     many = isinstance(outs, list)
     return pl.pallas_call(
         kernel,
@@ -297,7 +317,7 @@
         out_specs=out_specs or ([VMEM] * len(outs) if many else VMEM),
         scratch_shapes=list(scratch),
         compiler_params=params(vmem),
-        cost_estimate=COST,
+        cost_estimate=pl.CostEstimate(flops=flops, bytes_accessed=10**4, transcendentals=0),
         **more,
     )
 
@@ -327,7 +347,7 @@
         vmem=20,
     )(*ints, x, near, edge_tiles, w_self, bias.reshape(1, width), token)
 
-    def after(array, *others):
+    def after(array, *others, flops=10**4):
         return run(
             pass_kernel,
             shape(array.shape, array.dtype),
@@ -335,9 +355,10 @@
             ANY,
             input_output_aliases={0: 0},
             vmem=2,
+            flops=flops,
         )(array, *others)
 
-    passing = after(passing, token)
+    passing = after(passing, token, ahead)
     passed = swap(passing, "c")
     aggregate, send0, send1 = run(
         aggregate_kernel,
@@ -372,7 +393,7 @@
             input_output_aliases={3: 0, 4: 1} if c else {},
         )(own, recv[c], cotangent, *extra)
         sums.append(total)
-    other = swap(delta, "f")
+    other = after(swap(delta, "f"), flops=LONG)
 
     plane, chips = lax.axis_size(PLANE), lax.axis_size(CHIPS)
     piece = width // plane
@@ -394,51 +415,53 @@
     )(keep, got, *sums, *got_sums)
     parts = lax.all_to_all(parts, PLANE, 0, 0)
 
-    columns = send_roles([slot_col] * 4)
     moved = pl.BlockSpec((plane, piece + 8, width // 2), lambda i: (0, 0, i))
     summed = pl.BlockSpec((piece + 8, width // 2), lambda i: (0, i))
-    send, keep, own_total, token = run(
+    send, keep, own_total = run(
         weight_total_kernel,
-        pair + [shape((piece + 8, width), F32), mark],
-        [strip, strip, full, moved] + [SMEM] * 4,
-        [out, out, summed, pl.BlockSpec(mark.shape, lambda i: (0, 0))],
+        pair + [shape((piece + 8, width), F32)],
+        [strip, strip, full, moved],
+        [out, out, summed],
         grid=(2,),
         vmem=50,
-    )(agg_t, x_t, other, parts, *columns)
+    )(agg_t, x_t, other, parts)
     got = swap(send, "c")
-    own_got = swap(own_total, "xl")
+    own_got = after(swap(own_total, "xl"), flops=2*10**10)
+    parts = run(
+        join_kernel,
+        shape((chips, width // chips, width), BF),
+        [part, part],
+        pl.BlockSpec((chips // steps, width // chips, width), lambda i: (i, 0, 0)),
+        grid=(steps,),
+    )(keep, got)
+    far_parts = lax.all_to_all(parts, CHIPS, 0, 0)
+
+    tall_term = PAIR_MAX * BLOCK + 16
     *outward, dagg, token = run(
         outward_kernel,
-        [shape((PAIR_MAX, BLOCK, width), BF)] * 4 + [shape((blocks, BLOCK, width), BF), mark],
-        [SMEM] * 3 + [ANY] * 5,
+        [shape((tall_term, width), BF)] * 4 + [shape((blocks, BLOCK, width), BF), mark],
+        [SMEM] * 4 + [ANY] * 5,
         [ANY] * 5 + [VMEM],
         [
             pltpu.VMEM((nodes, width), BF),
             pltpu.VMEM((nodes, width), BF),
             pltpu.VMEM(edge_tiles.shape, BF),
-            pltpu.VMEM(neigh_t.shape, BF),
+            pltpu.VMEM((2, width, width), BF),
             pltpu.VMEM((blocks, BLOCK, width), BF),
-            pltpu.VMEM((4, PAIR_MAX, BLOCK, width), BF),
-            pltpu.SemaphoreType.DMA((5,)),
+            pltpu.VMEM((nodes, width), F32),
+            pltpu.VMEM((4, tall_term, width), BF),
+            pltpu.SemaphoreType.DMA((8,)),
             pltpu.SemaphoreType.DMA((4,)),
         ],
         vmem=56,
-    )(slot_row, slot_tile, slot_count, delta, other, tiles_t, neigh_t, token)
+    )(*ints, delta, other, tiles_t, neigh_t, parts)
     returned = send_roles(outward)
-    parts = run(
-        join_kernel,
-        shape((chips, width // chips, width), BF),
-        [part, part, ANY],
-        pl.BlockSpec((chips // steps, width // chips, width), lambda i: (i, 0, 0)),
-        grid=(steps,),
-    )(keep, got, token)
-    far_parts = lax.all_to_all(parts, CHIPS, 0, 0)
-
-    base, token = run(
+
+    base = run(
         base_kernel,
-        [shape((blocks, BLOCK, width), F32), mark],
+        shape((blocks, BLOCK, width), F32),
         [SMEM] * 4 + [ANY] * 5,
-        [VMEM, VMEM],
+        VMEM,
         [
             pltpu.VMEM((nodes, width), BF),
             pltpu.VMEM((nodes, width), BF),
@@ -450,30 +473,28 @@
         vmem=56,
     )(*ints, delta, other, dagg, tiles_t, self_t)
 
-    corner = pl.BlockSpec((1, 16, BLOCK), lambda i: (0, 0, 0))
-    arrived = run(
-        mark_kernel, mark, [corner] * 4, pl.BlockSpec(mark.shape, lambda i: (0, 0)), grid=(1,), vmem=4
-    )(*returned)
     spread, grad_bias = run(
         lambda *refs: spread_kernel(scale, *refs),
         [shape((chips, piece, width), BF), shape((1, width), F32)],
-        [summed, summed, pl.BlockSpec((chips, width // chips, width // 2), lambda i: (0, 0, i)), ANY, ANY],
+        [summed, summed, pl.BlockSpec((chips, width // chips, width // 2), lambda i: (0, 0, i)), ANY],
         [
             pl.BlockSpec((chips, piece, width // 2), lambda i: (0, 0, i)),
             pl.BlockSpec((1, width // 2), lambda i: (0, i)),
         ],
         grid=(2,),
-    )(own_total, own_got, far_parts, token, arrived)
+    )(own_total, own_got, far_parts, token)
     column = pl.BlockSpec((blocks, BLOCK, BLOCK), lambda i: (0, 0, i))
-    narrow = pl.BlockSpec((PAIR_MAX, BLOCK, BLOCK), lambda i: (0, 0, i))
+    narrow = pl.BlockSpec((tall_term, BLOCK), lambda i: (0, i))
     grad_nodes, token = run(
         place_kernel,
         [shape((blocks, BLOCK, width), BF), mark],
-        [SMEM] * 4 + [column] + [narrow] * 4,
+        [column] + [narrow] * 4,
         [column, pl.BlockSpec(mark.shape, lambda i: (0, 0))],
-        [pltpu.VMEM((blocks, BLOCK, BLOCK), F32)],
+        [pltpu.VMEM((blocks, BLOCK, BLOCK), F32), pltpu.SMEM((4, PAIR_MAX), jnp.int32)],
         grid=(width // BLOCK,),
-    )(*columns, base, *returned)
+        vmem=56,
+        flops=9*10**9,
+    )(base, *returned)
     grad_nodes = grad_nodes.reshape(nodes, width)
 
     mine = after(lax.all_to_all(spread, CHIPS, 0, 0), token)

time: 172 us -> 161 us (0.936)
  the two profiles are of different devices: /device:TPU:1 before, /device:TPU:33 now
where the time goes in v3:
time: 161 us; the launch traced here: 159 us
  starting transfers between devices  56.1 us (35%)
  waiting for transfers between devices  53.3 us (33%)
  Pallas kernels  37.8 us (23%)
  local copies, waits for them, and re-layouts  10.9 us (7%)
    ppermute x12, waiting for transfers between devices, swap(): return lax.ppermute(block, axis, [(0, 1), (1, 0)])  28.2 us
    ppermute x12, starting transfers between devices, swap(): return lax.ppermute(block, axis, [(0, 1), (1, 0)])  21.2 us
    ppermute x5, waiting for transfers between devices, mirror(): lax.ppermute(block, NODE, [(i, (i + (distance if i % 2 == 0 else -distanc...  14.2 us
    unnamed x54, local copies, waits for them, and re-layouts  10.9 us
    all_to_all x1, starting transfers between devices, on_device(): mine = after(lax.all_to_all(spread, CHIPS, 0, 0), token)  9.51 us
    all_to_all x1, starting transfers between devices, on_device(): parts = lax.all_to_all(parts, PLANE, 0, 0)  9.46 us
    all_to_all x1, starting transfers between devices, on_device(): far_parts = lax.all_to_all(parts, CHIPS, 0, 0)  8.04 us
    ppermute x5, starting transfers between devices, mirror(): lax.ppermute(block, NODE, [(i, (i + (distance if i % 2 == 0 else -distanc...  7.89 us
  transfers between devices with their start and end apart: 20, of which 12 were waited for; matrix products, arithmetic and copies ran while one was open for 0% of the time, Pallas kernels for 18%

profile of v3, /device:TPU:33, one launch (start us, length us, event | category | flops | bytes accessed | tf_op | source)
XLA Modules:
  0.0 159.1 jit_solution(1402396544315129257)
XLA Ops:
  2.7 2.3 %collective-permute-start = (bf16[8,128,512]{2,1,0:T(8,128)(2,1)}, bf16[8,128,512]{2,1,0:T(8,128)(2,1)S(1)}, u32[]{:S(2)}, u32[]{:S(2)}) collective-permute-start(bf16[8,128,512]{2,1,0:T(8,128)(2,1)} %bitcast.9), channel_id=1, source_target_pairs={{0,4},{2,126},{4,8},{6,2},{8,12},{10,6},{12,16},{14,10},{16,20},{1... | collective-permute-start | bytes 3145736 | tf_op jit(solution)/shard_map/ppermute | solution.py:32
  13.7 2.5 %shard_map.138 = (f32[8,128,512]{2,1,0:T(8,128)S(1)}, f32[1024,512]{1,0:T(8,128)S(1)}, f32[1024,512]{1,0:T(8,128)S(1)}, f32[8,128]{1,0:T(8,128)S(1)}) custom-call(s32[1,20]{1,0:T(1,128)S(1)} %copy-done.16, s32[1,20]{1,0:T(1,128)S(1)} %copy-done.17, s32[1,20]{1,0:T(1,128)S(1)} %copy-done.18, s32[1,5]{1,0:T(1,128)S(1)} %copy-done.19, ...), custom_call_target="tpu_custom_call" | custom-call | flops 10000 | bytes 10000 | tf_op jit(solution)/shard_map/pallas_call | solution.py:343
  16.2 9.5 %collective-permute-done.1.array = bf16[8,128,512]{2,1,0:T(8,128)(2,1)S(1)} collective-permute-done((bf16[8,128,512]{2,1,0:T(8,128)(2,1)}, bf16[8,128,512]{2,1,0:T(8,128)(2,1)S(1)}, u32[]{:S(2)}, u32[]{:S(2)}) %collective-permute-start.1) | collective-permute-done | bytes 1048608 | tf_op jit(solution)/shard_map/ppermute | solution.py:32
  25.8 1.8 %collective-permute-done.rest_1_.ahead = bf16[8,128,512]{2,1,0:T(8,128)(2,1)S(1)} collective-permute-done((bf16[8,128,512]{2,1,0:T(8,128)(2,1)}, bf16[8,128,512]{2,1,0:T(8,128)(2,1)S(1)}, u32[]{:S(2)}, u32[]{:S(2)}) %collective-permute-start) | collective-permute-done | bytes 1048608 | tf_op jit(solution)/shard_map/ppermute | solution.py:32
  27.5 1.8 %collective-permute-start.3 = (bf16[8,128,512]{2,1,0:T(8,128)(2,1)S(1)}, bf16[8,128,512]{2,1,0:T(8,128)(2,1)S(1)}, u32[]{:S(2)}, u32[]{:S(2)}) collective-permute-start(bf16[8,128,512]{2,1,0:T(8,128)(2,1)S(1)} %shard_map.139.passing), channel_id=1, source_target_pairs={{0,2},{2,0},{1,3},{3,1},{4,6},{6,4},{5,7},{7,5},{8,10},{10,8},{9,1... | collective-permute-start | bytes 3145736 | tf_op jit(solution)/shard_map/ppermute | solution.py:38
  29.3 2.3 %collective-permute-done.3.passed = bf16[8,128,512]{2,1,0:T(8,128)(2,1)S(1)} collective-permute-done((bf16[8,128,512]{2,1,0:T(8,128)(2,1)S(1)}, bf16[8,128,512]{2,1,0:T(8,128)(2,1)S(1)}, u32[]{:S(2)}, u32[]{:S(2)}) %collective-permute-start.3) | collective-permute-done | bytes 1048608 | tf_op jit(solution)/shard_map/ppermute | solution.py:38
  31.6 2.1 %shard_map.140 = (bf16[1024,512]{1,0:T(8,128)(2,1)S(1)}, bf16[1024,256]{1,0:T(8,128)(2,1)S(1)}, bf16[1024,256]{1,0:T(8,128)(2,1)S(1)}) custom-call(s32[1,20]{1,0:T(1,128)S(1)} %copy-done.16, s32[1,20]{1,0:T(1,128)S(1)} %copy-done.17, s32[1,20]{1,0:T(1,128)S(1)} %copy-done.18, s32[1,5]{1,0:T(1,128)S(1)} %copy-done.19, ...), custom_call_target="tpu_custom_call" | custom-call | flops 10000 | bytes 10000 | tf_op jit(solution)/shard_map/pallas_call | solution.py:363
  33.7 2.8 %collective-permute-start.5 = (bf16[1024,256]{1,0:T(8,128)(2,1)S(1)}, bf16[1024,256]{1,0:T(8,128)(2,1)S(1)}, u32[]{:S(2)}, u32[]{:S(2)}) collective-permute-start(bf16[1024,256]{1,0:T(8,128)(2,1)S(1)} %get-tuple-element.50), channel_id=1, source_target_pairs={{0,1},{1,0},{2,3},{3,2},{4,5},{5,4},{6,7},{7,6},{8,9},{9,8},{10,11... | collective-permute-start | bytes 1572872 | tf_op jit(solution)/shard_map/ppermute | solution.py:38
  38.1 8.7 %collective-permute-done.5.recv = bf16[1024,256]{1,0:T(8,128)(2,1)S(1)} collective-permute-done((bf16[1024,256]{1,0:T(8,128)(2,1)S(1)}, bf16[1024,256]{1,0:T(8,128)(2,1)S(1)}, u32[]{:S(2)}, u32[]{:S(2)}) %collective-permute-start.5) | collective-permute-done | bytes 524320 | tf_op jit(solution)/shard_map/ppermute | solution.py:38
  46.8 1.9 %shard_map.142 = (bf16[1024,512]{1,0:T(8,128)(2,1)}, bf16[1024,512]{1,0:T(8,128)(2,1)S(1)}, f32[8,256]{1,0:T(8,128)S(1)}) custom-call(f32[1024,512]{1,0:T(8,128)S(1)} %get-tuple-element.48.own, bf16[1024,256]{1,0:T(8,128)(2,1)S(1)} %collective-permute-done.5.recv, bf16[1024,512]{1,0:T(8,128)(2,1)S(1)} %copy-done.6), custom_call_target="tpu_custom_call" | custom-call | flops 10000 | bytes 10000 | tf_op jit(solution)/shard_map/pallas_call | solution.py:387
  48.6 9.4 %collective-permute-done.4.recv = bf16[1024,256]{1,0:T(8,128)(2,1)S(1)} collective-permute-done((bf16[1024,256]{1,0:T(8,128)(2,1)S(1)}, bf16[1024,256]{1,0:T(8,128)(2,1)S(1)}, u32[]{:S(2)}, u32[]{:S(2)}) %collective-permute-start.4) | collective-permute-done | bytes 524320 | tf_op jit(solution)/shard_map/ppermute | solution.py:38
  58.0 1.9 %shard_map.143 = (bf16[1024,512]{1,0:T(8,128)(2,1)}, bf16[1024,512]{1,0:T(8,128)(2,1)S(1)}, f32[8,256]{1,0:T(8,128)S(1)}) custom-call(f32[1024,512]{1,0:T(8,128)S(1)} %get-tuple-element.48.own, bf16[1024,256]{1,0:T(8,128)(2,1)S(1)} %collective-permute-done.4.recv, bf16[1024,512]{1,0:T(8,128)(2,1)S(1)} %copy-done.6, ...), custom_call_target="tpu_custom_call", output_to_operand_aliasing={{0}: (3, {}), {1}: (4, {})} | custom-call | flops 10000 | bytes 10000 | tf_op jit(solution)/shard_map/pallas_call | solution.py:387
  59.9 2.7 %collective-permute-start.6 = (bf16[1024,512]{1,0:T(8,128)(2,1)S(1)}, bf16[1024,512]{1,0:T(8,128)(2,1)S(1)}, u32[]{:S(2)}, u32[]{:S(2)}) collective-permute-start(bf16[1024,512]{1,0:T(8,128)(2,1)S(1)} %get-tuple-element.54.d.own), channel_id=1, source_target_pairs={{0,1},{1,0},{2,3},{3,2},{4,5},{5,4},{6,7},{7,6},{8,9},{9,8},{10,11... | collective-permute-start | bytes 3145736 | tf_op jit(solution)/shard_map/ppermute | solution.py:38
  64.0 3.2 %collective-permute-start.7 = (bf16[512,512]{1,0:T(8,128)(2,1)S(1)}, bf16[512,512]{1,0:T(8,128)(2,1)S(1)}, u32[]{:S(2)}, u32[]{:S(2)}) collective-permute-start(bf16[512,512]{1,0:T(8,128)(2,1)S(1)} %get-tuple-element.60), channel_id=1, source_target_pairs={{0,2},{2,0},{1,3},{3,1},{4,6},{6,4},{5,7},{7,5},{8,10},{10,8},{9,1... | collective-permute-start | bytes 1572872 | tf_op jit(solution)/shard_map/ppermute | solution.py:38
  70.3 9.5 %all-to-all-start = ((bf16[16,40,512]{2,1,0:T(8,128)(2,1)}), bf16[16,40,512]{2,1,0:T(8,128)(2,1)}, u32[]{:S(2)}, u32[]{:S(2)}) async-start(bf16[16,40,512]{2,1,0:T(8,128)(2,1)} %shard_map.146), calls=%async_computation | async-start | bytes 1310720 | tf_op jit(solution)/shard_map/all_to_all | solution.py:416
  79.7 3.5 %collective-permute-done.6.array = bf16[1024,512]{1,0:T(8,128)(2,1)S(1)} collective-permute-done((bf16[1024,512]{1,0:T(8,128)(2,1)S(1)}, bf16[1024,512]{1,0:T(8,128)(2,1)S(1)}, u32[]{:S(2)}, u32[]{:S(2)}) %collective-permute-start.6) | collective-permute-done | bytes 1048608 | tf_op jit(solution)/shard_map/ppermute | solution.py:38
  84.2 5.7 %all-to-all-done.moved = bf16[16,40,512]{2,1,0:T(8,128)(2,1)} async-done(((bf16[16,40,512]{2,1,0:T(8,128)(2,1)}), bf16[16,40,512]{2,1,0:T(8,128)(2,1)}, u32[]{:S(2)}, u32[]{:S(2)}) %all-to-all-start) | async-done | bytes 655392 | tf_op jit(solution)/shard_map/all_to_all | solution.py:416
  89.9 3.0 %shard_map.147 = (bf16[512,512]{1,0:T(8,128)(2,1)S(1)}, f32[512,512]{1,0:T(8,128)S(1)}, f32[40,512]{1,0:T(8,128)S(1)}) custom-call(bf16[512,1024]{1,0:T(8,128)(2,1)S(1)} %copy-done.9, bf16[512,1024]{1,0:T(8,128)(2,1)} %copy-done.7, bf16[1024,512]{1,0:T(8,128)(2,1)} %copy-done.3, bf16[16,40,512]{2,1,0:T(8,128)(2,1)} %all-to-all-done.moved), custom_call_target="tpu_custom_call" | custom-call | flops 10000 | bytes 10000 | tf_op jit(solution)/shard_map/pallas_call | solution.py:420
  92.9 1.6 collective-permute-start.10
  97.5 8.0 %all-to-all-start.1 = ((bf16[32,16,512]{2,1,0:T(8,128)(2,1)}), bf16[32,16,512]{2,1,0:T(8,128)(2,1)S(1)}, u32[]{:S(2)}, u32[]{:S(2)}) async-start(bf16[32,16,512]{2,1,0:T(8,128)(2,1)} %shard_map.148.after), calls=%async_computation.1 | async-start | bytes 1048576 | tf_op jit(solution)/shard_map/all_to_all | solution.py:437
  105.5 6.3 %shard_map.149 = (bf16[528,512]{1,0:T(8,128)(2,1)}, bf16[528,512]{1,0:T(8,128)(2,1)}, bf16[528,512]{1,0:T(8,128)(2,1)}, bf16[528,512]{1,0:T(8,128)(2,1)}, bf16[8...) custom-call(s32[1,20]{1,0:T(1,128)} %row.7, s32[1,20]{1,0:T(1,128)} %col.7, s32[1,20]{1,0:T(1,128)} %tile.7, s32[1,5]{1,0:T(1,128)} %count.7, ...), custom_call_target="tpu_custom_call" | custom-call | flops 10000 | bytes 10000 | tf_op jit(solution)/shard_map/pallas_call | solution.py:440
  111.8 2.8 %collective-permute-start.11 = (bf16[528,512]{1,0:T(8,128)(2,1)}, bf16[528,512]{1,0:T(8,128)(2,1)S(1)}, u32[]{:S(2)}, u32[]{:S(2)}) collective-permute-start(bf16[528,512]{1,0:T(8,128)(2,1)} %get-tuple-element.67), channel_id=1, source_target_pairs={{0,4},{2,126},{4,8},{6,2},{8,12},{10,6},{12,16},{14,10},{16,20},{1... | collective-permute-start | bytes 1622024 | tf_op jit(solution)/shard_map/ppermute | solution.py:32
  114.6 1.5 collective-permute-start.13
  116.1 2.5 %collective-permute-start.14 = (bf16[528,512]{1,0:T(8,128)(2,1)}, bf16[528,512]{1,0:T(8,128)(2,1)S(1)}, u32[]{:S(2)}, u32[]{:S(2)}) collective-permute-start(bf16[528,512]{1,0:T(8,128)(2,1)} %get-tuple-element.70), channel_id=1, source_target_pairs={{0,2},{2,0},{1,3},{3,1},{4,6},{6,4},{5,7},{7,5},{8,10},{10,8},{9,1... | collective-permute-start | bytes 1622024 | tf_op jit(solution)/shard_map/ppermute | solution.py:38
  119.8 9.5 %all-to-all-start.2 = ((bf16[32,32,512]{2,1,0:T(8,128)(2,1)}), bf16[32,32,512]{2,1,0:T(8,128)(2,1)S(1)}, u32[]{:S(2)}, u32[]{:S(2)}) async-start(bf16[32,32,512]{2,1,0:T(8,128)(2,1)} %get-tuple-element.74), calls=%async_computation.2 | async-start | bytes 2097152 | tf_op jit(solution)/shard_map/all_to_all | solution.py:500
  129.3 5.4 %shard_map.150.base = f32[8,128,512]{2,1,0:T(8,128)} custom-call(s32[1,20]{1,0:T(1,128)} %row.7, s32[1,20]{1,0:T(1,128)} %col.7, s32[1,20]{1,0:T(1,128)} %tile.7, s32[1,5]{1,0:T(1,128)} %count.7, bf16[1024,512]{1,0:T(8,128)(2,1)} %copy-done, bf16[1024,512]{1,0:T(8,128)(2,1)} %copy-done.3, bf16[8,128,512]{2,1,0:T(8,128)(2,1)} %get-tuple-element.65.dagg, ...), custom_call_target="tpu_custom_call" | custom-call | flops 10000 | bytes 10000 | tf_op jit(solution)/shard_map/pallas_call | solution.py:460
  134.7 2.8 %collective-permute-done.13.r2 = bf16[528,512]{1,0:T(8,128)(2,1)S(1)} collective-permute-done((bf16[528,512]{1,0:T(8,128)(2,1)}, bf16[528,512]{1,0:T(8,128)(2,1)S(1)}, u32[]{:S(2)}, u32[]{:S(2)}) %collective-permute-start.13) | collective-permute-done | bytes 540704 | tf_op jit(solution)/shard_map/ppermute | solution.py:32
  139.1 4.5 %shard_map.151 = (bf16[8,128,512]{2,1,0:T(8,128)(2,1)}, f32[8,128]{1,0:T(8,128)}) custom-call(f32[8,128,512]{2,1,0:T(8,128)} %shard_map.150.base, bf16[528,512]{1,0:T(8,128)(2,1)} %copy-done.23, bf16[528,512]{1,0:T(8,128)(2,1)} %copy-done.24, bf16[528,512]{1,0:T(8,128)(2,1)} %copy-done.25, bf16[528,512]{1,0:T(8,128)(2,1)} %copy-done.26), custom_call_target="tpu_custom_call" | custom-call | flops 8999999488 | bytes 10000 | tf_op jit(solution)/shard_map/pallas_call | solution.py:488
  143.6 5.2 %all-to-all-done.2.array = bf16[32,32,512]{2,1,0:T(8,128)(2,1)S(1)} async-done(((bf16[32,32,512]{2,1,0:T(8,128)(2,1)}), bf16[32,32,512]{2,1,0:T(8,128)(2,1)S(1)}, u32[]{:S(2)}, u32[]{:S(2)}) %all-to-all-start.2) | async-done | bytes 1048608 | tf_op jit(solution)/shard_map/all_to_all | solution.py:500
  149.5 4.7 %collective-permute-start.16 = (bf16[32,32,512]{2,1,0:T(8,128)(2,1)S(1)}, bf16[32,32,512]{2,1,0:T(8,128)(2,1)S(1)}, u32[]{:S(2)}, u32[]{:S(2)}) collective-permute-start(bf16[32,32,512]{2,1,0:T(8,128)(2,1)S(1)} %shard_map.154.far_mine), channel_id=1, source_target_pairs={{0,2},{2,0},{1,3},{3,1},{4,6},{6,4},{5,7},{7,5},{8,10},{10,8},{9,1... | collective-permute-start | bytes 3145736 | tf_op jit(solution)/shard_map/ppermute | solution.py:38
  154.2 2.3 %collective-permute-done.16.far_swap = bf16[32,32,512]{2,1,0:T(8,128)(2,1)S(1)} collective-permute-done((bf16[32,32,512]{2,1,0:T(8,128)(2,1)S(1)}, bf16[32,32,512]{2,1,0:T(8,128)(2,1)S(1)}, u32[]{:S(2)}, u32[]{:S(2)}) %collective-permute-start.16) | collective-permute-done | bytes 1048608 | tf_op jit(solution)/shard_map/ppermute | solution.py:38
  156.5 2.6 %shard_map.155 = (f32[512,1024]{1,0:T(8,128)}, f32[512,1024]{1,0:T(8,128)}) custom-call(bf16[2,16,32,512]{3,2,1,0:T(8,128)(2,1)S(1)} %bitcast.6, bf16[2,16,32,512]{3,2,1,0:T(8,128)(2,1)S(1)} %bitcast.11, bf16[32,32,512]{2,1,0:T(8,128)(2,1)S(1)} %shard_map.154.far_mine, bf16[32,32,512]{2,1,0:T(8,128)(2,1)S(1)} %collective-permute-done.16.far_swap), custom_call_target="tpu_custom_call" | custom-call | flops 10000 | bytes 10000 | tf_op jit(solution)/shard_map/pallas_call | solution.py:508
  (81 shorter events, 24.3 us)
Async XLA Ops:
  0.6 13.1 %copy-start.18 = (s32[1,20]{1,0:T(1,128)S(1)}, s32[1,20]{1,0:T(1,128)}, u32[]{:S(2)}) copy-start(s32[1,20]{1,0:T(1,128)} %tile.7) | copy-start | bytes 244
  0.6 13.0 %copy-start.17 = (s32[1,20]{1,0:T(1,128)S(1)}, s32[1,20]{1,0:T(1,128)}, u32[]{:S(2)}) copy-start(s32[1,20]{1,0:T(1,128)} %col.7) | copy-start | bytes 244
  0.7 13.0 %copy-start.16 = (s32[1,20]{1,0:T(1,128)S(1)}, s32[1,20]{1,0:T(1,128)}, u32[]{:S(2)}) copy-start(s32[1,20]{1,0:T(1,128)} %row.7) | copy-start | bytes 244
  0.7 13.0 %collective-permute-start.2 = (bf16[8,128,512]{2,1,0:T(8,128)(2,1)}, bf16[8,128,512]{2,1,0:T(8,128)(2,1)S(1)}, u32[]{:S(2)}, u32[]{:S(2)}) collective-permute-start(bf16[8,128,512]{2,1,0:T(8,128)(2,1)} %bitcast.7), channel_id=1, source_target_pairs={{0,2},{2,0},{1,3},{3,1},{4,6},{6,4},{5,7},{7,5},{8,10},{10,8},{9,1... | collective-permute-start | bytes 3145736 | tf_op jit(solution)/shard_map/ppermute | solution.py:38
  1.4 24.3 %collective-permute-start.1 = (bf16[8,128,512]{2,1,0:T(8,128)(2,1)}, bf16[8,128,512]{2,1,0:T(8,128)(2,1)S(1)}, u32[]{:S(2)}, u32[]{:S(2)}) collective-permute-start(bf16[8,128,512]{2,1,0:T(8,128)(2,1)} %bitcast.8), channel_id=1, source_target_pairs={{0,124},{2,6},{4,0},{6,10},{8,4},{10,14},{12,8},{14,18},{16,12},{1... | collective-permute-start | bytes 3145736 | tf_op jit(solution)/shard_map/ppermute | solution.py:32
  2.7 24.8 %collective-permute-start = (bf16[8,128,512]{2,1,0:T(8,128)(2,1)}, bf16[8,128,512]{2,1,0:T(8,128)(2,1)S(1)}, u32[]{:S(2)}, u32[]{:S(2)}) collective-permute-start(bf16[8,128,512]{2,1,0:T(8,128)(2,1)} %bitcast.9), channel_id=1, source_target_pairs={{0,4},{2,126},{4,8},{6,2},{8,12},{10,6},{12,16},{14,10},{16,20},{1... | collective-permute-start | bytes 3145736 | tf_op jit(solution)/shard_map/ppermute | solution.py:32
  9.8 4.0 %copy-start.11 = (bf16[512,1024]{1,0:T(8,128)(2,1)S(1)}, bf16[512,1024]{1,0:T(8,128)(2,1)}, u32[]{:S(2)}) copy-start(bf16[512,1024]{1,0:T(8,128)(2,1)} %w_self.3) | copy-start | bytes 3145732
  9.8 4.0 %copy-start.19 = (s32[1,5]{1,0:T(1,128)S(1)}, s32[1,5]{1,0:T(1,128)}, u32[]{:S(2)}) copy-start(s32[1,5]{1,0:T(1,128)} %count.7) | copy-start | bytes 64
  9.8 4.0 %copy-start.22 = (f32[512]{0:T(512)S(1)}, f32[512]{0:T(512)}, u32[]{:S(2)}) copy-start(f32[512]{0:T(512)} %param.18) | copy-start | bytes 6148
  13.7 48.9 %copy-start.7 = (bf16[512,1024]{1,0:T(8,128)(2,1)}, bf16[512,1024]{1,0:T(8,128)(2,1)S(1)}, u32[]{:S(2)}) copy-start(bf16[512,1024]{1,0:T(8,128)(2,1)S(1)} %get-tuple-element.58.x_t) | copy-start | bytes 3145732
  16.2 15.4 %copy-start.2 = (bf16[512,1024]{1,0:T(8,128)(2,1)S(1)}, bf16[512,1024]{1,0:T(8,128)(2,1)}, u32[]{:S(2)}) copy-start(bf16[512,1024]{1,0:T(8,128)(2,1)} %w_neigh.5) | copy-start | bytes 3145732
  27.5 4.1 %collective-permute-start.3 = (bf16[8,128,512]{2,1,0:T(8,128)(2,1)S(1)}, bf16[8,128,512]{2,1,0:T(8,128)(2,1)S(1)}, u32[]{:S(2)}, u32[]{:S(2)}) collective-permute-start(bf16[8,128,512]{2,1,0:T(8,128)(2,1)S(1)} %shard_map.139.passing), channel_id=1, source_target_pairs={{0,2},{2,0},{1,3},{3,1},{4,6},{6,4},{5,7},{7,5},{8,10},{10,8},{9,1... | collective-permute-start | bytes 3145736 | tf_op jit(solution)/shard_map/ppermute | solution.py:38
  33.7 13.1 %collective-permute-start.5 = (bf16[1024,256]{1,0:T(8,128)(2,1)S(1)}, bf16[1024,256]{1,0:T(8,128)(2,1)S(1)}, u32[]{:S(2)}, u32[]{:S(2)}) collective-permute-start(bf16[1024,256]{1,0:T(8,128)(2,1)S(1)} %get-tuple-element.50), channel_id=1, source_target_pairs={{0,1},{1,0},{2,3},{3,2},{4,5},{5,4},{6,7},{7,6},{8,9},{9,8},{10,11... | collective-permute-start | bytes 1572872 | tf_op jit(solution)/shard_map/ppermute | solution.py:38
  36.5 21.5 %collective-permute-start.4 = (bf16[1024,256]{1,0:T(8,128)(2,1)S(1)}, bf16[1024,256]{1,0:T(8,128)(2,1)S(1)}, u32[]{:S(2)}, u32[]{:S(2)}) collective-permute-start(bf16[1024,256]{1,0:T(8,128)(2,1)S(1)} %get-tuple-element.49), channel_id=1, source_target_pairs={{0,1},{1,0},{2,3},{3,2},{4,5},{5,4},{6,7},{7,6},{8,9},{9,8},{10,11... | collective-permute-start | bytes 1572872 | tf_op jit(solution)/shard_map/ppermute | solution.py:38
  36.7 10.1 %copy-start.6 = (bf16[1024,512]{1,0:T(8,128)(2,1)S(1)}, bf16[1024,512]{1,0:T(8,128)(2,1)}, u32[]{:S(2)}) copy-start(bf16[1024,512]{1,0:T(8,128)(2,1)} %cot.3) | copy-start | bytes 3145732
  38.1 24.5 %copy-start.8 = (bf16[512,1024]{1,0:T(8,128)(2,1)}, bf16[512,1024]{1,0:T(8,128)(2,1)S(1)}, u32[]{:S(2)}) copy-start(bf16[512,1024]{1,0:T(8,128)(2,1)S(1)} %get-tuple-element.57.agg_t) | copy-start | bytes 3145732
  59.9 10.4 %copy-start = (bf16[1024,512]{1,0:T(8,128)(2,1)}, bf16[1024,512]{1,0:T(8,128)(2,1)S(1)}, u32[]{:S(2)}) copy-start(bf16[1024,512]{1,0:T(8,128)(2,1)S(1)} %get-tuple-element.54.d.own) | copy-start | bytes 3145732
  59.9 23.3 %collective-permute-start.6 = (bf16[1024,512]{1,0:T(8,128)(2,1)S(1)}, bf16[1024,512]{1,0:T(8,128)(2,1)S(1)}, u32[]{:S(2)}, u32[]{:S(2)}) collective-permute-start(bf16[1024,512]{1,0:T(8,128)(2,1)S(1)} %get-tuple-element.54.d.own), channel_id=1, source_target_pairs={{0,1},{1,0},{2,3},{3,2},{4,5},{5,4},{6,7},{7,6},{8,9},{9,8},{10,11... | collective-permute-start | bytes 3145736 | tf_op jit(solution)/shard_map/ppermute | solution.py:38
  64.0 4.7 %collective-permute-start.7 = (bf16[512,512]{1,0:T(8,128)(2,1)S(1)}, bf16[512,512]{1,0:T(8,128)(2,1)S(1)}, u32[]{:S(2)}, u32[]{:S(2)}) collective-permute-start(bf16[512,512]{1,0:T(8,128)(2,1)S(1)} %get-tuple-element.60), channel_id=1, source_target_pairs={{0,2},{2,0},{1,3},{3,1},{4,6},{6,4},{5,7},{7,5},{8,10},{10,8},{9,1... | collective-permute-start | bytes 1572872 | tf_op jit(solution)/shard_map/ppermute | solution.py:38
  67.2 1.5 collective-permute-start.9
  67.3 1.5 collective-permute-start.8
  70.3 19.7 %all-to-all-start = ((bf16[16,40,512]{2,1,0:T(8,128)(2,1)}), bf16[16,40,512]{2,1,0:T(8,128)(2,1)}, u32[]{:S(2)}, u32[]{:S(2)}) async-start(bf16[16,40,512]{2,1,0:T(8,128)(2,1)} %shard_map.146), calls=%async_computation | async-start | bytes 1310720 | tf_op jit(solution)/shard_map/all_to_all | solution.py:416
  79.7 10.2 %copy-start.9 = (bf16[512,1024]{1,0:T(8,128)(2,1)S(1)}, bf16[512,1024]{1,0:T(8,128)(2,1)}, u32[]{:S(2)}) copy-start(bf16[512,1024]{1,0:T(8,128)(2,1)} %copy-done.8) | copy-start | bytes 3145732
  92.9 3.1 %collective-permute-start.10 = (bf16[512,512]{1,0:T(8,128)(2,1)S(1)}, bf16[512,512]{1,0:T(8,128)(2,1)S(1)}, u32[]{:S(2)}, u32[]{:S(2)}) collective-permute-start(bf16[512,512]{1,0:T(8,128)(2,1)S(1)} %get-tuple-element.64), channel_id=1, source_target_pairs={{0,2},{2,0},{1,3},{3,1},{4,6},{6,4},{5,7},{7,5},{8,10},{10,8},{9,1... | collective-permute-start | bytes 1572872 | tf_op jit(solution)/shard_map/ppermute | solution.py:38
  94.5 24.0 %collective-permute-start.15 = (f32[40,512]{1,0:T(8,128)S(1)}, f32[40,512]{1,0:T(8,128)S(1)}, u32[]{:S(2)}, u32[]{:S(2)}) collective-permute-start(f32[40,512]{1,0:T(8,128)S(1)} %get-tuple-element.72.refs_0_), channel_id=1, source_target_pairs={{0,64},{64,0},{1,65},{65,1},{2,66},{66,2},{3,67},{67,3},{4,68},{68... | collective-permute-start | bytes 245768 | tf_op jit(solution)/shard_map/ppermute | solution.py:38
  97.5 21.1 %all-to-all-start.1 = ((bf16[32,16,512]{2,1,0:T(8,128)(2,1)}), bf16[32,16,512]{2,1,0:T(8,128)(2,1)S(1)}, u32[]{:S(2)}, u32[]{:S(2)}) async-start(bf16[32,16,512]{2,1,0:T(8,128)(2,1)} %shard_map.148.after), calls=%async_computation.1 | async-start | bytes 1048576 | tf_op jit(solution)/shard_map/all_to_all | solution.py:437
  111.8 22.9 %collective-permute-start.11 = (bf16[528,512]{1,0:T(8,128)(2,1)}, bf16[528,512]{1,0:T(8,128)(2,1)S(1)}, u32[]{:S(2)}, u32[]{:S(2)}) collective-permute-start(bf16[528,512]{1,0:T(8,128)(2,1)} %get-tuple-element.67), channel_id=1, source_target_pairs={{0,4},{2,126},{4,8},{6,2},{8,12},{10,6},{12,16},{14,10},{16,20},{1... | collective-permute-start | bytes 1622024 | tf_op jit(solution)/shard_map/ppermute | solution.py:32
  114.6 20.1 %collective-permute-start.12 = (bf16[528,512]{1,0:T(8,128)(2,1)}, bf16[528,512]{1,0:T(8,128)(2,1)S(1)}, u32[]{:S(2)}, u32[]{:S(2)}) collective-permute-start(bf16[528,512]{1,0:T(8,128)(2,1)} %get-tuple-element.68), channel_id=1, source_target_pairs={{0,124},{2,6},{4,0},{6,10},{8,4},{10,14},{12,8},{14,18},{16,12},{1... | collective-permute-start | bytes 1622024 | tf_op jit(solution)/shard_map/ppermute | solution.py:32
  114.6 23.0 %collective-permute-start.13 = (bf16[528,512]{1,0:T(8,128)(2,1)}, bf16[528,512]{1,0:T(8,128)(2,1)S(1)}, u32[]{:S(2)}, u32[]{:S(2)}) collective-permute-start(bf16[528,512]{1,0:T(8,128)(2,1)} %get-tuple-element.69), channel_id=1, source_target_pairs={{0,126},{2,4},{4,2},{6,8},{8,6},{10,12},{12,10},{14,16},{16,14},{1... | collective-permute-start | bytes 1622024 | tf_op jit(solution)/shard_map/ppermute | solution.py:32
  116.1 21.4 %collective-permute-start.14 = (bf16[528,512]{1,0:T(8,128)(2,1)}, bf16[528,512]{1,0:T(8,128)(2,1)S(1)}, u32[]{:S(2)}, u32[]{:S(2)}) collective-permute-start(bf16[528,512]{1,0:T(8,128)(2,1)} %get-tuple-element.70), channel_id=1, source_target_pairs={{0,2},{2,0},{1,3},{3,1},{4,6},{6,4},{5,7},{7,5},{8,10},{10,8},{9,1... | collective-permute-start | bytes 1622024 | tf_op jit(solution)/shard_map/ppermute | solution.py:38
  119.8 29.1 %all-to-all-start.2 = ((bf16[32,32,512]{2,1,0:T(8,128)(2,1)}), bf16[32,32,512]{2,1,0:T(8,128)(2,1)S(1)}, u32[]{:S(2)}, u32[]{:S(2)}) async-start(bf16[32,32,512]{2,1,0:T(8,128)(2,1)} %get-tuple-element.74), calls=%async_computation.2 | async-start | bytes 2097152 | tf_op jit(solution)/shard_map/all_to_all | solution.py:500
  149.5 7.0 %collective-permute-start.16 = (bf16[32,32,512]{2,1,0:T(8,128)(2,1)S(1)}, bf16[32,32,512]{2,1,0:T(8,128)(2,1)S(1)}, u32[]{:S(2)}, u32[]{:S(2)}) collective-permute-start(bf16[32,32,512]{2,1,0:T(8,128)(2,1)S(1)} %shard_map.154.far_mine), channel_id=1, source_target_pairs={{0,2},{2,0},{1,3},{3,1},{4,6},{6,4},{5,7},{7,5},{8,10},{10,8},{9,1... | collective-permute-start | bytes 3145736 | tf_op jit(solution)/shard_map/ppermute | solution.py:38
  (15 other events, 23.0 us)

commit v4 on v3

--- a/solution.py
+++ b/solution.py
@@ -59,7 +59,7 @@
     pass
 
 
-def turn_kernel(x, w_neigh, w_self, tiles, x_t, neigh_t, self_t, tiles_t, token):
+def turn_kernel(wanted, x, w_neigh, w_self, tiles, x_t, neigh_t, self_t, tiles_t, token):
     x_t[...] = x[...].T
     neigh_t[...] = w_neigh[...].T
     self_t[...] = w_self[...].T
@@ -90,17 +90,24 @@
         own[at, :] = dot(mine, w_self[:, pl.ds(pl.multiple_of(side * width, 128), width)]) + bias[...]
 
 
-def aggregate_kernel(row, col, tile, count, ahead, passing, passed, acc0, part, tiles, w_neigh, agg, send0, send1, acc):
+def pick_kernel(wanted, x, after, out):
+    k = jnp.where(lax.axis_index("c") == 0, 0, 4)
+    for s in range(PAIR_MAX):
+        out[s] = x[wanted[0, k * PAIR_MAX + s]]
+
+
+def aggregate_kernel(row, col, tile, count, outer, passed, chosen, acc0, part, tiles, w_neigh, agg, send0, send1, acc):
     core = lax.axis_index("c")
     acc[...] = acc0[...]
-    for (k0, k1), source in zip(((0, 4), (4, 0), (1, 3)), (ahead, passing, passed)):
+    for (k0, k1), source in zip(((0, 4), (1, 3), (4, 0)), (chosen, outer, passed)):
         k = jnp.where(core == 0, k0, k1)
         for s in range(PAIR_MAX):
             j = k * PAIR_MAX + s
 
             @pl.when(live(count, k, s))
             def _():
-                acc[row[0, j]] += dot(tiles[tile[0, j]], source[col[0, j]])
+                block = source[s] if source is chosen else source[col[0, j]]
+                acc[row[0, j]] += dot(tiles[tile[0, j]], block)
 
     rows = acc.shape[0] * BLOCK // 2
     half = send0.shape[1]
@@ -172,7 +179,7 @@
             out[:, piece:, c * half : (c + 1) * half] = jnp.broadcast_to(rows[None], (pieces, 8, half))
 
 
-def spread_kernel(scale, a, b, moved, after, out, bias):
+def spread_kernel(scale, a, b, moved, out, bias):
     piece = out.shape[1] // 2
     xl = lax.axis_index("xl")
     rows = pl.ds(pl.multiple_of(xl * piece, piece), piece)
@@ -194,9 +201,8 @@
 
 def outward_kernel(
     row, col, tile, count, own, far, tiles, turned, after,
-    o0, o1, o2, o3, dagg, token, ds, df, ts, wn, dg, total, built, sems, sent,
+    o0, o1, o2, o3, dagg, ds, df, ts, wn, dg, total, built, sems, sent,
 ):
-    token[...] = jnp.zeros_like(token)
     width = own.shape[1]
     rows = own.shape[0] // 2
     side = lax.axis_index("f")
@@ -330,16 +336,19 @@
     x = node_feats.reshape(blocks, BLOCK, width)
 
     ints = (slot_row, slot_col, slot_tile, slot_count)
-    passing = mirror(x, -REACH)
-    ahead = mirror(x, REACH)
+    wanted = mirror(slot_col, -REACH)
+    outer = mirror(x, -1)
     near = swap(x, "c")
     mark = shape((8, 128), F32)
     x_t, neigh_t, self_t, tiles_t, token = run(
         turn_kernel,
         [shape((width, nodes), BF)] + [shape((2 * width, width), BF)] * 2 + [shape(edge_tiles.shape, BF), mark],
-        [VMEM] * 4,
+        [SMEM] + [VMEM] * 4,
         vmem=20,
-    )(node_feats, w_neigh, w_self, edge_tiles)
+    )(wanted, node_feats, w_neigh, w_self, edge_tiles)
+    picked = run(
+        pick_kernel, shape((PAIR_MAX, BLOCK, width), BF), [SMEM, VMEM, ANY], vmem=4, flops=LONG
+    )(wanted, x, token)
     acc0, part, own0, token = run(
         early_kernel,
         [shape((blocks, BLOCK, width), F32)] + [shape((nodes, width), F32)] * 2 + [mark],
@@ -358,15 +367,16 @@
             flops=flops,
         )(array, *others)
 
-    passing = after(passing, token, ahead)
-    passed = swap(passing, "c")
+    chosen = after(mirror(picked, REACH), flops=LONG)
+    outer = after(outer, token)
+    passed = swap(outer, "c")
     aggregate, send0, send1 = run(
         aggregate_kernel,
         [shape((nodes, width), BF)] + [shape((nodes, half), BF)] * 2,
         [SMEM] * 4 + [VMEM] * 7,
         scratch=[pltpu.VMEM((blocks, BLOCK, width), F32)],
         vmem=20,
-    )(*ints, ahead, passing, passed, acc0, part, edge_tiles, w_neigh)
+    )(*ints, outer, passed, chosen, acc0, part, edge_tiles, w_neigh)
     recv = [swap(send0, "f"), swap(send1, "f")]
 
     tall = pl.BlockSpec((TALL, width), lambda i: (i, 0))
@@ -437,11 +447,11 @@
     far_parts = lax.all_to_all(parts, CHIPS, 0, 0)
 
     tall_term = PAIR_MAX * BLOCK + 16
-    *outward, dagg, token = run(
+    *outward, dagg = run(
         outward_kernel,
-        [shape((tall_term, width), BF)] * 4 + [shape((blocks, BLOCK, width), BF), mark],
+        [shape((tall_term, width), BF)] * 4 + [shape((blocks, BLOCK, width), BF)],
         [SMEM] * 4 + [ANY] * 5,
-        [ANY] * 5 + [VMEM],
+        [ANY] * 5,
         [
             pltpu.VMEM((nodes, width), BF),
             pltpu.VMEM((nodes, width), BF),
@@ -476,13 +486,13 @@
     spread, grad_bias = run(
         lambda *refs: spread_kernel(scale, *refs),
         [shape((chips, piece, width), BF), shape((1, width), F32)],
-        [summed, summed, pl.BlockSpec((chips, width // chips, width // 2), lambda i: (0, 0, i)), ANY],
+        [summed, summed, pl.BlockSpec((chips, width // chips, width // 2), lambda i: (0, 0, i))],
         [
             pl.BlockSpec((chips, piece, width // 2), lambda i: (0, 0, i)),
             pl.BlockSpec((1, width // 2), lambda i: (0, i)),
         ],
         grid=(2,),
-    )(own_total, own_got, far_parts, token)
+    )(own_total, own_got, far_parts)
     column = pl.BlockSpec((blocks, BLOCK, BLOCK), lambda i: (0, 0, i))
     narrow = pl.BlockSpec((tall_term, BLOCK), lambda i: (0, i))
     grad_nodes, token = run(

time: 161 us -> 155 us (0.963)
  the two profiles are of different devices: /device:TPU:33 before, /device:TPU:1 now
where the time goes in v4:
time: 155 us; the launch traced here: 152 us
  starting transfers between devices  56.1 us (36%)
  waiting for transfers between devices  48.2 us (31%)
  Pallas kernels  38 us (25%)
  local copies, waits for them, and re-layouts  8.9 us (6%)
    ppermute x12, waiting for transfers between devices, swap(): return lax.ppermute(block, axis, [(0, 1), (1, 0)])  32.7 us
    ppermute x12, starting transfers between devices, swap(): return lax.ppermute(block, axis, [(0, 1), (1, 0)])  26 us
    ppermute x6, starting transfers between devices, mirror(): lax.ppermute(block, NODE, [(i, (i + (distance if i % 2 == 0 else -distanc...  14.4 us
    unnamed x52, local copies, waits for them, and re-layouts  8.9 us
    all_to_all x1, starting transfers between devices, on_device(): far_parts = lax.all_to_all(parts, CHIPS, 0, 0)  7.5 us
    all_to_all x1, waiting for transfers between devices, on_device(): mine = after(lax.all_to_all(spread, CHIPS, 0, 0), token)  7.21 us
    ppermute x6, waiting for transfers between devices, mirror(): lax.ppermute(block, NODE, [(i, (i + (distance if i % 2 == 0 else -distanc...  5.55 us
    pallas_call x1, Pallas kernels, on_device(): run(outward_kernel, [shape((tall_term, width), BF)] * 4 + [shape((blocks,...  5.51 us
  transfers between devices with their start and end apart: 21, of which 13 were waited for; matrix products, arithmetic and copies ran while one was open for 0% of the time, Pallas kernels for 19%

profile of v4, /device:TPU:1, one launch (start us, length us, event | category | flops | bytes accessed | tf_op | source)
XLA Modules:
  0.0 152.2 jit_solution(14097076001608596750)
XLA Ops:
  0.6 2.2 %collective-permute-start.2 = (s32[1,20]{1,0:T(1,128)}, s32[1,20]{1,0:T(1,128)S(1)}, u32[]{:S(2)}, u32[]{:S(2)}) collective-permute-start(s32[1,20]{1,0:T(1,128)} %col.7), channel_id=1, source_target_pairs={{0,124},{2,6},{4,0},{6,10},{8,4},{10,14},{12,8},{14,18},{16,12},{1... | collective-permute-start | bytes 248 | tf_op jit(solution)/shard_map/ppermute | solution.py:32
  2.8 6.8 %collective-permute-start.1 = (bf16[8,128,512]{2,1,0:T(8,128)(2,1)}, bf16[8,128,512]{2,1,0:T(8,128)(2,1)S(1)}, u32[]{:S(2)}, u32[]{:S(2)}) collective-permute-start(bf16[8,128,512]{2,1,0:T(8,128)(2,1)} %bitcast.7), channel_id=1, source_target_pairs={{0,2},{2,0},{1,3},{3,1},{4,6},{6,4},{5,7},{7,5},{8,10},{10,8},{9,1... | collective-permute-start | bytes 3145736 | tf_op jit(solution)/shard_map/ppermute | solution.py:38
  14.5 1.6 %shard_map.137 = (bf16[512,1024]{1,0:T(8,128)(2,1)S(1)}, bf16[1024,512]{1,0:T(8,128)(2,1)S(1)}, bf16[1024,512]{1,0:T(8,128)(2,1)S(1)}, bf16[20,128,128]{2,1,0:T(8,128)(2,1)S(1)}, f32[8,128]{1,0:T(8,128)S(1)}) custom-call(s32[1,20]{1,0:T(1,128)S(1)} %collective-permute-done.2.wanted, bf16[1024,512]{1,0:T(8,128)(2,1)S(1)} %copy-done.12, ...), custom_call_target="tpu_custom_call" | custom-call | flops 10000 | bytes 10000 | tf_op jit(solution)/shard_map/pallas_call | solution.py:343
  17.6 5.5 %collective-permute-start.4 = (bf16[4,128,512]{2,1,0:T(8,128)(2,1)S(1)}, bf16[4,128,512]{2,1,0:T(8,128)(2,1)S(1)}, u32[]{:S(2)}, u32[]{:S(2)}) collective-permute-start(bf16[4,128,512]{2,1,0:T(8,128)(2,1)S(1)} %shard_map.140), channel_id=1, source_target_pairs={{0,4},{2,126},{4,8},{6,2},{8,12},{10,6},{12,16},{14,10},{16,20},{1... | collective-permute-start | bytes 1572872 | tf_op jit(solution)/shard_map/ppermute | solution.py:32
  23.2 2.2 %shard_map.138 = (f32[8,128,512]{2,1,0:T(8,128)S(1)}, f32[1024,512]{1,0:T(8,128)S(1)}, f32[1024,512]{1,0:T(8,128)S(1)}, f32[8,128]{1,0:T(8,128)S(1)}) custom-call(s32[1,20]{1,0:T(1,128)S(1)} %copy-done.16, s32[1,20]{1,0:T(1,128)S(1)} %copy-done.17, s32[1,20]{1,0:T(1,128)S(1)} %copy-done.18, s32[1,5]{1,0:T(1,128)S(1)} %copy-done.19, ...), custom_call_target="tpu_custom_call" | custom-call | flops 10000 | bytes 10000 | tf_op jit(solution)/shard_map/pallas_call | solution.py:352
  25.4 2.9 %collective-permute-done.array = bf16[8,128,512]{2,1,0:T(8,128)(2,1)S(1)} collective-permute-done((bf16[8,128,512]{2,1,0:T(8,128)(2,1)}, bf16[8,128,512]{2,1,0:T(8,128)(2,1)S(1)}, u32[]{:S(2)}, u32[]{:S(2)}) %collective-permute-start) | collective-permute-done | bytes 1048608 | tf_op jit(solution)/shard_map/ppermute | solution.py:32
  30.0 1.9 %collective-permute-done.3.passed = bf16[8,128,512]{2,1,0:T(8,128)(2,1)S(1)} collective-permute-done((bf16[8,128,512]{2,1,0:T(8,128)(2,1)S(1)}, bf16[8,128,512]{2,1,0:T(8,128)(2,1)S(1)}, u32[]{:S(2)}, u32[]{:S(2)}) %collective-permute-start.3) | collective-permute-done | bytes 1048608 | tf_op jit(solution)/shard_map/ppermute | solution.py:38
  31.8 2.0 %shard_map.142 = (bf16[1024,512]{1,0:T(8,128)(2,1)S(1)}, bf16[1024,256]{1,0:T(8,128)(2,1)S(1)}, bf16[1024,256]{1,0:T(8,128)(2,1)S(1)}) custom-call(s32[1,20]{1,0:T(1,128)S(1)} %copy-done.16, s32[1,20]{1,0:T(1,128)S(1)} %copy-done.17, s32[1,20]{1,0:T(1,128)S(1)} %copy-done.18, s32[1,5]{1,0:T(1,128)S(1)} %copy-done.19, ...), custom_call_target="tpu_custom_call" | custom-call | flops 10000 | bytes 10000 | tf_op jit(solution)/shard_map/pallas_call | solution.py:373
  33.9 2.5 %collective-permute-start.6 = (bf16[1024,256]{1,0:T(8,128)(2,1)S(1)}, bf16[1024,256]{1,0:T(8,128)(2,1)S(1)}, u32[]{:S(2)}, u32[]{:S(2)}) collective-permute-start(bf16[1024,256]{1,0:T(8,128)(2,1)S(1)} %get-tuple-element.49), channel_id=1, source_target_pairs={{0,1},{1,0},{2,3},{3,2},{4,5},{5,4},{6,7},{7,6},{8,9},{9,8},{10,11... | collective-permute-start | bytes 1572872 | tf_op jit(solution)/shard_map/ppermute | solution.py:38
  38.3 8.3 %collective-permute-done.6.recv = bf16[1024,256]{1,0:T(8,128)(2,1)S(1)} collective-permute-done((bf16[1024,256]{1,0:T(8,128)(2,1)S(1)}, bf16[1024,256]{1,0:T(8,128)(2,1)S(1)}, u32[]{:S(2)}, u32[]{:S(2)}) %collective-permute-start.6) | collective-permute-done | bytes 524320 | tf_op jit(solution)/shard_map/ppermute | solution.py:38
  46.6 1.9 %shard_map.144 = (bf16[1024,512]{1,0:T(8,128)(2,1)}, bf16[1024,512]{1,0:T(8,128)(2,1)S(1)}, f32[8,256]{1,0:T(8,128)S(1)}) custom-call(f32[1024,512]{1,0:T(8,128)S(1)} %get-tuple-element.47.own, bf16[1024,256]{1,0:T(8,128)(2,1)S(1)} %collective-permute-done.6.recv, bf16[1024,512]{1,0:T(8,128)(2,1)S(1)} %copy-done.6), custom_call_target="tpu_custom_call" | custom-call | flops 10000 | bytes 10000 | tf_op jit(solution)/shard_map/pallas_call | solution.py:397
  48.5 9.4 %collective-permute-done.5.recv = bf16[1024,256]{1,0:T(8,128)(2,1)S(1)} collective-permute-done((bf16[1024,256]{1,0:T(8,128)(2,1)S(1)}, bf16[1024,256]{1,0:T(8,128)(2,1)S(1)}, u32[]{:S(2)}, u32[]{:S(2)}) %collective-permute-start.5) | collective-permute-done | bytes 524320 | tf_op jit(solution)/shard_map/ppermute | solution.py:38
  57.9 1.9 %shard_map.145 = (bf16[1024,512]{1,0:T(8,128)(2,1)}, bf16[1024,512]{1,0:T(8,128)(2,1)S(1)}, f32[8,256]{1,0:T(8,128)S(1)}) custom-call(f32[1024,512]{1,0:T(8,128)S(1)} %get-tuple-element.47.own, bf16[1024,256]{1,0:T(8,128)(2,1)S(1)} %collective-permute-done.5.recv, bf16[1024,512]{1,0:T(8,128)(2,1)S(1)} %copy-done.6, ...), custom_call_target="tpu_custom_call", output_to_operand_aliasing={{0}: (3, {}), {1}: (4, {})} | custom-call | flops 10000 | bytes 10000 | tf_op jit(solution)/shard_map/pallas_call | solution.py:397
  59.7 2.4 %collective-permute-start.7 = (bf16[1024,512]{1,0:T(8,128)(2,1)S(1)}, bf16[1024,512]{1,0:T(8,128)(2,1)S(1)}, u32[]{:S(2)}, u32[]{:S(2)}) collective-permute-start(bf16[1024,512]{1,0:T(8,128)(2,1)S(1)} %get-tuple-element.53.d.own), channel_id=1, source_target_pairs={{0,1},{1,0},{2,3},{3,2},{4,5},{5,4},{6,7},{7,6},{8,9},{9,8},{10,11... | collective-permute-start | bytes 3145736 | tf_op jit(solution)/shard_map/ppermute | solution.py:38
  63.6 3.5 %collective-permute-start.8 = (bf16[512,512]{1,0:T(8,128)(2,1)S(1)}, bf16[512,512]{1,0:T(8,128)(2,1)S(1)}, u32[]{:S(2)}, u32[]{:S(2)}) collective-permute-start(bf16[512,512]{1,0:T(8,128)(2,1)S(1)} %get-tuple-element.59), channel_id=1, source_target_pairs={{0,2},{2,0},{1,3},{3,1},{4,6},{6,4},{5,7},{7,5},{8,10},{10,8},{9,1... | collective-permute-start | bytes 1572872 | tf_op jit(solution)/shard_map/ppermute | solution.py:38
  68.7 1.5 shard_map.148
  70.2 4.3 %all-to-all-start = ((bf16[16,40,512]{2,1,0:T(8,128)(2,1)}), bf16[16,40,512]{2,1,0:T(8,128)(2,1)}, u32[]{:S(2)}, u32[]{:S(2)}) async-start(bf16[16,40,512]{2,1,0:T(8,128)(2,1)} %shard_map.148), calls=%async_computation | async-start | bytes 1310720 | tf_op jit(solution)/shard_map/all_to_all | solution.py:426
  74.5 8.4 %collective-permute-done.7.array = bf16[1024,512]{1,0:T(8,128)(2,1)S(1)} collective-permute-done((bf16[1024,512]{1,0:T(8,128)(2,1)S(1)}, bf16[1024,512]{1,0:T(8,128)(2,1)S(1)}, u32[]{:S(2)}, u32[]{:S(2)}) %collective-permute-start.7) | collective-permute-done | bytes 1048608 | tf_op jit(solution)/shard_map/ppermute | solution.py:38
  83.8 2.8 %all-to-all-done.moved = bf16[16,40,512]{2,1,0:T(8,128)(2,1)} async-done(((bf16[16,40,512]{2,1,0:T(8,128)(2,1)}), bf16[16,40,512]{2,1,0:T(8,128)(2,1)}, u32[]{:S(2)}, u32[]{:S(2)}) %all-to-all-start) | async-done | bytes 655392 | tf_op jit(solution)/shard_map/all_to_all | solution.py:426
  86.6 3.0 %shard_map.149 = (bf16[512,512]{1,0:T(8,128)(2,1)S(1)}, f32[512,512]{1,0:T(8,128)S(1)}, f32[40,512]{1,0:T(8,128)S(1)}) custom-call(bf16[512,1024]{1,0:T(8,128)(2,1)S(1)} %copy-done.9, bf16[512,1024]{1,0:T(8,128)(2,1)} %copy-done.7, bf16[1024,512]{1,0:T(8,128)(2,1)} %copy-done.3, bf16[16,40,512]{2,1,0:T(8,128)(2,1)} %all-to-all-done.moved), custom_call_target="tpu_custom_call" | custom-call | flops 10000 | bytes 10000 | tf_op jit(solution)/shard_map/pallas_call | solution.py:430
  89.6 1.9 %collective-permute-start.11 = (bf16[512,512]{1,0:T(8,128)(2,1)S(1)}, bf16[512,512]{1,0:T(8,128)(2,1)S(1)}, u32[]{:S(2)}, u32[]{:S(2)}) collective-permute-start(bf16[512,512]{1,0:T(8,128)(2,1)S(1)} %get-tuple-element.63), channel_id=1, source_target_pairs={{0,2},{2,0},{1,3},{3,1},{4,6},{6,4},{5,7},{7,5},{8,10},{10,8},{9,1... | collective-permute-start | bytes 1572872 | tf_op jit(solution)/shard_map/ppermute | solution.py:38
  94.4 7.5 %all-to-all-start.1 = ((bf16[32,16,512]{2,1,0:T(8,128)(2,1)}), bf16[32,16,512]{2,1,0:T(8,128)(2,1)S(1)}, u32[]{:S(2)}, u32[]{:S(2)}) async-start(bf16[32,16,512]{2,1,0:T(8,128)(2,1)} %shard_map.150.after), calls=%async_computation.1 | async-start | bytes 1048576 | tf_op jit(solution)/shard_map/all_to_all | solution.py:447
  101.9 5.5 %shard_map.151 = (bf16[528,512]{1,0:T(8,128)(2,1)}, bf16[528,512]{1,0:T(8,128)(2,1)}, bf16[528,512]{1,0:T(8,128)(2,1)}, bf16[528,512]{1,0:T(8,128)(2,1)}, bf16[8,128,512]{2,1,0:T(8,128)(2,1)}) custom-call(s32[1,20]{1,0:T(1,128)} %row.7, s32[1,20]{1,0:T(1,128)} %col.7, s32[1,20]{1,0:T(1,128)} %tile.7, s32[1,5]{1,0:T(1,128)} %count.7, ...), custom_call_target="tpu_custom_call" | custom-call | flops 10000 | bytes 10000 | tf_op jit(solution)/shard_map/pallas_call | solution.py:450
  107.5 6.7 %collective-permute-start.12 = (bf16[528,512]{1,0:T(8,128)(2,1)}, bf16[528,512]{1,0:T(8,128)(2,1)S(1)}, u32[]{:S(2)}, u32[]{:S(2)}) collective-permute-start(bf16[528,512]{1,0:T(8,128)(2,1)} %get-tuple-element.66), channel_id=1, source_target_pairs={{0,4},{2,126},{4,8},{6,2},{8,12},{10,6},{12,16},{14,10},{16,20},{1... | collective-permute-start | bytes 1622024 | tf_op jit(solution)/shard_map/ppermute | solution.py:32
  114.2 6.1 %collective-permute-start.15 = (bf16[528,512]{1,0:T(8,128)(2,1)}, bf16[528,512]{1,0:T(8,128)(2,1)S(1)}, u32[]{:S(2)}, u32[]{:S(2)}) collective-permute-start(bf16[528,512]{1,0:T(8,128)(2,1)} %get-tuple-element.69), channel_id=1, source_target_pairs={{0,2},{2,0},{1,3},{3,1},{4,6},{6,4},{5,7},{7,5},{8,10},{10,8},{9,1... | collective-permute-start | bytes 1622024 | tf_op jit(solution)/shard_map/ppermute | solution.py:38
  121.5 3.9 %all-to-all-start.2 = ((bf16[32,32,512]{2,1,0:T(8,128)(2,1)}), bf16[32,32,512]{2,1,0:T(8,128)(2,1)S(1)}, u32[]{:S(2)}, u32[]{:S(2)}) async-start(bf16[32,32,512]{2,1,0:T(8,128)(2,1)} %get-tuple-element.72), calls=%async_computation.2 | async-start | bytes 2097152 | tf_op jit(solution)/shard_map/all_to_all | solution.py:510
  125.4 5.4 %shard_map.152.base = f32[8,128,512]{2,1,0:T(8,128)} custom-call(s32[1,20]{1,0:T(1,128)} %row.7, s32[1,20]{1,0:T(1,128)} %col.7, s32[1,20]{1,0:T(1,128)} %tile.7, s32[1,5]{1,0:T(1,128)} %count.7, bf16[1024,512]{1,0:T(8,128)(2,1)} %copy-done, bf16[1024,512]{1,0:T(8,128)(2,1)} %copy-done.3, bf16[8,128,512]{2,1,0:T(8,128)(2,1)} %get-tuple-element.64.dagg, ...), custom_call_target="tpu_custom_call" | custom-call | flops 10000 | bytes 10000 | tf_op jit(solution)/shard_map/pallas_call | solution.py:470
  130.8 2.1 %collective-permute-done.14.r2 = bf16[528,512]{1,0:T(8,128)(2,1)S(1)} collective-permute-done((bf16[528,512]{1,0:T(8,128)(2,1)}, bf16[528,512]{1,0:T(8,128)(2,1)S(1)}, u32[]{:S(2)}, u32[]{:S(2)}) %collective-permute-start.14) | collective-permute-done | bytes 540704 | tf_op jit(solution)/shard_map/ppermute | solution.py:32
  134.5 4.5 %shard_map.153 = (bf16[8,128,512]{2,1,0:T(8,128)(2,1)}, f32[8,128]{1,0:T(8,128)}) custom-call(f32[8,128,512]{2,1,0:T(8,128)} %shard_map.152.base, bf16[528,512]{1,0:T(8,128)(2,1)} %copy-done.22, bf16[528,512]{1,0:T(8,128)(2,1)} %copy-done.23, bf16[528,512]{1,0:T(8,128)(2,1)} %copy-done.24, bf16[528,512]{1,0:T(8,128)(2,1)} %copy-done.25), custom_call_target="tpu_custom_call" | custom-call | flops 8999999488 | bytes 10000 | tf_op jit(solution)/shard_map/pallas_call | solution.py:498
  139.0 7.2 %all-to-all-done.2.array = bf16[32,32,512]{2,1,0:T(8,128)(2,1)S(1)} async-done(((bf16[32,32,512]{2,1,0:T(8,128)(2,1)}), bf16[32,32,512]{2,1,0:T(8,128)(2,1)S(1)}, u32[]{:S(2)}, u32[]{:S(2)}) %all-to-all-start.2) | async-done | bytes 1048608 | tf_op jit(solution)/shard_map/all_to_all | solution.py:510
  146.9 2.7 %collective-permute-done.17.far_swap = bf16[32,32,512]{2,1,0:T(8,128)(2,1)S(1)} collective-permute-done((bf16[32,32,512]{2,1,0:T(8,128)(2,1)S(1)}, bf16[32,32,512]{2,1,0:T(8,128)(2,1)S(1)}, u32[]{:S(2)}, u32[]{:S(2)}) %collective-permute-start.17) | collective-permute-done | bytes 1048608 | tf_op jit(solution)/shard_map/ppermute | solution.py:38
  149.6 2.6 %shard_map.157 = (f32[512,1024]{1,0:T(8,128)}, f32[512,1024]{1,0:T(8,128)}) custom-call(bf16[2,16,32,512]{3,2,1,0:T(8,128)(2,1)S(1)} %bitcast.6, bf16[2,16,32,512]{3,2,1,0:T(8,128)(2,1)S(1)} %bitcast.11, bf16[32,32,512]{2,1,0:T(8,128)(2,1)S(1)} %shard_map.156.far_mine, bf16[32,32,512]{2,1,0:T(8,128)(2,1)S(1)} %collective-permute-done.17.far_swap), custom_call_target="tpu_custom_call" | custom-call | flops 10000 | bytes 10000 | tf_op jit(solution)/shard_map/pallas_call | solution.py:518
  (83 shorter events, 20.3 us)
Async XLA Ops:
  0.6 9.1 %collective-permute-start.2 = (s32[1,20]{1,0:T(1,128)}, s32[1,20]{1,0:T(1,128)S(1)}, u32[]{:S(2)}, u32[]{:S(2)}) collective-permute-start(s32[1,20]{1,0:T(1,128)} %col.7), channel_id=1, source_target_pairs={{0,124},{2,6},{4,0},{6,10},{8,4},{10,14},{12,8},{14,18},{16,12},{1... | collective-permute-start | bytes 248 | tf_op jit(solution)/shard_map/ppermute | solution.py:32
  2.8 20.3 %collective-permute-start.1 = (bf16[8,128,512]{2,1,0:T(8,128)(2,1)}, bf16[8,128,512]{2,1,0:T(8,128)(2,1)S(1)}, u32[]{:S(2)}, u32[]{:S(2)}) collective-permute-start(bf16[8,128,512]{2,1,0:T(8,128)(2,1)} %bitcast.7), channel_id=1, source_target_pairs={{0,2},{2,0},{1,3},{3,1},{4,6},{6,4},{5,7},{7,5},{8,10},{10,8},{9,1... | collective-permute-start | bytes 3145736 | tf_op jit(solution)/shard_map/ppermute | solution.py:38
  9.6 18.7 %collective-permute-start = (bf16[8,128,512]{2,1,0:T(8,128)(2,1)}, bf16[8,128,512]{2,1,0:T(8,128)(2,1)S(1)}, u32[]{:S(2)}, u32[]{:S(2)}) collective-permute-start(bf16[8,128,512]{2,1,0:T(8,128)(2,1)} %bitcast.8), channel_id=1, source_target_pairs={{0,126},{2,4},{4,2},{6,8},{8,6},{10,12},{12,10},{14,16},{16,14},{1... | collective-permute-start | bytes 3145736 | tf_op jit(solution)/shard_map/ppermute | solution.py:32
  16.1 46.0 %copy-start.7 = (bf16[512,1024]{1,0:T(8,128)(2,1)}, bf16[512,1024]{1,0:T(8,128)(2,1)S(1)}, u32[]{:S(2)}) copy-start(bf16[512,1024]{1,0:T(8,128)(2,1)S(1)} %get-tuple-element.57.x_t) | copy-start | bytes 3145732
  16.1 7.0 %copy-start.5 = (bf16[20,128,128]{2,1,0:T(8,128)(2,1)S(1)}, bf16[20,128,128]{2,1,0:T(8,128)(2,1)}, u32[]{:S(2)}) copy-start(bf16[20,128,128]{2,1,0:T(8,128)(2,1)} %tiles.5) | copy-start | bytes 1966084
  16.2 7.0 %copy-start.11 = (bf16[512,1024]{1,0:T(8,128)(2,1)S(1)}, bf16[512,1024]{1,0:T(8,128)(2,1)}, u32[]{:S(2)}) copy-start(bf16[512,1024]{1,0:T(8,128)(2,1)} %w_self.3) | copy-start | bytes 3145732
  16.2 6.9 %copy-start.16 = (s32[1,20]{1,0:T(1,128)S(1)}, s32[1,20]{1,0:T(1,128)}, u32[]{:S(2)}) copy-start(s32[1,20]{1,0:T(1,128)} %row.7) | copy-start | bytes 244
  16.2 6.9 %copy-start.17 = (s32[1,20]{1,0:T(1,128)S(1)}, s32[1,20]{1,0:T(1,128)}, u32[]{:S(2)}) copy-start(s32[1,20]{1,0:T(1,128)} %col.7) | copy-start | bytes 244
  16.2 6.9 %copy-start.18 = (s32[1,20]{1,0:T(1,128)S(1)}, s32[1,20]{1,0:T(1,128)}, u32[]{:S(2)}) copy-start(s32[1,20]{1,0:T(1,128)} %tile.7) | copy-start | bytes 244
  16.2 6.9 %copy-start.19 = (s32[1,5]{1,0:T(1,128)S(1)}, s32[1,5]{1,0:T(1,128)}, u32[]{:S(2)}) copy-start(s32[1,5]{1,0:T(1,128)} %count.7) | copy-start | bytes 64
  17.6 12.3 %collective-permute-start.4 = (bf16[4,128,512]{2,1,0:T(8,128)(2,1)S(1)}, bf16[4,128,512]{2,1,0:T(8,128)(2,1)S(1)}, u32[]{:S(2)}, u32[]{:S(2)}) collective-permute-start(bf16[4,128,512]{2,1,0:T(8,128)(2,1)S(1)} %shard_map.140), channel_id=1, source_target_pairs={{0,4},{2,126},{4,8},{6,2},{8,12},{10,6},{12,16},{14,10},{16,20},{1... | collective-permute-start | bytes 1572872 | tf_op jit(solution)/shard_map/ppermute | solution.py:32
  28.3 3.5 %collective-permute-start.3 = (bf16[8,128,512]{2,1,0:T(8,128)(2,1)S(1)}, bf16[8,128,512]{2,1,0:T(8,128)(2,1)S(1)}, u32[]{:S(2)}, u32[]{:S(2)}) collective-permute-start(bf16[8,128,512]{2,1,0:T(8,128)(2,1)S(1)} %shard_map.139.outer), channel_id=1, source_target_pairs={{0,2},{2,0},{1,3},{3,1},{4,6},{6,4},{5,7},{7,5},{8,10},{10,8},{9,1... | collective-permute-start | bytes 3145736 | tf_op jit(solution)/shard_map/ppermute | solution.py:38
  33.9 12.8 %collective-permute-start.6 = (bf16[1024,256]{1,0:T(8,128)(2,1)S(1)}, bf16[1024,256]{1,0:T(8,128)(2,1)S(1)}, u32[]{:S(2)}, u32[]{:S(2)}) collective-permute-start(bf16[1024,256]{1,0:T(8,128)(2,1)S(1)} %get-tuple-element.49), channel_id=1, source_target_pairs={{0,1},{1,0},{2,3},{3,2},{4,5},{5,4},{6,7},{7,6},{8,9},{9,8},{10,11... | collective-permute-start | bytes 1572872 | tf_op jit(solution)/shard_map/ppermute | solution.py:38
  36.4 21.5 %collective-permute-start.5 = (bf16[1024,256]{1,0:T(8,128)(2,1)S(1)}, bf16[1024,256]{1,0:T(8,128)(2,1)S(1)}, u32[]{:S(2)}, u32[]{:S(2)}) collective-permute-start(bf16[1024,256]{1,0:T(8,128)(2,1)S(1)} %get-tuple-element.48), channel_id=1, source_target_pairs={{0,1},{1,0},{2,3},{3,2},{4,5},{5,4},{6,7},{7,6},{8,9},{9,8},{10,11... | collective-permute-start | bytes 1572872 | tf_op jit(solution)/shard_map/ppermute | solution.py:38
  36.9 9.7 %copy-start.6 = (bf16[1024,512]{1,0:T(8,128)(2,1)S(1)}, bf16[1024,512]{1,0:T(8,128)(2,1)}, u32[]{:S(2)}) copy-start(bf16[1024,512]{1,0:T(8,128)(2,1)} %cot.3) | copy-start | bytes 3145732
  38.3 23.9 %copy-start.8 = (bf16[512,1024]{1,0:T(8,128)(2,1)}, bf16[512,1024]{1,0:T(8,128)(2,1)S(1)}, u32[]{:S(2)}) copy-start(bf16[512,1024]{1,0:T(8,128)(2,1)S(1)} %get-tuple-element.56.agg_t) | copy-start | bytes 3145732
  59.7 10.5 %copy-start = (bf16[1024,512]{1,0:T(8,128)(2,1)}, bf16[1024,512]{1,0:T(8,128)(2,1)S(1)}, u32[]{:S(2)}) copy-start(bf16[1024,512]{1,0:T(8,128)(2,1)S(1)} %get-tuple-element.53.d.own) | copy-start | bytes 3145732
  59.7 23.1 %collective-permute-start.7 = (bf16[1024,512]{1,0:T(8,128)(2,1)S(1)}, bf16[1024,512]{1,0:T(8,128)(2,1)S(1)}, u32[]{:S(2)}, u32[]{:S(2)}) collective-permute-start(bf16[1024,512]{1,0:T(8,128)(2,1)S(1)} %get-tuple-element.53.d.own), channel_id=1, source_target_pairs={{0,1},{1,0},{2,3},{3,2},{4,5},{5,4},{6,7},{7,6},{8,9},{9,8},{10,11... | collective-permute-start | bytes 3145736 | tf_op jit(solution)/shard_map/ppermute | solution.py:38
  63.6 5.1 %collective-permute-start.8 = (bf16[512,512]{1,0:T(8,128)(2,1)S(1)}, bf16[512,512]{1,0:T(8,128)(2,1)S(1)}, u32[]{:S(2)}, u32[]{:S(2)}) collective-permute-start(bf16[512,512]{1,0:T(8,128)(2,1)S(1)} %get-tuple-element.59), channel_id=1, source_target_pairs={{0,2},{2,0},{1,3},{3,1},{4,6},{6,4},{5,7},{7,5},{8,10},{10,8},{9,1... | collective-permute-start | bytes 1572872 | tf_op jit(solution)/shard_map/ppermute | solution.py:38
  67.1 1.5 %collective-permute-start.10 = (f32[8,256]{1,0:T(8,128)S(1)}, f32[8,256]{1,0:T(8,128)S(1)}, u32[]{:S(2)}, u32[]{:S(2)}) collective-permute-start(f32[8,256]{1,0:T(8,128)S(1)} %get-tuple-element.61.rest_1_), channel_id=1, source_target_pairs={{0,2},{2,0},{1,3},{3,1},{4,6},{6,4},{5,7},{7,5},{8,10},{10,8},{9,1... | collective-permute-start | bytes 24584 | tf_op jit(solution)/shard_map/ppermute | solution.py:38
  67.2 1.5 collective-permute-start.9
  70.2 16.4 %all-to-all-start = ((bf16[16,40,512]{2,1,0:T(8,128)(2,1)}), bf16[16,40,512]{2,1,0:T(8,128)(2,1)}, u32[]{:S(2)}, u32[]{:S(2)}) async-start(bf16[16,40,512]{2,1,0:T(8,128)(2,1)} %shard_map.148), calls=%async_computation | async-start | bytes 1310720 | tf_op jit(solution)/shard_map/all_to_all | solution.py:426
  74.5 12.1 %copy-start.9 = (bf16[512,1024]{1,0:T(8,128)(2,1)S(1)}, bf16[512,1024]{1,0:T(8,128)(2,1)}, u32[]{:S(2)}) copy-start(bf16[512,1024]{1,0:T(8,128)(2,1)} %copy-done.8) | copy-start | bytes 3145732
  89.6 3.4 %collective-permute-start.11 = (bf16[512,512]{1,0:T(8,128)(2,1)S(1)}, bf16[512,512]{1,0:T(8,128)(2,1)S(1)}, u32[]{:S(2)}, u32[]{:S(2)}) collective-permute-start(bf16[512,512]{1,0:T(8,128)(2,1)S(1)} %get-tuple-element.63), channel_id=1, source_target_pairs={{0,2},{2,0},{1,3},{3,1},{4,6},{6,4},{5,7},{7,5},{8,10},{10,8},{9,1... | collective-permute-start | bytes 1572872 | tf_op jit(solution)/shard_map/ppermute | solution.py:38
  91.5 28.8 %collective-permute-start.16 = (f32[40,512]{1,0:T(8,128)S(1)}, f32[40,512]{1,0:T(8,128)S(1)}, u32[]{:S(2)}, u32[]{:S(2)}) collective-permute-start(f32[40,512]{1,0:T(8,128)S(1)} %get-tuple-element.71.refs_0_), channel_id=1, source_target_pairs={{0,64},{64,0},{1,65},{65,1},{2,66},{66,2},{3,67},{67,3},{4,68},{68... | collective-permute-start | bytes 245768 | tf_op jit(solution)/shard_map/ppermute | solution.py:38
  94.4 25.9 %all-to-all-start.1 = ((bf16[32,16,512]{2,1,0:T(8,128)(2,1)}), bf16[32,16,512]{2,1,0:T(8,128)(2,1)S(1)}, u32[]{:S(2)}, u32[]{:S(2)}) async-start(bf16[32,16,512]{2,1,0:T(8,128)(2,1)} %shard_map.150.after), calls=%async_computation.1 | async-start | bytes 1048576 | tf_op jit(solution)/shard_map/all_to_all | solution.py:447
  107.5 23.3 %collective-permute-start.12 = (bf16[528,512]{1,0:T(8,128)(2,1)}, bf16[528,512]{1,0:T(8,128)(2,1)S(1)}, u32[]{:S(2)}, u32[]{:S(2)}) collective-permute-start(bf16[528,512]{1,0:T(8,128)(2,1)} %get-tuple-element.66), channel_id=1, source_target_pairs={{0,4},{2,126},{4,8},{6,2},{8,12},{10,6},{12,16},{14,10},{16,20},{1... | collective-permute-start | bytes 1622024 | tf_op jit(solution)/shard_map/ppermute | solution.py:32
  114.2 16.6 %collective-permute-start.13 = (bf16[528,512]{1,0:T(8,128)(2,1)}, bf16[528,512]{1,0:T(8,128)(2,1)S(1)}, u32[]{:S(2)}, u32[]{:S(2)}) collective-permute-start(bf16[528,512]{1,0:T(8,128)(2,1)} %get-tuple-element.67), channel_id=1, source_target_pairs={{0,124},{2,6},{4,0},{6,10},{8,4},{10,14},{12,8},{14,18},{16,12},{1... | collective-permute-start | bytes 1622024 | tf_op jit(solution)/shard_map/ppermute | solution.py:32
  114.2 18.7 %collective-permute-start.14 = (bf16[528,512]{1,0:T(8,128)(2,1)}, bf16[528,512]{1,0:T(8,128)(2,1)S(1)}, u32[]{:S(2)}, u32[]{:S(2)}) collective-permute-start(bf16[528,512]{1,0:T(8,128)(2,1)} %get-tuple-element.68), channel_id=1, source_target_pairs={{0,126},{2,4},{4,2},{6,8},{8,6},{10,12},{12,10},{14,16},{16,14},{1... | collective-permute-start | bytes 1622024 | tf_op jit(solution)/shard_map/ppermute | solution.py:32
  114.2 18.7 %collective-permute-start.15 = (bf16[528,512]{1,0:T(8,128)(2,1)}, bf16[528,512]{1,0:T(8,128)(2,1)S(1)}, u32[]{:S(2)}, u32[]{:S(2)}) collective-permute-start(bf16[528,512]{1,0:T(8,128)(2,1)} %get-tuple-element.69), channel_id=1, source_target_pairs={{0,2},{2,0},{1,3},{3,1},{4,6},{6,4},{5,7},{7,5},{8,10},{10,8},{9,1... | collective-permute-start | bytes 1622024 | tf_op jit(solution)/shard_map/ppermute | solution.py:38
  121.5 24.8 %all-to-all-start.2 = ((bf16[32,32,512]{2,1,0:T(8,128)(2,1)}), bf16[32,32,512]{2,1,0:T(8,128)(2,1)S(1)}, u32[]{:S(2)}, u32[]{:S(2)}) async-start(bf16[32,32,512]{2,1,0:T(8,128)(2,1)} %get-tuple-element.72), calls=%async_computation.2 | async-start | bytes 2097152 | tf_op jit(solution)/shard_map/all_to_all | solution.py:510
  146.9 2.7 %collective-permute-start.17 = (bf16[32,32,512]{2,1,0:T(8,128)(2,1)S(1)}, bf16[32,32,512]{2,1,0:T(8,128)(2,1)S(1)}, u32[]{:S(2)}, u32[]{:S(2)}) collective-permute-start(bf16[32,32,512]{2,1,0:T(8,128)(2,1)S(1)} %shard_map.156.far_mine), channel_id=1, source_target_pairs={{0,2},{2,0},{1,3},{3,1},{4,6},{6,4},{5,7},{7,5},{8,10},{10,8},{9,1... | collective-permute-start | bytes 3145736 | tf_op jit(solution)/shard_map/ppermute | solution.py:38
  (15 other events, 26.4 us)

commit v5 on v4

--- a/solution.py
+++ b/solution.py
@@ -20,6 +20,7 @@
 MIB = 1 << 20
 ROLES = ((4, 0), (0, 4), (1, 3), (3, 1))
 TALL = 256
+SPLIT = (384, 128)
 LONG = 20000000000
 
 
@@ -110,15 +111,17 @@
                 acc[row[0, j]] += dot(tiles[tile[0, j]], block)
 
     rows = acc.shape[0] * BLOCK // 2
-    half = send0.shape[1]
     agg[...] = acc[...].astype(BF).reshape(agg.shape)
-    other = (1 - lax.axis_index("f")) * (2 * half)
-    for c, send in enumerate((send0, send1)):
-        cols = pl.ds(pl.multiple_of(other + c * half, 128), half)
-        span = slice(c * half, (c + 1) * half)
+    start = 0
+    other = (1 - lax.axis_index("f")) * agg.shape[1]
+    for send in (send0, send1):
+        count_of = send.shape[1]
+        cols = pl.ds(pl.multiple_of(other + start, 128), count_of)
+        span = slice(start, start + count_of)
         for r in range(2):
             at = slice(r * rows, (r + 1) * rows)
             send[at, :] = (dot(agg[at, :], w_neigh[:, cols]) + part[at, span]).astype(BF)
+        start += count_of
 
 
 def own_kernel(agg, own0, w_neigh, out, agg_t):
@@ -173,10 +176,12 @@
     out[:, :piece, :] = both.reshape(pieces, piece, width)
     if tall > piece:
         s0, s1, g0, g1 = rest[:-1]
-        half = s0.shape[1]
-        for c, (s, g) in enumerate(((s0, g0), (s1, g1))):
+        start = 0
+        for s, g in ((s0, g0), (s1, g1)):
             rows = bias_rows(jnp.concatenate([s[...], g[...]], axis=0))
-            out[:, piece:, c * half : (c + 1) * half] = jnp.broadcast_to(rows[None], (pieces, 8, half))
+            end = start + rows.shape[1]
+            out[:, piece:, start:end] = jnp.broadcast_to(rows[None], (pieces, *rows.shape))
+            start = end
 
 
 def spread_kernel(scale, a, b, moved, out, bias):
@@ -331,7 +336,6 @@
 def on_device(node_feats, edge_tiles, slot_row, slot_col, slot_tile, slot_count, w_self, w_neigh, bias, cotangent):
     nodes, width = node_feats.shape
     blocks = nodes // BLOCK
-    half = width // 2
     scale = float(nodes * lax.axis_size(NODE)) ** (-0.5)
     x = node_feats.reshape(blocks, BLOCK, width)
 
@@ -372,7 +376,7 @@
     passed = swap(outer, "c")
     aggregate, send0, send1 = run(
         aggregate_kernel,
-        [shape((nodes, width), BF)] + [shape((nodes, half), BF)] * 2,
+        [shape((nodes, width), BF)] + [shape((nodes, n), BF) for n in SPLIT],
         [SMEM] * 4 + [VMEM] * 7,
         scratch=[pltpu.VMEM((blocks, BLOCK, width), F32)],
         vmem=20,
@@ -391,15 +395,17 @@
     hidden, delta = None, None
     sums = []
     for c in range(2):
-        column = pl.BlockSpec((TALL, half), lambda i, c=c: (i, c))
-        alone = pl.BlockSpec((TALL, half), lambda i: (i, 0))
+        narrow = SPLIT[c]
+        rows = (1 + c) * TALL
+        column = pl.BlockSpec((rows, narrow), lambda i, at=c * SPLIT[0] // narrow: (i, at))
+        alone = pl.BlockSpec((rows, narrow), lambda i: (i, 0))
         extra = [hidden, delta] if c else []
         hidden, delta, total = run(
             act_kernel,
-            [shape((nodes, width), BF), shape((nodes, width), BF), shape((8, half), F32)],
+            [shape((nodes, width), BF), shape((nodes, width), BF), shape((8, narrow), F32)],
             [column, alone, column] + [ANY] * len(extra),
-            [column, column, pl.BlockSpec((8, half), lambda i: (0, 0))],
-            grid=(nodes // TALL,),
+            [column, column, pl.BlockSpec((8, narrow), lambda i: (0, 0))],
+            grid=(nodes // rows,),
             input_output_aliases={3: 0, 4: 1} if c else {},
         )(own, recv[c], cotangent, *extra)
         sums.append(total)
@@ -413,13 +419,13 @@
     pair = [shape((width, width), BF), shape((width, width), F32)]
     send, keep = run(weight_kernel, pair, [strip, strip, full], [out, out], grid=(2,))(agg_t, x_t, delta)
     got, *got_sums = [swap(v, "c") for v in (send, *sums)]
-    steps = 4
+    steps = 2
     part = pl.BlockSpec((width // steps, width), lambda i: (i, 0))
-    small = pl.BlockSpec((8, half), lambda i: (0, 0))
+    small = [pl.BlockSpec((8, n), lambda i: (0, 0)) for n in SPLIT]
     parts = run(
         join_kernel,
         shape((plane, piece + 8, width), BF),
-        [part, part] + [small] * 4,
+        [part, part] + small * 2,
         pl.BlockSpec((plane // steps, piece + 8, width), lambda i: (i, 0, 0)),
         grid=(steps,),
     )(keep, got, *sums, *got_sums)
@@ -493,15 +499,16 @@
         ],
         grid=(2,),
     )(own_total, own_got, far_parts)
-    column = pl.BlockSpec((blocks, BLOCK, BLOCK), lambda i: (0, 0, i))
-    narrow = pl.BlockSpec((tall_term, BLOCK), lambda i: (0, i))
+    lanes = 2 * BLOCK
+    column = pl.BlockSpec((blocks, BLOCK, lanes), lambda i: (0, 0, i))
+    narrow = pl.BlockSpec((tall_term, lanes), lambda i: (0, i))
     grad_nodes, token = run(
         place_kernel,
         [shape((blocks, BLOCK, width), BF), mark],
         [column] + [narrow] * 4,
         [column, pl.BlockSpec(mark.shape, lambda i: (0, 0))],
-        [pltpu.VMEM((blocks, BLOCK, BLOCK), F32), pltpu.SMEM((4, PAIR_MAX), jnp.int32)],
-        grid=(width // BLOCK,),
+        [pltpu.VMEM((blocks, BLOCK, lanes), F32), pltpu.SMEM((4, PAIR_MAX), jnp.int32)],
+        grid=(width // lanes,),
         vmem=56,
         flops=9*10**9,
     )(base, *returned)

time: 155 us -> 151 us (0.974)
  starting transfers between devices: 56.1 us -> 53.3 us
    ppermute x6, waiting for transfers between devices: 5.55 us -> 7.67 us  [mirror(): lax.ppermute(block, NODE, [(i, (i + (distance if i % 2 == 0 else -distanc...]
    ppermute x6, starting transfers between devices: 14.4 us -> 12.6 us  [mirror(): lax.ppermute(block, NODE, [(i, (i + (distance if i % 2 == 0 else -distanc...]
    all_to_all x1, waiting for transfers between devices: 7.21 us -> 5.64 us  [on_device(): mine = after(lax.all_to_all(spread, CHIPS, 0, 0), token)]
where the time goes in v5:
time: 151 us; the launch traced here: 149 us
  starting transfers between devices  53.3 us (35%)
  waiting for transfers between devices  48.9 us (32%)
  Pallas kernels  36.9 us (24%)
  local copies, waits for them, and re-layouts  8.89 us (6%)
    ppermute x12, waiting for transfers between devices, swap(): return lax.ppermute(block, axis, [(0, 1), (1, 0)])  33.5 us
    ppermute x12, starting transfers between devices, swap(): return lax.ppermute(block, axis, [(0, 1), (1, 0)])  25.6 us
    ppermute x6, starting transfers between devices, mirror(): lax.ppermute(block, NODE, [(i, (i + (distance if i % 2 == 0 else -distanc...  12.6 us
    unnamed x52, local copies, waits for them, and re-layouts  8.89 us
    ppermute x6, waiting for transfers between devices, mirror(): lax.ppermute(block, NODE, [(i, (i + (distance if i % 2 == 0 else -distanc...  7.67 us
    all_to_all x1, starting transfers between devices, on_device(): far_parts = lax.all_to_all(parts, CHIPS, 0, 0)  6.76 us
    pallas_call x1, Pallas kernels, on_device(): run(outward_kernel, [shape((tall_term, width), BF)] * 4 + [shape((blocks,...  6.16 us
    all_to_all x1, waiting for transfers between devices, on_device(): mine = after(lax.all_to_all(spread, CHIPS, 0, 0), token)  5.64 us
  transfers between devices with their start and end apart: 21, of which 13 were waited for; matrix products, arithmetic and copies ran while one was open for 0% of the time, Pallas kernels for 19%

profile of v5, /device:TPU:1, one launch (start us, length us, event | category | flops | bytes accessed | tf_op | source)
XLA Modules:
  0.0 148.9 jit_solution(11215822975550471148)
XLA Ops:
  0.6 2.2 %collective-permute-start.2 = (s32[1,20]{1,0:T(1,128)}, s32[1,20]{1,0:T(1,128)S(1)}, u32[]{:S(2)}, u32[]{:S(2)}) collective-permute-start(s32[1,20]{1,0:T(1,128)} %col.7), channel_id=1, source_target_pairs={{0,124},{2,6},{4,0},{6,10},{8,4},{10,14},{12,8},{14,18},{16,12},{1... | collective-permute-start | bytes 248 | tf_op jit(solution)/shard_map/ppermute | solution.py:33
  2.8 6.8 %collective-permute-start.1 = (bf16[8,128,512]{2,1,0:T(8,128)(2,1)}, bf16[8,128,512]{2,1,0:T(8,128)(2,1)S(1)}, u32[]{:S(2)}, u32[]{:S(2)}) collective-permute-start(bf16[8,128,512]{2,1,0:T(8,128)(2,1)} %bitcast.7), channel_id=1, source_target_pairs={{0,2},{2,0},{1,3},{3,1},{4,6},{6,4},{5,7},{7,5},{8,10},{10,8},{9,1... | collective-permute-start | bytes 3145736 | tf_op jit(solution)/shard_map/ppermute | solution.py:39
  14.5 1.6 %shard_map.137 = (bf16[512,1024]{1,0:T(8,128)(2,1)S(1)}, bf16[1024,512]{1,0:T(8,128)(2,1)S(1)}, bf16[1024,512]{1,0:T(8,128)(2,1)S(1)}, bf16[20,128,128]{2,1,0:T(8,128)(2,1)S(1)}, f32[8,128]{1,0:T(8,128)S(1)}) custom-call(s32[1,20]{1,0:T(1,128)S(1)} %collective-permute-done.2.wanted, bf16[1024,512]{1,0:T(8,128)(2,1)S(1)} %copy-done.11, ...), custom_call_target="tpu_custom_call" | custom-call | flops 10000 | bytes 10000 | tf_op jit(solution)/shard_map/pallas_call | solution.py:347
  17.6 5.5 %collective-permute-start.4 = (bf16[4,128,512]{2,1,0:T(8,128)(2,1)S(1)}, bf16[4,128,512]{2,1,0:T(8,128)(2,1)S(1)}, u32[]{:S(2)}, u32[]{:S(2)}) collective-permute-start(bf16[4,128,512]{2,1,0:T(8,128)(2,1)S(1)} %shard_map.140), channel_id=1, source_target_pairs={{0,4},{2,126},{4,8},{6,2},{8,12},{10,6},{12,16},{14,10},{16,20},{1... | collective-permute-start | bytes 1572872 | tf_op jit(solution)/shard_map/ppermute | solution.py:33
  23.2 2.6 %shard_map.138 = (f32[8,128,512]{2,1,0:T(8,128)S(1)}, f32[1024,512]{1,0:T(8,128)S(1)}, f32[1024,512]{1,0:T(8,128)S(1)}, f32[8,128]{1,0:T(8,128)S(1)}) custom-call(s32[1,20]{1,0:T(1,128)S(1)} %copy-done.16, s32[1,20]{1,0:T(1,128)S(1)} %copy-done.17, s32[1,20]{1,0:T(1,128)S(1)} %copy-done.18, s32[1,5]{1,0:T(1,128)S(1)} %copy-done.19, ...), custom_call_target="tpu_custom_call" | custom-call | flops 10000 | bytes 10000 | tf_op jit(solution)/shard_map/pallas_call | solution.py:356
  25.7 2.6 %collective-permute-done.array = bf16[8,128,512]{2,1,0:T(8,128)(2,1)S(1)} collective-permute-done((bf16[8,128,512]{2,1,0:T(8,128)(2,1)}, bf16[8,128,512]{2,1,0:T(8,128)(2,1)S(1)}, u32[]{:S(2)}, u32[]{:S(2)}) %collective-permute-start) | collective-permute-done | bytes 1048608 | tf_op jit(solution)/shard_map/ppermute | solution.py:33
  30.0 1.9 %collective-permute-done.3.passed = bf16[8,128,512]{2,1,0:T(8,128)(2,1)S(1)} collective-permute-done((bf16[8,128,512]{2,1,0:T(8,128)(2,1)S(1)}, bf16[8,128,512]{2,1,0:T(8,128)(2,1)S(1)}, u32[]{:S(2)}, u32[]{:S(2)}) %collective-permute-start.3) | collective-permute-done | bytes 1048608 | tf_op jit(solution)/shard_map/ppermute | solution.py:39
  31.8 2.8 %shard_map.142 = (bf16[1024,512]{1,0:T(8,128)(2,1)S(1)}, bf16[1024,384]{1,0:T(8,128)(2,1)S(1)}, bf16[1024,128]{1,0:T(8,128)(2,1)S(1)}) custom-call(s32[1,20]{1,0:T(1,128)S(1)} %copy-done.16, s32[1,20]{1,0:T(1,128)S(1)} %copy-done.17, s32[1,20]{1,0:T(1,128)S(1)} %copy-done.18, s32[1,5]{1,0:T(1,128)S(1)} %copy-done.19, ...), custom_call_target="tpu_custom_call" | custom-call | flops 10000 | bytes 10000 | tf_op jit(solution)/shard_map/pallas_call | solution.py:377
  34.6 2.5 %collective-permute-start.6 = (bf16[1024,384]{1,0:T(8,128)(2,1)S(1)}, bf16[1024,384]{1,0:T(8,128)(2,1)S(1)}, u32[]{:S(2)}, u32[]{:S(2)}) collective-permute-start(bf16[1024,384]{1,0:T(8,128)(2,1)S(1)} %get-tuple-element.49), channel_id=1, source_target_pairs={{0,1},{1,0},{2,3},{3,2},{4,5},{5,4},{6,7},{7,6},{8,9},{9,8},{10,11... | collective-permute-start | bytes 2359304 | tf_op jit(solution)/shard_map/ppermute | solution.py:39
  39.1 14.1 %collective-permute-done.6.recv = bf16[1024,384]{1,0:T(8,128)(2,1)S(1)} collective-permute-done((bf16[1024,384]{1,0:T(8,128)(2,1)S(1)}, bf16[1024,384]{1,0:T(8,128)(2,1)S(1)}, u32[]{:S(2)}, u32[]{:S(2)}) %collective-permute-start.6) | collective-permute-done | bytes 786464 | tf_op jit(solution)/shard_map/ppermute | solution.py:39
  53.2 2.2 %shard_map.144 = (bf16[1024,512]{1,0:T(8,128)(2,1)}, bf16[1024,512]{1,0:T(8,128)(2,1)S(1)}, f32[8,384]{1,0:T(8,128)S(1)}) custom-call(f32[1024,512]{1,0:T(8,128)S(1)} %get-tuple-element.47.own, bf16[1024,384]{1,0:T(8,128)(2,1)S(1)} %collective-permute-done.6.recv, bf16[1024,512]{1,0:T(8,128)(2,1)S(1)} %copy-done.12), custom_call_target="tpu_custom_call" | custom-call | flops 10000 | bytes 10000 | tf_op jit(solution)/shard_map/pallas_call | solution.py:403
  55.4 3.4 %collective-permute-done.5.recv = bf16[1024,128]{1,0:T(8,128)(2,1)S(1)} collective-permute-done((bf16[1024,128]{1,0:T(8,128)(2,1)S(1)}, bf16[1024,128]{1,0:T(8,128)(2,1)S(1)}, u32[]{:S(2)}, u32[]{:S(2)}) %collective-permute-start.5) | collective-permute-done | bytes 262176 | tf_op jit(solution)/shard_map/ppermute | solution.py:39
  59.9 2.4 %collective-permute-start.7 = (bf16[1024,512]{1,0:T(8,128)(2,1)S(1)}, bf16[1024,512]{1,0:T(8,128)(2,1)S(1)}, u32[]{:S(2)}, u32[]{:S(2)}) collective-permute-start(bf16[1024,512]{1,0:T(8,128)(2,1)S(1)} %get-tuple-element.53.d.own), channel_id=1, source_target_pairs={{0,1},{1,0},{2,3},{3,2},{4,5},{5,4},{6,7},{7,6},{8,9},{9,8},{10,11... | collective-permute-start | bytes 3145736 | tf_op jit(solution)/shard_map/ppermute | solution.py:39
  62.4 1.4 shard_map.147
  63.8 3.4 %collective-permute-start.8 = (bf16[512,512]{1,0:T(8,128)(2,1)S(1)}, bf16[512,512]{1,0:T(8,128)(2,1)S(1)}, u32[]{:S(2)}, u32[]{:S(2)}) collective-permute-start(bf16[512,512]{1,0:T(8,128)(2,1)S(1)} %get-tuple-element.59), channel_id=1, source_target_pairs={{0,2},{2,0},{1,3},{3,1},{4,6},{6,4},{5,7},{7,5},{8,10},{10,8},{9,1... | collective-permute-start | bytes 1572872 | tf_op jit(solution)/shard_map/ppermute | solution.py:39
  69.7 4.3 %all-to-all-start = ((bf16[16,40,512]{2,1,0:T(8,128)(2,1)}), bf16[16,40,512]{2,1,0:T(8,128)(2,1)}, u32[]{:S(2)}, u32[]{:S(2)}) async-start(bf16[16,40,512]{2,1,0:T(8,128)(2,1)} %shard_map.148), calls=%async_computation | async-start | bytes 1310720 | tf_op jit(solution)/shard_map/all_to_all | solution.py:432
  74.0 9.2 %collective-permute-done.7.array = bf16[1024,512]{1,0:T(8,128)(2,1)S(1)} collective-permute-done((bf16[1024,512]{1,0:T(8,128)(2,1)S(1)}, bf16[1024,512]{1,0:T(8,128)(2,1)S(1)}, u32[]{:S(2)}, u32[]{:S(2)}) %collective-permute-start.7) | collective-permute-done | bytes 1048608 | tf_op jit(solution)/shard_map/ppermute | solution.py:39
  84.2 2.0 %all-to-all-done.moved = bf16[16,40,512]{2,1,0:T(8,128)(2,1)} async-done(((bf16[16,40,512]{2,1,0:T(8,128)(2,1)}), bf16[16,40,512]{2,1,0:T(8,128)(2,1)}, u32[]{:S(2)}, u32[]{:S(2)}) %all-to-all-start) | async-done | bytes 655392 | tf_op jit(solution)/shard_map/all_to_all | solution.py:432
  86.2 3.0 %shard_map.149 = (bf16[512,512]{1,0:T(8,128)(2,1)S(1)}, f32[512,512]{1,0:T(8,128)S(1)}, f32[40,512]{1,0:T(8,128)S(1)}) custom-call(bf16[512,1024]{1,0:T(8,128)(2,1)S(1)} %copy-done.8, bf16[512,1024]{1,0:T(8,128)(2,1)} %copy-done.6, bf16[1024,512]{1,0:T(8,128)(2,1)} %copy-done.3, bf16[16,40,512]{2,1,0:T(8,128)(2,1)} %all-to-all-done.moved), custom_call_target="tpu_custom_call" | custom-call | flops 10000 | bytes 10000 | tf_op jit(solution)/shard_map/pallas_call | solution.py:436
  89.2 1.9 %collective-permute-start.11 = (bf16[512,512]{1,0:T(8,128)(2,1)S(1)}, bf16[512,512]{1,0:T(8,128)(2,1)S(1)}, u32[]{:S(2)}, u32[]{:S(2)}) collective-permute-start(bf16[512,512]{1,0:T(8,128)(2,1)S(1)} %get-tuple-element.63), channel_id=1, source_target_pairs={{0,2},{2,0},{1,3},{3,1},{4,6},{6,4},{5,7},{7,5},{8,10},{10,8},{9,1... | collective-permute-start | bytes 1572872 | tf_op jit(solution)/shard_map/ppermute | solution.py:39
  91.1 1.5 %collective-permute-done.11.got = bf16[512,512]{1,0:T(8,128)(2,1)S(1)} collective-permute-done((bf16[512,512]{1,0:T(8,128)(2,1)S(1)}, bf16[512,512]{1,0:T(8,128)(2,1)S(1)}, u32[]{:S(2)}, u32[]{:S(2)}) %collective-permute-start.11) | collective-permute-done | bytes 524320 | tf_op jit(solution)/shard_map/ppermute | solution.py:39
  93.5 6.8 %all-to-all-start.1 = ((bf16[32,16,512]{2,1,0:T(8,128)(2,1)}), bf16[32,16,512]{2,1,0:T(8,128)(2,1)S(1)}, u32[]{:S(2)}, u32[]{:S(2)}) async-start(bf16[32,16,512]{2,1,0:T(8,128)(2,1)} %shard_map.150.after), calls=%async_computation.1 | async-start | bytes 1048576 | tf_op jit(solution)/shard_map/all_to_all | solution.py:453
  100.2 6.2 %shard_map.151 = (bf16[528,512]{1,0:T(8,128)(2,1)}, bf16[528,512]{1,0:T(8,128)(2,1)}, bf16[528,512]{1,0:T(8,128)(2,1)}, bf16[528,512]{1,0:T(8,128)(2,1)}, bf16[8,128,512]{2,1,0:T(8,128)(2,1)}) custom-call(s32[1,20]{1,0:T(1,128)} %row.7, s32[1,20]{1,0:T(1,128)} %col.7, s32[1,20]{1,0:T(1,128)} %tile.7, s32[1,5]{1,0:T(1,128)} %count.7, ...), custom_call_target="tpu_custom_call" | custom-call | flops 10000 | bytes 10000 | tf_op jit(solution)/shard_map/pallas_call | solution.py:456
  106.4 5.0 %collective-permute-start.12 = (bf16[528,512]{1,0:T(8,128)(2,1)}, bf16[528,512]{1,0:T(8,128)(2,1)S(1)}, u32[]{:S(2)}, u32[]{:S(2)}) collective-permute-start(bf16[528,512]{1,0:T(8,128)(2,1)} %get-tuple-element.66), channel_id=1, source_target_pairs={{0,4},{2,126},{4,8},{6,2},{8,12},{10,6},{12,16},{14,10},{16,20},{1... | collective-permute-start | bytes 1622024 | tf_op jit(solution)/shard_map/ppermute | solution.py:33
  111.4 6.1 %collective-permute-start.15 = (bf16[528,512]{1,0:T(8,128)(2,1)}, bf16[528,512]{1,0:T(8,128)(2,1)S(1)}, u32[]{:S(2)}, u32[]{:S(2)}) collective-permute-start(bf16[528,512]{1,0:T(8,128)(2,1)} %get-tuple-element.69), channel_id=1, source_target_pairs={{0,2},{2,0},{1,3},{3,1},{4,6},{6,4},{5,7},{7,5},{8,10},{10,8},{9,1... | collective-permute-start | bytes 1622024 | tf_op jit(solution)/shard_map/ppermute | solution.py:39
  118.7 3.9 %all-to-all-start.2 = ((bf16[32,32,512]{2,1,0:T(8,128)(2,1)}), bf16[32,32,512]{2,1,0:T(8,128)(2,1)S(1)}, u32[]{:S(2)}, u32[]{:S(2)}) async-start(bf16[32,32,512]{2,1,0:T(8,128)(2,1)} %get-tuple-element.72), calls=%async_computation.2 | async-start | bytes 2097152 | tf_op jit(solution)/shard_map/all_to_all | solution.py:517
  122.6 5.5 %shard_map.152.base = f32[8,128,512]{2,1,0:T(8,128)} custom-call(s32[1,20]{1,0:T(1,128)} %row.7, s32[1,20]{1,0:T(1,128)} %col.7, s32[1,20]{1,0:T(1,128)} %tile.7, s32[1,5]{1,0:T(1,128)} %count.7, bf16[1024,512]{1,0:T(8,128)(2,1)} %copy-done, bf16[1024,512]{1,0:T(8,128)(2,1)} %copy-done.3, bf16[8,128,512]{2,1,0:T(8,128)(2,1)} %get-tuple-element.64.dagg, ...), custom_call_target="tpu_custom_call" | custom-call | flops 10000 | bytes 10000 | tf_op jit(solution)/shard_map/pallas_call | solution.py:476
  128.2 4.6 %collective-permute-done.14.r2 = bf16[528,512]{1,0:T(8,128)(2,1)S(1)} collective-permute-done((bf16[528,512]{1,0:T(8,128)(2,1)}, bf16[528,512]{1,0:T(8,128)(2,1)S(1)}, u32[]{:S(2)}, u32[]{:S(2)}) %collective-permute-start.14) | collective-permute-done | bytes 540704 | tf_op jit(solution)/shard_map/ppermute | solution.py:33
  134.4 3.3 %shard_map.153 = (bf16[8,128,512]{2,1,0:T(8,128)(2,1)}, f32[8,128]{1,0:T(8,128)}) custom-call(f32[8,128,512]{2,1,0:T(8,128)} %shard_map.152.base, bf16[528,512]{1,0:T(8,128)(2,1)} %copy-done.22, bf16[528,512]{1,0:T(8,128)(2,1)} %copy-done.23, bf16[528,512]{1,0:T(8,128)(2,1)} %copy-done.24, bf16[528,512]{1,0:T(8,128)(2,1)} %copy-done.25), custom_call_target="tpu_custom_call" | custom-call | flops 8999999488 | bytes 10000 | tf_op jit(solution)/shard_map/pallas_call | solution.py:505
  137.6 5.6 %all-to-all-done.2.array = bf16[32,32,512]{2,1,0:T(8,128)(2,1)S(1)} async-done(((bf16[32,32,512]{2,1,0:T(8,128)(2,1)}), bf16[32,32,512]{2,1,0:T(8,128)(2,1)S(1)}, u32[]{:S(2)}, u32[]{:S(2)}) %all-to-all-start.2) | async-done | bytes 1048608 | tf_op jit(solution)/shard_map/all_to_all | solution.py:517
  144.2 2.4 %collective-permute-done.17.far_swap = bf16[32,32,512]{2,1,0:T(8,128)(2,1)S(1)} collective-permute-done((bf16[32,32,512]{2,1,0:T(8,128)(2,1)S(1)}, bf16[32,32,512]{2,1,0:T(8,128)(2,1)S(1)}, u32[]{:S(2)}, u32[]{:S(2)}) %collective-permute-start.17) | collective-permute-done | bytes 1048608 | tf_op jit(solution)/shard_map/ppermute | solution.py:39
  146.6 2.3 %shard_map.157 = (f32[512,1024]{1,0:T(8,128)}, f32[512,1024]{1,0:T(8,128)}) custom-call(bf16[2,16,32,512]{3,2,1,0:T(8,128)(2,1)S(1)} %bitcast.6, bf16[2,16,32,512]{3,2,1,0:T(8,128)(2,1)S(1)} %bitcast.11, bf16[32,32,512]{2,1,0:T(8,128)(2,1)S(1)} %shard_map.156.far_mine, bf16[32,32,512]{2,1,0:T(8,128)(2,1)S(1)} %collective-permute-done.17.far_swap), custom_call_target="tpu_custom_call" | custom-call | flops 10000 | bytes 10000 | tf_op jit(solution)/shard_map/pallas_call | solution.py:525
  (83 shorter events, 19.1 us)
Async XLA Ops:
  0.6 9.1 %collective-permute-start.2 = (s32[1,20]{1,0:T(1,128)}, s32[1,20]{1,0:T(1,128)S(1)}, u32[]{:S(2)}, u32[]{:S(2)}) collective-permute-start(s32[1,20]{1,0:T(1,128)} %col.7), channel_id=1, source_target_pairs={{0,124},{2,6},{4,0},{6,10},{8,4},{10,14},{12,8},{14,18},{16,12},{1... | collective-permute-start | bytes 248 | tf_op jit(solution)/shard_map/ppermute | solution.py:33
  2.8 20.3 %collective-permute-start.1 = (bf16[8,128,512]{2,1,0:T(8,128)(2,1)}, bf16[8,128,512]{2,1,0:T(8,128)(2,1)S(1)}, u32[]{:S(2)}, u32[]{:S(2)}) collective-permute-start(bf16[8,128,512]{2,1,0:T(8,128)(2,1)} %bitcast.7), channel_id=1, source_target_pairs={{0,2},{2,0},{1,3},{3,1},{4,6},{6,4},{5,7},{7,5},{8,10},{10,8},{9,1... | collective-permute-start | bytes 3145736 | tf_op jit(solution)/shard_map/ppermute | solution.py:39
  9.6 18.7 %collective-permute-start = (bf16[8,128,512]{2,1,0:T(8,128)(2,1)}, bf16[8,128,512]{2,1,0:T(8,128)(2,1)S(1)}, u32[]{:S(2)}, u32[]{:S(2)}) collective-permute-start(bf16[8,128,512]{2,1,0:T(8,128)(2,1)} %bitcast.8), channel_id=1, source_target_pairs={{0,126},{2,4},{4,2},{6,8},{8,6},{10,12},{12,10},{14,16},{16,14},{1... | collective-permute-start | bytes 3145736 | tf_op jit(solution)/shard_map/ppermute | solution.py:33
  16.1 46.2 %copy-start.6 = (bf16[512,1024]{1,0:T(8,128)(2,1)}, bf16[512,1024]{1,0:T(8,128)(2,1)S(1)}, u32[]{:S(2)}) copy-start(bf16[512,1024]{1,0:T(8,128)(2,1)S(1)} %get-tuple-element.57.x_t) | copy-start | bytes 3145732
  16.1 7.0 %copy-start.5 = (bf16[20,128,128]{2,1,0:T(8,128)(2,1)S(1)}, bf16[20,128,128]{2,1,0:T(8,128)(2,1)}, u32[]{:S(2)}) copy-start(bf16[20,128,128]{2,1,0:T(8,128)(2,1)} %tiles.5) | copy-start | bytes 1966084
  16.2 7.0 %copy-start.10 = (bf16[512,1024]{1,0:T(8,128)(2,1)S(1)}, bf16[512,1024]{1,0:T(8,128)(2,1)}, u32[]{:S(2)}) copy-start(bf16[512,1024]{1,0:T(8,128)(2,1)} %w_self.3) | copy-start | bytes 3145732
  16.2 6.9 %copy-start.16 = (s32[1,20]{1,0:T(1,128)S(1)}, s32[1,20]{1,0:T(1,128)}, u32[]{:S(2)}) copy-start(s32[1,20]{1,0:T(1,128)} %row.7) | copy-start | bytes 244
  16.2 6.9 %copy-start.17 = (s32[1,20]{1,0:T(1,128)S(1)}, s32[1,20]{1,0:T(1,128)}, u32[]{:S(2)}) copy-start(s32[1,20]{1,0:T(1,128)} %col.7) | copy-start | bytes 244
  16.2 6.9 %copy-start.18 = (s32[1,20]{1,0:T(1,128)S(1)}, s32[1,20]{1,0:T(1,128)}, u32[]{:S(2)}) copy-start(s32[1,20]{1,0:T(1,128)} %tile.7) | copy-start | bytes 244
  16.2 6.9 %copy-start.19 = (s32[1,5]{1,0:T(1,128)S(1)}, s32[1,5]{1,0:T(1,128)}, u32[]{:S(2)}) copy-start(s32[1,5]{1,0:T(1,128)} %count.7) | copy-start | bytes 64
  17.6 12.3 %collective-permute-start.4 = (bf16[4,128,512]{2,1,0:T(8,128)(2,1)S(1)}, bf16[4,128,512]{2,1,0:T(8,128)(2,1)S(1)}, u32[]{:S(2)}, u32[]{:S(2)}) collective-permute-start(bf16[4,128,512]{2,1,0:T(8,128)(2,1)S(1)} %shard_map.140), channel_id=1, source_target_pairs={{0,4},{2,126},{4,8},{6,2},{8,12},{10,6},{12,16},{14,10},{16,20},{1... | collective-permute-start | bytes 1572872 | tf_op jit(solution)/shard_map/ppermute | solution.py:33
  28.3 3.5 %collective-permute-start.3 = (bf16[8,128,512]{2,1,0:T(8,128)(2,1)S(1)}, bf16[8,128,512]{2,1,0:T(8,128)(2,1)S(1)}, u32[]{:S(2)}, u32[]{:S(2)}) collective-permute-start(bf16[8,128,512]{2,1,0:T(8,128)(2,1)S(1)} %shard_map.139.outer), channel_id=1, source_target_pairs={{0,2},{2,0},{1,3},{3,1},{4,6},{6,4},{5,7},{7,5},{8,10},{10,8},{9,1... | collective-permute-start | bytes 3145736 | tf_op jit(solution)/shard_map/ppermute | solution.py:39
  34.6 18.5 %collective-permute-start.6 = (bf16[1024,384]{1,0:T(8,128)(2,1)S(1)}, bf16[1024,384]{1,0:T(8,128)(2,1)S(1)}, u32[]{:S(2)}, u32[]{:S(2)}) collective-permute-start(bf16[1024,384]{1,0:T(8,128)(2,1)S(1)} %get-tuple-element.49), channel_id=1, source_target_pairs={{0,1},{1,0},{2,3},{3,2},{4,5},{5,4},{6,7},{7,6},{8,9},{9,8},{10,11... | collective-permute-start | bytes 2359304 | tf_op jit(solution)/shard_map/ppermute | solution.py:39
  37.2 21.6 %collective-permute-start.5 = (bf16[1024,128]{1,0:T(8,128)(2,1)S(1)}, bf16[1024,128]{1,0:T(8,128)(2,1)S(1)}, u32[]{:S(2)}, u32[]{:S(2)}) collective-permute-start(bf16[1024,128]{1,0:T(8,128)(2,1)S(1)} %get-tuple-element.48), channel_id=1, source_target_pairs={{0,1},{1,0},{2,3},{3,2},{4,5},{5,4},{6,7},{7,6},{8,9},{9,8},{10,11... | collective-permute-start | bytes 786440 | tf_op jit(solution)/shard_map/ppermute | solution.py:39
  37.7 15.5 %copy-start.12 = (bf16[1024,512]{1,0:T(8,128)(2,1)S(1)}, bf16[1024,512]{1,0:T(8,128)(2,1)}, u32[]{:S(2)}) copy-start(bf16[1024,512]{1,0:T(8,128)(2,1)} %cot.3) | copy-start | bytes 3145732
  39.1 23.3 %copy-start.7 = (bf16[512,1024]{1,0:T(8,128)(2,1)}, bf16[512,1024]{1,0:T(8,128)(2,1)S(1)}, u32[]{:S(2)}) copy-start(bf16[512,1024]{1,0:T(8,128)(2,1)S(1)} %get-tuple-element.56.agg_t) | copy-start | bytes 3145732
  59.9 9.8 %copy-start = (bf16[1024,512]{1,0:T(8,128)(2,1)}, bf16[1024,512]{1,0:T(8,128)(2,1)S(1)}, u32[]{:S(2)}) copy-start(bf16[1024,512]{1,0:T(8,128)(2,1)S(1)} %get-tuple-element.53.d.own) | copy-start | bytes 3145732
  59.9 23.3 %collective-permute-start.7 = (bf16[1024,512]{1,0:T(8,128)(2,1)S(1)}, bf16[1024,512]{1,0:T(8,128)(2,1)S(1)}, u32[]{:S(2)}, u32[]{:S(2)}) collective-permute-start(bf16[1024,512]{1,0:T(8,128)(2,1)S(1)} %get-tuple-element.53.d.own), channel_id=1, source_target_pairs={{0,1},{1,0},{2,3},{3,2},{4,5},{5,4},{6,7},{7,6},{8,9},{9,8},{10,11... | collective-permute-start | bytes 3145736 | tf_op jit(solution)/shard_map/ppermute | solution.py:39
  63.8 4.9 %collective-permute-start.8 = (bf16[512,512]{1,0:T(8,128)(2,1)S(1)}, bf16[512,512]{1,0:T(8,128)(2,1)S(1)}, u32[]{:S(2)}, u32[]{:S(2)}) collective-permute-start(bf16[512,512]{1,0:T(8,128)(2,1)S(1)} %get-tuple-element.59), channel_id=1, source_target_pairs={{0,2},{2,0},{1,3},{3,1},{4,6},{6,4},{5,7},{7,5},{8,10},{10,8},{9,1... | collective-permute-start | bytes 1572872 | tf_op jit(solution)/shard_map/ppermute | solution.py:39
  67.2 1.6 %collective-permute-start.9 = (f32[8,384]{1,0:T(8,128)S(1)}, f32[8,384]{1,0:T(8,128)S(1)}, u32[]{:S(2)}, u32[]{:S(2)}) collective-permute-start(f32[8,384]{1,0:T(8,128)S(1)} %get-tuple-element.60.rest_0_), channel_id=1, source_target_pairs={{0,2},{2,0},{1,3},{3,1},{4,6},{6,4},{5,7},{7,5},{8,10},{10,8},{9,1... | collective-permute-start | bytes 36872 | tf_op jit(solution)/shard_map/ppermute | solution.py:39
  67.3 1.5 collective-permute-start.10
  69.7 16.5 %all-to-all-start = ((bf16[16,40,512]{2,1,0:T(8,128)(2,1)}), bf16[16,40,512]{2,1,0:T(8,128)(2,1)}, u32[]{:S(2)}, u32[]{:S(2)}) async-start(bf16[16,40,512]{2,1,0:T(8,128)(2,1)} %shard_map.148), calls=%async_computation | async-start | bytes 1310720 | tf_op jit(solution)/shard_map/all_to_all | solution.py:432
  74.0 12.2 %copy-start.8 = (bf16[512,1024]{1,0:T(8,128)(2,1)S(1)}, bf16[512,1024]{1,0:T(8,128)(2,1)}, u32[]{:S(2)}) copy-start(bf16[512,1024]{1,0:T(8,128)(2,1)} %copy-done.7) | copy-start | bytes 3145732
  89.2 3.4 %collective-permute-start.11 = (bf16[512,512]{1,0:T(8,128)(2,1)S(1)}, bf16[512,512]{1,0:T(8,128)(2,1)S(1)}, u32[]{:S(2)}, u32[]{:S(2)}) collective-permute-start(bf16[512,512]{1,0:T(8,128)(2,1)S(1)} %get-tuple-element.63), channel_id=1, source_target_pairs={{0,2},{2,0},{1,3},{3,1},{4,6},{6,4},{5,7},{7,5},{8,10},{10,8},{9,1... | collective-permute-start | bytes 1572872 | tf_op jit(solution)/shard_map/ppermute | solution.py:39
  91.1 26.4 %collective-permute-start.16 = (f32[40,512]{1,0:T(8,128)S(1)}, f32[40,512]{1,0:T(8,128)S(1)}, u32[]{:S(2)}, u32[]{:S(2)}) collective-permute-start(f32[40,512]{1,0:T(8,128)S(1)} %get-tuple-element.71.refs_0_), channel_id=1, source_target_pairs={{0,64},{64,0},{1,65},{65,1},{2,66},{66,2},{3,67},{67,3},{4,68},{68... | collective-permute-start | bytes 245768 | tf_op jit(solution)/shard_map/ppermute | solution.py:39
  93.5 24.0 %all-to-all-start.1 = ((bf16[32,16,512]{2,1,0:T(8,128)(2,1)}), bf16[32,16,512]{2,1,0:T(8,128)(2,1)S(1)}, u32[]{:S(2)}, u32[]{:S(2)}) async-start(bf16[32,16,512]{2,1,0:T(8,128)(2,1)} %shard_map.150.after), calls=%async_computation.1 | async-start | bytes 1048576 | tf_op jit(solution)/shard_map/all_to_all | solution.py:453
  106.4 21.7 %collective-permute-start.12 = (bf16[528,512]{1,0:T(8,128)(2,1)}, bf16[528,512]{1,0:T(8,128)(2,1)S(1)}, u32[]{:S(2)}, u32[]{:S(2)}) collective-permute-start(bf16[528,512]{1,0:T(8,128)(2,1)} %get-tuple-element.66), channel_id=1, source_target_pairs={{0,4},{2,126},{4,8},{6,2},{8,12},{10,6},{12,16},{14,10},{16,20},{1... | collective-permute-start | bytes 1622024 | tf_op jit(solution)/shard_map/ppermute | solution.py:33
  111.4 16.8 %collective-permute-start.13 = (bf16[528,512]{1,0:T(8,128)(2,1)}, bf16[528,512]{1,0:T(8,128)(2,1)S(1)}, u32[]{:S(2)}, u32[]{:S(2)}) collective-permute-start(bf16[528,512]{1,0:T(8,128)(2,1)} %get-tuple-element.67), channel_id=1, source_target_pairs={{0,124},{2,6},{4,0},{6,10},{8,4},{10,14},{12,8},{14,18},{16,12},{1... | collective-permute-start | bytes 1622024 | tf_op jit(solution)/shard_map/ppermute | solution.py:33
  111.4 21.4 %collective-permute-start.14 = (bf16[528,512]{1,0:T(8,128)(2,1)}, bf16[528,512]{1,0:T(8,128)(2,1)S(1)}, u32[]{:S(2)}, u32[]{:S(2)}) collective-permute-start(bf16[528,512]{1,0:T(8,128)(2,1)} %get-tuple-element.68), channel_id=1, source_target_pairs={{0,126},{2,4},{4,2},{6,8},{8,6},{10,12},{12,10},{14,16},{16,14},{1... | collective-permute-start | bytes 1622024 | tf_op jit(solution)/shard_map/ppermute | solution.py:33
  111.4 21.4 %collective-permute-start.15 = (bf16[528,512]{1,0:T(8,128)(2,1)}, bf16[528,512]{1,0:T(8,128)(2,1)S(1)}, u32[]{:S(2)}, u32[]{:S(2)}) collective-permute-start(bf16[528,512]{1,0:T(8,128)(2,1)} %get-tuple-element.69), channel_id=1, source_target_pairs={{0,2},{2,0},{1,3},{3,1},{4,6},{6,4},{5,7},{7,5},{8,10},{10,8},{9,1... | collective-permute-start | bytes 1622024 | tf_op jit(solution)/shard_map/ppermute | solution.py:39
  118.7 24.6 %all-to-all-start.2 = ((bf16[32,32,512]{2,1,0:T(8,128)(2,1)}), bf16[32,32,512]{2,1,0:T(8,128)(2,1)S(1)}, u32[]{:S(2)}, u32[]{:S(2)}) async-start(bf16[32,32,512]{2,1,0:T(8,128)(2,1)} %get-tuple-element.72), calls=%async_computation.2 | async-start | bytes 2097152 | tf_op jit(solution)/shard_map/all_to_all | solution.py:517
  143.9 2.7 %collective-permute-start.17 = (bf16[32,32,512]{2,1,0:T(8,128)(2,1)S(1)}, bf16[32,32,512]{2,1,0:T(8,128)(2,1)S(1)}, u32[]{:S(2)}, u32[]{:S(2)}) collective-permute-start(bf16[32,32,512]{2,1,0:T(8,128)(2,1)S(1)} %shard_map.156.far_mine), channel_id=1, source_target_pairs={{0,2},{2,0},{1,3},{3,1},{4,6},{6,4},{5,7},{7,5},{8,10},{10,8},{9,1... | collective-permute-start | bytes 3145736 | tf_op jit(solution)/shard_map/ppermute | solution.py:39
  (15 other events, 31.3 us)

commit v6 on v5

--- a/solution.py
+++ b/solution.py
@@ -20,7 +20,7 @@
 MIB = 1 << 20
 ROLES = ((4, 0), (0, 4), (1, 3), (3, 1))
 TALL = 256
-SPLIT = (384, 128)
+SPLIT = (256, 256)
 LONG = 20000000000
 
 
@@ -492,12 +492,7 @@
     spread, grad_bias = run(
         lambda *refs: spread_kernel(scale, *refs),
         [shape((chips, piece, width), BF), shape((1, width), F32)],
-        [summed, summed, pl.BlockSpec((chips, width // chips, width // 2), lambda i: (0, 0, i))],
-        [
-            pl.BlockSpec((chips, piece, width // 2), lambda i: (0, 0, i)),
-            pl.BlockSpec((1, width // 2), lambda i: (0, i)),
-        ],
-        grid=(2,),
+        [VMEM] * 3,
     )(own_total, own_got, far_parts)
     lanes = 2 * BLOCK
     column = pl.BlockSpec((blocks, BLOCK, lanes), lambda i: (0, 0, i))

time: 151 us -> 151 us (level)
    ppermute x6, waiting for transfers between devices: 7.67 us -> 3.92 us  [mirror(): lax.ppermute(block, NODE, [(i, (i + (distance if i % 2 == 0 else -distanc...]
    ppermute x12, waiting for transfers between devices: 33.5 us -> 36.4 us  [swap(): return lax.ppermute(block, axis, [(0, 1), (1, 0)])]
    all_to_all x1, waiting for transfers between devices: 5.64 us -> 8.21 us  [on_device(): mine = after(lax.all_to_all(spread, CHIPS, 0, 0), token)]
where the time goes in v6:
time: 151 us; the launch traced here: 150 us
  starting transfers between devices  52.7 us (35%)
  waiting for transfers between devices  49 us (32%)
  Pallas kernels  38 us (25%)
  local copies, waits for them, and re-layouts  8.89 us (6%)
    ppermute x12, waiting for transfers between devices, swap(): return lax.ppermute(block, axis, [(0, 1), (1, 0)])  36.4 us
    ppermute x12, starting transfers between devices, swap(): return lax.ppermute(block, axis, [(0, 1), (1, 0)])  25.5 us
    ppermute x6, starting transfers between devices, mirror(): lax.ppermute(block, NODE, [(i, (i + (distance if i % 2 == 0 else -distanc...  13.4 us
    unnamed x52, local copies, waits for them, and re-layouts  8.89 us
    all_to_all x1, waiting for transfers between devices, on_device(): mine = after(lax.all_to_all(spread, CHIPS, 0, 0), token)  8.21 us
    pallas_call x1, Pallas kernels, on_device(): run(outward_kernel, [shape((tall_term, width), BF)] * 4 + [shape((blocks,...  6.65 us
    pallas_call x1, Pallas kernels, on_device(): run(base_kernel, shape((blocks, BLOCK, width), F32), [SMEM] * 4 + [ANY] *...  5.69 us
    all_to_all x1, starting transfers between devices, on_device(): far_parts = lax.all_to_all(parts, CHIPS, 0, 0)  5.59 us
  transfers between devices with their start and end apart: 21, of which 13 were waited for; matrix products, arithmetic and copies ran while one was open for 0% of the time, Pallas kernels for 19%

profile of v6, /device:TPU:1, one launch (start us, length us, event | category | flops | bytes accessed | tf_op | source)
XLA Modules:
  0.0 149.6 jit_solution(17194763331997898222)
XLA Ops:
  0.6 2.2 %collective-permute-start.2 = (s32[1,20]{1,0:T(1,128)}, s32[1,20]{1,0:T(1,128)S(1)}, u32[]{:S(2)}, u32[]{:S(2)}) collective-permute-start(s32[1,20]{1,0:T(1,128)} %col.7), channel_id=1, source_target_pairs={{0,124},{2,6},{4,0},{6,10},{8,4},{10,14},{12,8},{14,18},{16,12},{1... | collective-permute-start | bytes 248 | tf_op jit(solution)/shard_map/ppermute | solution.py:33
  2.8 6.8 %collective-permute-start.1 = (bf16[8,128,512]{2,1,0:T(8,128)(2,1)}, bf16[8,128,512]{2,1,0:T(8,128)(2,1)S(1)}, u32[]{:S(2)}, u32[]{:S(2)}) collective-permute-start(bf16[8,128,512]{2,1,0:T(8,128)(2,1)} %bitcast.7), channel_id=1, source_target_pairs={{0,2},{2,0},{1,3},{3,1},{4,6},{6,4},{5,7},{7,5},{8,10},{10,8},{9,1... | collective-permute-start | bytes 3145736 | tf_op jit(solution)/shard_map/ppermute | solution.py:39
  14.5 1.6 %shard_map.137 = (bf16[512,1024]{1,0:T(8,128)(2,1)S(1)}, bf16[1024,512]{1,0:T(8,128)(2,1)S(1)}, bf16[1024,512]{1,0:T(8,128)(2,1)S(1)}, bf16[20,128,128]{2,1,0:T(8,128)(2,1)S(1)}, f32[8,128]{1,0:T(8,128)S(1)}) custom-call(s32[1,20]{1,0:T(1,128)S(1)} %collective-permute-done.2.wanted, bf16[1024,512]{1,0:T(8,128)(2,1)S(1)} %copy-done.12, ...), custom_call_target="tpu_custom_call" | custom-call | flops 10000 | bytes 10000 | tf_op jit(solution)/shard_map/pallas_call | solution.py:347
  17.6 5.5 %collective-permute-start.4 = (bf16[4,128,512]{2,1,0:T(8,128)(2,1)S(1)}, bf16[4,128,512]{2,1,0:T(8,128)(2,1)S(1)}, u32[]{:S(2)}, u32[]{:S(2)}) collective-permute-start(bf16[4,128,512]{2,1,0:T(8,128)(2,1)S(1)} %shard_map.140), channel_id=1, source_target_pairs={{0,4},{2,126},{4,8},{6,2},{8,12},{10,6},{12,16},{14,10},{16,20},{1... | collective-permute-start | bytes 1572872 | tf_op jit(solution)/shard_map/ppermute | solution.py:33
  23.2 2.9 %shard_map.138 = (f32[8,128,512]{2,1,0:T(8,128)S(1)}, f32[1024,512]{1,0:T(8,128)S(1)}, f32[1024,512]{1,0:T(8,128)S(1)}, f32[8,128]{1,0:T(8,128)S(1)}) custom-call(s32[1,20]{1,0:T(1,128)S(1)} %copy-done.16, s32[1,20]{1,0:T(1,128)S(1)} %copy-done.17, s32[1,20]{1,0:T(1,128)S(1)} %copy-done.18, s32[1,5]{1,0:T(1,128)S(1)} %copy-done.19, ...), custom_call_target="tpu_custom_call" | custom-call | flops 10000 | bytes 10000 | tf_op jit(solution)/shard_map/pallas_call | solution.py:356
  26.1 2.2 %collective-permute-done.array = bf16[8,128,512]{2,1,0:T(8,128)(2,1)S(1)} collective-permute-done((bf16[8,128,512]{2,1,0:T(8,128)(2,1)}, bf16[8,128,512]{2,1,0:T(8,128)(2,1)S(1)}, u32[]{:S(2)}, u32[]{:S(2)}) %collective-permute-start) | collective-permute-done | bytes 1048608 | tf_op jit(solution)/shard_map/ppermute | solution.py:33
  30.0 1.9 %collective-permute-done.3.passed = bf16[8,128,512]{2,1,0:T(8,128)(2,1)S(1)} collective-permute-done((bf16[8,128,512]{2,1,0:T(8,128)(2,1)S(1)}, bf16[8,128,512]{2,1,0:T(8,128)(2,1)S(1)}, u32[]{:S(2)}, u32[]{:S(2)}) %collective-permute-start.3) | collective-permute-done | bytes 1048608 | tf_op jit(solution)/shard_map/ppermute | solution.py:39
  31.8 2.9 %shard_map.142 = (bf16[1024,512]{1,0:T(8,128)(2,1)S(1)}, bf16[1024,256]{1,0:T(8,128)(2,1)S(1)}, bf16[1024,256]{1,0:T(8,128)(2,1)S(1)}) custom-call(s32[1,20]{1,0:T(1,128)S(1)} %copy-done.16, s32[1,20]{1,0:T(1,128)S(1)} %copy-done.17, s32[1,20]{1,0:T(1,128)S(1)} %copy-done.18, s32[1,5]{1,0:T(1,128)S(1)} %copy-done.19, ...), custom_call_target="tpu_custom_call" | custom-call | flops 10000 | bytes 10000 | tf_op jit(solution)/shard_map/pallas_call | solution.py:377
  34.7 2.5 %collective-permute-start.6 = (bf16[1024,256]{1,0:T(8,128)(2,1)S(1)}, bf16[1024,256]{1,0:T(8,128)(2,1)S(1)}, u32[]{:S(2)}, u32[]{:S(2)}) collective-permute-start(bf16[1024,256]{1,0:T(8,128)(2,1)S(1)} %get-tuple-element.49), channel_id=1, source_target_pairs={{0,1},{1,0},{2,3},{3,2},{4,5},{5,4},{6,7},{7,6},{8,9},{9,8},{10,11... | collective-permute-start | bytes 1572872 | tf_op jit(solution)/shard_map/ppermute | solution.py:39
  37.8 1.4 shard_map.143
  39.1 9.3 %collective-permute-done.6.recv = bf16[1024,256]{1,0:T(8,128)(2,1)S(1)} collective-permute-done((bf16[1024,256]{1,0:T(8,128)(2,1)S(1)}, bf16[1024,256]{1,0:T(8,128)(2,1)S(1)}, u32[]{:S(2)}, u32[]{:S(2)}) %collective-permute-start.6) | collective-permute-done | bytes 524320 | tf_op jit(solution)/shard_map/ppermute | solution.py:39
  48.5 1.9 %shard_map.144 = (bf16[1024,512]{1,0:T(8,128)(2,1)}, bf16[1024,512]{1,0:T(8,128)(2,1)S(1)}, f32[8,256]{1,0:T(8,128)S(1)}) custom-call(f32[1024,512]{1,0:T(8,128)S(1)} %get-tuple-element.47.own, bf16[1024,256]{1,0:T(8,128)(2,1)S(1)} %collective-permute-done.6.recv, bf16[1024,512]{1,0:T(8,128)(2,1)S(1)} %copy-done.6), custom_call_target="tpu_custom_call" | custom-call | flops 10000 | bytes 10000 | tf_op jit(solution)/shard_map/pallas_call | solution.py:403
  50.3 9.4 %collective-permute-done.5.recv = bf16[1024,256]{1,0:T(8,128)(2,1)S(1)} collective-permute-done((bf16[1024,256]{1,0:T(8,128)(2,1)S(1)}, bf16[1024,256]{1,0:T(8,128)(2,1)S(1)}, u32[]{:S(2)}, u32[]{:S(2)}) %collective-permute-start.5) | collective-permute-done | bytes 524320 | tf_op jit(solution)/shard_map/ppermute | solution.py:39
  59.7 1.4 shard_map.145
  61.1 2.4 %collective-permute-start.7 = (bf16[1024,512]{1,0:T(8,128)(2,1)S(1)}, bf16[1024,512]{1,0:T(8,128)(2,1)S(1)}, u32[]{:S(2)}, u32[]{:S(2)}) collective-permute-start(bf16[1024,512]{1,0:T(8,128)(2,1)S(1)} %get-tuple-element.53.d.own), channel_id=1, source_target_pairs={{0,1},{1,0},{2,3},{3,2},{4,5},{5,4},{6,7},{7,6},{8,9},{9,8},{10,11... | collective-permute-start | bytes 3145736 | tf_op jit(solution)/shard_map/ppermute | solution.py:39
  63.6 1.4 shard_map.147
  65.0 2.5 %collective-permute-start.8 = (bf16[512,512]{1,0:T(8,128)(2,1)S(1)}, bf16[512,512]{1,0:T(8,128)(2,1)S(1)}, u32[]{:S(2)}, u32[]{:S(2)}) collective-permute-start(bf16[512,512]{1,0:T(8,128)(2,1)S(1)} %get-tuple-element.59), channel_id=1, source_target_pairs={{0,2},{2,0},{1,3},{3,1},{4,6},{6,4},{5,7},{7,5},{8,10},{10,8},{9,1... | collective-permute-start | bytes 1572872 | tf_op jit(solution)/shard_map/ppermute | solution.py:39
  70.1 4.3 %all-to-all-start = ((bf16[16,40,512]{2,1,0:T(8,128)(2,1)}), bf16[16,40,512]{2,1,0:T(8,128)(2,1)}, u32[]{:S(2)}, u32[]{:S(2)}) async-start(bf16[16,40,512]{2,1,0:T(8,128)(2,1)} %shard_map.148), calls=%async_computation | async-start | bytes 1310720 | tf_op jit(solution)/shard_map/all_to_all | solution.py:432
  74.3 10.9 %collective-permute-done.7.array = bf16[1024,512]{1,0:T(8,128)(2,1)S(1)} collective-permute-done((bf16[1024,512]{1,0:T(8,128)(2,1)S(1)}, bf16[1024,512]{1,0:T(8,128)(2,1)S(1)}, u32[]{:S(2)}, u32[]{:S(2)}) %collective-permute-start.7) | collective-permute-done | bytes 1048608 | tf_op jit(solution)/shard_map/ppermute | solution.py:39
  86.7 3.0 %shard_map.149 = (bf16[512,512]{1,0:T(8,128)(2,1)S(1)}, f32[512,512]{1,0:T(8,128)S(1)}, f32[40,512]{1,0:T(8,128)S(1)}) custom-call(bf16[512,1024]{1,0:T(8,128)(2,1)S(1)} %copy-done.9, bf16[512,1024]{1,0:T(8,128)(2,1)} %copy-done.7, bf16[1024,512]{1,0:T(8,128)(2,1)} %copy-done.3, bf16[16,40,512]{2,1,0:T(8,128)(2,1)} %all-to-all-done.moved), custom_call_target="tpu_custom_call" | custom-call | flops 10000 | bytes 10000 | tf_op jit(solution)/shard_map/pallas_call | solution.py:436
  89.7 2.6 %collective-permute-start.11 = (bf16[512,512]{1,0:T(8,128)(2,1)S(1)}, bf16[512,512]{1,0:T(8,128)(2,1)S(1)}, u32[]{:S(2)}, u32[]{:S(2)}) collective-permute-start(bf16[512,512]{1,0:T(8,128)(2,1)S(1)} %get-tuple-element.63), channel_id=1, source_target_pairs={{0,2},{2,0},{1,3},{3,1},{4,6},{6,4},{5,7},{7,5},{8,10},{10,8},{9,1... | collective-permute-start | bytes 1572872 | tf_op jit(solution)/shard_map/ppermute | solution.py:39
  92.6 1.3 collective-permute-done.11.got
  94.7 5.6 %all-to-all-start.1 = ((bf16[32,16,512]{2,1,0:T(8,128)(2,1)}), bf16[32,16,512]{2,1,0:T(8,128)(2,1)S(1)}, u32[]{:S(2)}, u32[]{:S(2)}) async-start(bf16[32,16,512]{2,1,0:T(8,128)(2,1)} %shard_map.150.after), calls=%async_computation.1 | async-start | bytes 1048576 | tf_op jit(solution)/shard_map/all_to_all | solution.py:453
  100.3 6.6 %shard_map.151 = (bf16[528,512]{1,0:T(8,128)(2,1)}, bf16[528,512]{1,0:T(8,128)(2,1)}, bf16[528,512]{1,0:T(8,128)(2,1)}, bf16[528,512]{1,0:T(8,128)(2,1)}, bf16[8,128,512]{2,1,0:T(8,128)(2,1)}) custom-call(s32[1,20]{1,0:T(1,128)} %row.7, s32[1,20]{1,0:T(1,128)} %col.7, s32[1,20]{1,0:T(1,128)} %tile.7, s32[1,5]{1,0:T(1,128)} %count.7, ...), custom_call_target="tpu_custom_call" | custom-call | flops 10000 | bytes 10000 | tf_op jit(solution)/shard_map/pallas_call | solution.py:456
  106.9 5.8 %collective-permute-start.12 = (bf16[528,512]{1,0:T(8,128)(2,1)}, bf16[528,512]{1,0:T(8,128)(2,1)S(1)}, u32[]{:S(2)}, u32[]{:S(2)}) collective-permute-start(bf16[528,512]{1,0:T(8,128)(2,1)} %get-tuple-element.66), channel_id=1, source_target_pairs={{0,4},{2,126},{4,8},{6,2},{8,12},{10,6},{12,16},{14,10},{16,20},{1... | collective-permute-start | bytes 1622024 | tf_op jit(solution)/shard_map/ppermute | solution.py:33
  112.7 6.1 %collective-permute-start.15 = (bf16[528,512]{1,0:T(8,128)(2,1)}, bf16[528,512]{1,0:T(8,128)(2,1)S(1)}, u32[]{:S(2)}, u32[]{:S(2)}) collective-permute-start(bf16[528,512]{1,0:T(8,128)(2,1)} %get-tuple-element.69), channel_id=1, source_target_pairs={{0,2},{2,0},{1,3},{3,1},{4,6},{6,4},{5,7},{7,5},{8,10},{10,8},{9,1... | collective-permute-start | bytes 1622024 | tf_op jit(solution)/shard_map/ppermute | solution.py:39
  120.0 3.9 %all-to-all-start.2 = ((bf16[32,32,512]{2,1,0:T(8,128)(2,1)}), bf16[32,32,512]{2,1,0:T(8,128)(2,1)S(1)}, u32[]{:S(2)}, u32[]{:S(2)}) async-start(bf16[32,32,512]{2,1,0:T(8,128)(2,1)} %get-tuple-element.72), calls=%async_computation.2 | async-start | bytes 2097152 | tf_op jit(solution)/shard_map/all_to_all | solution.py:512
  123.9 5.7 %shard_map.152.base = f32[8,128,512]{2,1,0:T(8,128)} custom-call(s32[1,20]{1,0:T(1,128)} %row.7, s32[1,20]{1,0:T(1,128)} %col.7, s32[1,20]{1,0:T(1,128)} %tile.7, s32[1,5]{1,0:T(1,128)} %count.7, bf16[1024,512]{1,0:T(8,128)(2,1)} %copy-done, bf16[1024,512]{1,0:T(8,128)(2,1)} %copy-done.3, bf16[8,128,512]{2,1,0:T(8,128)(2,1)} %get-tuple-element.64.dagg, ...), custom_call_target="tpu_custom_call" | custom-call | flops 10000 | bytes 10000 | tf_op jit(solution)/shard_map/pallas_call | solution.py:476
  132.4 3.3 %shard_map.153 = (bf16[8,128,512]{2,1,0:T(8,128)(2,1)}, f32[8,128]{1,0:T(8,128)}) custom-call(f32[8,128,512]{2,1,0:T(8,128)} %shard_map.152.base, bf16[528,512]{1,0:T(8,128)(2,1)} %copy-done.22, bf16[528,512]{1,0:T(8,128)(2,1)} %copy-done.23, bf16[528,512]{1,0:T(8,128)(2,1)} %copy-done.24, bf16[528,512]{1,0:T(8,128)(2,1)} %copy-done.25), custom_call_target="tpu_custom_call" | custom-call | flops 8999999488 | bytes 10000 | tf_op jit(solution)/shard_map/pallas_call | solution.py:500
  135.7 8.2 %all-to-all-done.2.array = bf16[32,32,512]{2,1,0:T(8,128)(2,1)S(1)} async-done(((bf16[32,32,512]{2,1,0:T(8,128)(2,1)}), bf16[32,32,512]{2,1,0:T(8,128)(2,1)S(1)}, u32[]{:S(2)}, u32[]{:S(2)}) %all-to-all-start.2) | async-done | bytes 1048608 | tf_op jit(solution)/shard_map/all_to_all | solution.py:512
  144.7 2.6 %collective-permute-done.17.far_swap = bf16[32,32,512]{2,1,0:T(8,128)(2,1)S(1)} collective-permute-done((bf16[32,32,512]{2,1,0:T(8,128)(2,1)S(1)}, bf16[32,32,512]{2,1,0:T(8,128)(2,1)S(1)}, u32[]{:S(2)}, u32[]{:S(2)}) %collective-permute-start.17) | collective-permute-done | bytes 1048608 | tf_op jit(solution)/shard_map/ppermute | solution.py:39
  147.3 2.3 %shard_map.157 = (f32[512,1024]{1,0:T(8,128)}, f32[512,1024]{1,0:T(8,128)}) custom-call(bf16[2,16,32,512]{3,2,1,0:T(8,128)(2,1)S(1)} %bitcast.6, bf16[2,16,32,512]{3,2,1,0:T(8,128)(2,1)S(1)} %bitcast.11, bf16[32,32,512]{2,1,0:T(8,128)(2,1)S(1)} %shard_map.156.far_mine, bf16[32,32,512]{2,1,0:T(8,128)(2,1)S(1)} %collective-permute-done.17.far_swap), custom_call_target="tpu_custom_call" | custom-call | flops 10000 | bytes 10000 | tf_op jit(solution)/shard_map/pallas_call | solution.py:520
  (83 shorter events, 18.4 us)
Async XLA Ops:
  0.6 9.1 %collective-permute-start.2 = (s32[1,20]{1,0:T(1,128)}, s32[1,20]{1,0:T(1,128)S(1)}, u32[]{:S(2)}, u32[]{:S(2)}) collective-permute-start(s32[1,20]{1,0:T(1,128)} %col.7), channel_id=1, source_target_pairs={{0,124},{2,6},{4,0},{6,10},{8,4},{10,14},{12,8},{14,18},{16,12},{1... | collective-permute-start | bytes 248 | tf_op jit(solution)/shard_map/ppermute | solution.py:33
  2.8 20.3 %collective-permute-start.1 = (bf16[8,128,512]{2,1,0:T(8,128)(2,1)}, bf16[8,128,512]{2,1,0:T(8,128)(2,1)S(1)}, u32[]{:S(2)}, u32[]{:S(2)}) collective-permute-start(bf16[8,128,512]{2,1,0:T(8,128)(2,1)} %bitcast.7), channel_id=1, source_target_pairs={{0,2},{2,0},{1,3},{3,1},{4,6},{6,4},{5,7},{7,5},{8,10},{10,8},{9,1... | collective-permute-start | bytes 3145736 | tf_op jit(solution)/shard_map/ppermute | solution.py:39
  9.6 18.7 %collective-permute-start = (bf16[8,128,512]{2,1,0:T(8,128)(2,1)}, bf16[8,128,512]{2,1,0:T(8,128)(2,1)S(1)}, u32[]{:S(2)}, u32[]{:S(2)}) collective-permute-start(bf16[8,128,512]{2,1,0:T(8,128)(2,1)} %bitcast.8), channel_id=1, source_target_pairs={{0,126},{2,4},{4,2},{6,8},{8,6},{10,12},{12,10},{14,16},{16,14},{1... | collective-permute-start | bytes 3145736 | tf_op jit(solution)/shard_map/ppermute | solution.py:33
  16.1 47.4 %copy-start.7 = (bf16[512,1024]{1,0:T(8,128)(2,1)}, bf16[512,1024]{1,0:T(8,128)(2,1)S(1)}, u32[]{:S(2)}) copy-start(bf16[512,1024]{1,0:T(8,128)(2,1)S(1)} %get-tuple-element.57.x_t) | copy-start | bytes 3145732
  16.1 7.0 %copy-start.5 = (bf16[20,128,128]{2,1,0:T(8,128)(2,1)S(1)}, bf16[20,128,128]{2,1,0:T(8,128)(2,1)}, u32[]{:S(2)}) copy-start(bf16[20,128,128]{2,1,0:T(8,128)(2,1)} %tiles.5) | copy-start | bytes 1966084
  16.2 7.0 %copy-start.11 = (bf16[512,1024]{1,0:T(8,128)(2,1)S(1)}, bf16[512,1024]{1,0:T(8,128)(2,1)}, u32[]{:S(2)}) copy-start(bf16[512,1024]{1,0:T(8,128)(2,1)} %w_self.3) | copy-start | bytes 3145732
  16.2 6.9 %copy-start.16 = (s32[1,20]{1,0:T(1,128)S(1)}, s32[1,20]{1,0:T(1,128)}, u32[]{:S(2)}) copy-start(s32[1,20]{1,0:T(1,128)} %row.7) | copy-start | bytes 244
  16.2 6.9 %copy-start.17 = (s32[1,20]{1,0:T(1,128)S(1)}, s32[1,20]{1,0:T(1,128)}, u32[]{:S(2)}) copy-start(s32[1,20]{1,0:T(1,128)} %col.7) | copy-start | bytes 244
  16.2 6.9 %copy-start.18 = (s32[1,20]{1,0:T(1,128)S(1)}, s32[1,20]{1,0:T(1,128)}, u32[]{:S(2)}) copy-start(s32[1,20]{1,0:T(1,128)} %tile.7) | copy-start | bytes 244
  16.2 6.9 %copy-start.19 = (s32[1,5]{1,0:T(1,128)S(1)}, s32[1,5]{1,0:T(1,128)}, u32[]{:S(2)}) copy-start(s32[1,5]{1,0:T(1,128)} %count.7) | copy-start | bytes 64
  17.6 12.3 %collective-permute-start.4 = (bf16[4,128,512]{2,1,0:T(8,128)(2,1)S(1)}, bf16[4,128,512]{2,1,0:T(8,128)(2,1)S(1)}, u32[]{:S(2)}, u32[]{:S(2)}) collective-permute-start(bf16[4,128,512]{2,1,0:T(8,128)(2,1)S(1)} %shard_map.140), channel_id=1, source_target_pairs={{0,4},{2,126},{4,8},{6,2},{8,12},{10,6},{12,16},{14,10},{16,20},{1... | collective-permute-start | bytes 1572872 | tf_op jit(solution)/shard_map/ppermute | solution.py:33
  28.3 3.5 %collective-permute-start.3 = (bf16[8,128,512]{2,1,0:T(8,128)(2,1)S(1)}, bf16[8,128,512]{2,1,0:T(8,128)(2,1)S(1)}, u32[]{:S(2)}, u32[]{:S(2)}) collective-permute-start(bf16[8,128,512]{2,1,0:T(8,128)(2,1)S(1)} %shard_map.139.outer), channel_id=1, source_target_pairs={{0,2},{2,0},{1,3},{3,1},{4,6},{6,4},{5,7},{7,5},{8,10},{10,8},{9,1... | collective-permute-start | bytes 3145736 | tf_op jit(solution)/shard_map/ppermute | solution.py:39
  34.7 13.8 %collective-permute-start.6 = (bf16[1024,256]{1,0:T(8,128)(2,1)S(1)}, bf16[1024,256]{1,0:T(8,128)(2,1)S(1)}, u32[]{:S(2)}, u32[]{:S(2)}) collective-permute-start(bf16[1024,256]{1,0:T(8,128)(2,1)S(1)} %get-tuple-element.49), channel_id=1, source_target_pairs={{0,1},{1,0},{2,3},{3,2},{4,5},{5,4},{6,7},{7,6},{8,9},{9,8},{10,11... | collective-permute-start | bytes 1572872 | tf_op jit(solution)/shard_map/ppermute | solution.py:39
  37.2 22.5 %collective-permute-start.5 = (bf16[1024,256]{1,0:T(8,128)(2,1)S(1)}, bf16[1024,256]{1,0:T(8,128)(2,1)S(1)}, u32[]{:S(2)}, u32[]{:S(2)}) collective-permute-start(bf16[1024,256]{1,0:T(8,128)(2,1)S(1)} %get-tuple-element.48), channel_id=1, source_target_pairs={{0,1},{1,0},{2,3},{3,2},{4,5},{5,4},{6,7},{7,6},{8,9},{9,8},{10,11... | collective-permute-start | bytes 1572872 | tf_op jit(solution)/shard_map/ppermute | solution.py:39
  37.8 10.7 %copy-start.6 = (bf16[1024,512]{1,0:T(8,128)(2,1)S(1)}, bf16[1024,512]{1,0:T(8,128)(2,1)}, u32[]{:S(2)}) copy-start(bf16[1024,512]{1,0:T(8,128)(2,1)} %cot.3) | copy-start | bytes 3145732
  39.1 24.4 %copy-start.8 = (bf16[512,1024]{1,0:T(8,128)(2,1)}, bf16[512,1024]{1,0:T(8,128)(2,1)S(1)}, u32[]{:S(2)}) copy-start(bf16[512,1024]{1,0:T(8,128)(2,1)S(1)} %get-tuple-element.56.agg_t) | copy-start | bytes 3145732
  61.1 8.9 %copy-start = (bf16[1024,512]{1,0:T(8,128)(2,1)}, bf16[1024,512]{1,0:T(8,128)(2,1)S(1)}, u32[]{:S(2)}) copy-start(bf16[1024,512]{1,0:T(8,128)(2,1)S(1)} %get-tuple-element.53.d.own) | copy-start | bytes 3145732
  61.1 24.1 %collective-permute-start.7 = (bf16[1024,512]{1,0:T(8,128)(2,1)S(1)}, bf16[1024,512]{1,0:T(8,128)(2,1)S(1)}, u32[]{:S(2)}, u32[]{:S(2)}) collective-permute-start(bf16[1024,512]{1,0:T(8,128)(2,1)S(1)} %get-tuple-element.53.d.own), channel_id=1, source_target_pairs={{0,1},{1,0},{2,3},{3,2},{4,5},{5,4},{6,7},{7,6},{8,9},{9,8},{10,11... | collective-permute-start | bytes 3145736 | tf_op jit(solution)/shard_map/ppermute | solution.py:39
  65.0 4.1 %collective-permute-start.8 = (bf16[512,512]{1,0:T(8,128)(2,1)S(1)}, bf16[512,512]{1,0:T(8,128)(2,1)S(1)}, u32[]{:S(2)}, u32[]{:S(2)}) collective-permute-start(bf16[512,512]{1,0:T(8,128)(2,1)S(1)} %get-tuple-element.59), channel_id=1, source_target_pairs={{0,2},{2,0},{1,3},{3,1},{4,6},{6,4},{5,7},{7,5},{8,10},{10,8},{9,1... | collective-permute-start | bytes 1572872 | tf_op jit(solution)/shard_map/ppermute | solution.py:39
  67.6 1.5 %collective-permute-start.10 = (f32[8,256]{1,0:T(8,128)S(1)}, f32[8,256]{1,0:T(8,128)S(1)}, u32[]{:S(2)}, u32[]{:S(2)}) collective-permute-start(f32[8,256]{1,0:T(8,128)S(1)} %get-tuple-element.61.rest_1_), channel_id=1, source_target_pairs={{0,2},{2,0},{1,3},{3,1},{4,6},{6,4},{5,7},{7,5},{8,10},{10,8},{9,1... | collective-permute-start | bytes 24584 | tf_op jit(solution)/shard_map/ppermute | solution.py:39
  67.6 1.5 collective-permute-start.9
  70.1 16.7 %all-to-all-start = ((bf16[16,40,512]{2,1,0:T(8,128)(2,1)}), bf16[16,40,512]{2,1,0:T(8,128)(2,1)}, u32[]{:S(2)}, u32[]{:S(2)}) async-start(bf16[16,40,512]{2,1,0:T(8,128)(2,1)} %shard_map.148), calls=%async_computation | async-start | bytes 1310720 | tf_op jit(solution)/shard_map/all_to_all | solution.py:432
  74.3 12.4 %copy-start.9 = (bf16[512,1024]{1,0:T(8,128)(2,1)S(1)}, bf16[512,1024]{1,0:T(8,128)(2,1)}, u32[]{:S(2)}) copy-start(bf16[512,1024]{1,0:T(8,128)(2,1)} %copy-done.8) | copy-start | bytes 3145732
  89.7 4.1 %collective-permute-start.11 = (bf16[512,512]{1,0:T(8,128)(2,1)S(1)}, bf16[512,512]{1,0:T(8,128)(2,1)S(1)}, u32[]{:S(2)}, u32[]{:S(2)}) collective-permute-start(bf16[512,512]{1,0:T(8,128)(2,1)S(1)} %get-tuple-element.63), channel_id=1, source_target_pairs={{0,2},{2,0},{1,3},{3,1},{4,6},{6,4},{5,7},{7,5},{8,10},{10,8},{9,1... | collective-permute-start | bytes 1572872 | tf_op jit(solution)/shard_map/ppermute | solution.py:39
  92.3 26.5 %collective-permute-start.16 = (f32[40,512]{1,0:T(8,128)S(1)}, f32[40,512]{1,0:T(8,128)S(1)}, u32[]{:S(2)}, u32[]{:S(2)}) collective-permute-start(f32[40,512]{1,0:T(8,128)S(1)} %get-tuple-element.71.refs_0_), channel_id=1, source_target_pairs={{0,64},{64,0},{1,65},{65,1},{2,66},{66,2},{3,67},{67,3},{4,68},{68... | collective-permute-start | bytes 245768 | tf_op jit(solution)/shard_map/ppermute | solution.py:39
  94.7 24.1 %all-to-all-start.1 = ((bf16[32,16,512]{2,1,0:T(8,128)(2,1)}), bf16[32,16,512]{2,1,0:T(8,128)(2,1)S(1)}, u32[]{:S(2)}, u32[]{:S(2)}) async-start(bf16[32,16,512]{2,1,0:T(8,128)(2,1)} %shard_map.150.after), calls=%async_computation.1 | async-start | bytes 1048576 | tf_op jit(solution)/shard_map/all_to_all | solution.py:453
  106.9 22.7 %collective-permute-start.12 = (bf16[528,512]{1,0:T(8,128)(2,1)}, bf16[528,512]{1,0:T(8,128)(2,1)S(1)}, u32[]{:S(2)}, u32[]{:S(2)}) collective-permute-start(bf16[528,512]{1,0:T(8,128)(2,1)} %get-tuple-element.66), channel_id=1, source_target_pairs={{0,4},{2,126},{4,8},{6,2},{8,12},{10,6},{12,16},{14,10},{16,20},{1... | collective-permute-start | bytes 1622024 | tf_op jit(solution)/shard_map/ppermute | solution.py:33
  112.7 16.9 %collective-permute-start.13 = (bf16[528,512]{1,0:T(8,128)(2,1)}, bf16[528,512]{1,0:T(8,128)(2,1)S(1)}, u32[]{:S(2)}, u32[]{:S(2)}) collective-permute-start(bf16[528,512]{1,0:T(8,128)(2,1)} %get-tuple-element.67), channel_id=1, source_target_pairs={{0,124},{2,6},{4,0},{6,10},{8,4},{10,14},{12,8},{14,18},{16,12},{1... | collective-permute-start | bytes 1622024 | tf_op jit(solution)/shard_map/ppermute | solution.py:33
  112.7 18.1 %collective-permute-start.14 = (bf16[528,512]{1,0:T(8,128)(2,1)}, bf16[528,512]{1,0:T(8,128)(2,1)S(1)}, u32[]{:S(2)}, u32[]{:S(2)}) collective-permute-start(bf16[528,512]{1,0:T(8,128)(2,1)} %get-tuple-element.68), channel_id=1, source_target_pairs={{0,126},{2,4},{4,2},{6,8},{8,6},{10,12},{12,10},{14,16},{16,14},{1... | collective-permute-start | bytes 1622024 | tf_op jit(solution)/shard_map/ppermute | solution.py:33
  112.7 18.1 %collective-permute-start.15 = (bf16[528,512]{1,0:T(8,128)(2,1)}, bf16[528,512]{1,0:T(8,128)(2,1)S(1)}, u32[]{:S(2)}, u32[]{:S(2)}) collective-permute-start(bf16[528,512]{1,0:T(8,128)(2,1)} %get-tuple-element.69), channel_id=1, source_target_pairs={{0,2},{2,0},{1,3},{3,1},{4,6},{6,4},{5,7},{7,5},{8,10},{10,8},{9,1... | collective-permute-start | bytes 1622024 | tf_op jit(solution)/shard_map/ppermute | solution.py:39
  120.0 23.9 %all-to-all-start.2 = ((bf16[32,32,512]{2,1,0:T(8,128)(2,1)}), bf16[32,32,512]{2,1,0:T(8,128)(2,1)S(1)}, u32[]{:S(2)}, u32[]{:S(2)}) async-start(bf16[32,32,512]{2,1,0:T(8,128)(2,1)} %get-tuple-element.72), calls=%async_computation.2 | async-start | bytes 2097152 | tf_op jit(solution)/shard_map/all_to_all | solution.py:512
  144.6 2.7 %collective-permute-start.17 = (bf16[32,32,512]{2,1,0:T(8,128)(2,1)S(1)}, bf16[32,32,512]{2,1,0:T(8,128)(2,1)S(1)}, u32[]{:S(2)}, u32[]{:S(2)}) collective-permute-start(bf16[32,32,512]{2,1,0:T(8,128)(2,1)S(1)} %shard_map.156.far_mine), channel_id=1, source_target_pairs={{0,2},{2,0},{1,3},{3,1},{4,6},{6,4},{5,7},{7,5},{8,10},{10,8},{9,1... | collective-permute-start | bytes 3145736 | tf_op jit(solution)/shard_map/ppermute | solution.py:39
  (15 other events, 24.5 us)
